TPU v7x, 32 devices: a whole 2x2x4 slice. The times are simulated.
32 devices in a mesh: ctx: 8 (over z, core), chan: 4 (over y, x).
Axes of the slice: x: 2, y: 2, z: 4, core: 2. Of those that a mesh axis runs over, the one named last changes fastest.
Arguments:
- key_stream: bfloat16 [2048, 8192], P('ctx', 'chan'), may hold values from -6 to 6
- value_stream: bfloat16 [2048, 8192], P('ctx', 'chan'), may hold values from -6 to 6
- query_stream: bfloat16 [2048, 8192], P('ctx', 'chan'), may hold values from -6 to 6
- grad_out: bfloat16 [2048, 8192], P('ctx', 'chan'), may hold values from -6 to 6
- distant_lag_taps: bfloat16 [16, 2, 512], replicated, may hold values from -0.21875 to 0.21875
- near_taps: bfloat16 [16, 256], replicated, may hold values from -0.21875 to 0.21875
- lag_blocks: int32 [16, 2], replicated, may hold values from 1 to 3, as said below
Outputs:
- block_out: bfloat16 [2048, 8192], P('ctx', 'chan')
- grad_values: bfloat16 [2048, 8192], P('ctx', 'chan')
- grad_far: float32 [16, 2, 512], replicated
- grad_near: float32 [16, 256], replicated
Inputs may be any that keep to these rules, and one draw needn't show every extreme that they name: `lag_blocks`: the lags of one group are distinct, and every group lists the lag block 3.
All inputs are finite; a program needn't handle non-finite values.
Results may differ from a plain program's by a relative error of at most 0.0049.
Values may be sent and summed in bfloat16 or wider, within the bound.
No kernel may reach another device: no remote copies, remote signals or barrier semaphores. Data moves between devices by JAX's collectives and lax.ppermute only.
A program may use at most 128 MiB of HBM per device.

v0:
```python
import functools
import math

import jax
import jax.numpy as jnp
from jax import lax
from jax.experimental import pallas as pl
from jax.experimental.pallas import tpu as pltpu
from jax.sharding import PartitionSpec as P

GSIZE = 512
WIN = 4
VMEM_LIMIT = 16 * 1024 * 1024
FIRST_LIMIT = 60 * 1024 * 1024
SECOND_LIMIT = 16 * 1024 * 1024
SCALE = 32
BF16 = jnp.bfloat16
F32 = jnp.float32

VMEM = pl.BlockSpec(memory_space=pltpu.VMEM)
SMEM = pl.BlockSpec(memory_space=pltpu.SMEM)
HBM = pl.BlockSpec(memory_space=pltpu.HBM)


def core_of():
    return lax.rem(lax.axis_index("ctx"), 2)


def call(body, name, out_shape, in_specs, out_specs, scratch=(), aliases=None, limit=VMEM_LIMIT, flops=1):
    def run(*args):
        moved = sum(a.size * a.dtype.itemsize for a in args + tuple(jax.tree.leaves(out_shape)))
        return pl.pallas_call(
            body,
            in_specs=in_specs,
            out_specs=out_specs,
            out_shape=out_shape,
            scratch_shapes=scratch,
            input_output_aliases=aliases or {},
            compiler_params=pltpu.CompilerParams(vmem_limit_bytes=limit),
            cost_estimate=pl.CostEstimate(flops=flops, bytes_accessed=max(1, moved // SCALE), transcendentals=0),
            name=name,
        )(*args)

    return run


def block_group(half, block, width, bw):
    first = lax.axis_index("chan") * width + half * (width // 2) + block * bw
    return lax.div(first, GSIZE)


def rolled(value, shift):
    shift %= value.shape[1]
    if shift % 128 == 0:
        return value if shift == 0 else jnp.concatenate([value[:, -shift:], value[:, :-shift]], axis=1)
    return pltpu.roll(value, shift, 1)


def skew(taps, span):
    width = 2 * span
    row = rolled(jnp.broadcast_to(taps, (8, width)), span)
    index = lax.broadcasted_iota(jnp.int32, (8, width), 0)
    for bit in (1, 2, 4):
        row = jnp.where((index & bit) != 0, rolled(row, bit), row)
    filled = 8
    while filled < span:
        row = jnp.concatenate([row, rolled(row, filled)], axis=0)
        filled *= 2
    return row[:, :span]


def diagonal_sums(matrix, span):
    width = 2 * span
    rows = jnp.concatenate([matrix, jnp.zeros((span, span), F32)], axis=1)
    half = span // 2
    while half >= 8:
        rows = rows[:half] + rolled(rows[half:], -half)
        half //= 2
    index = lax.broadcasted_iota(jnp.int32, (8, width), 0)
    for bit in (1, 2, 4):
        rows = jnp.where((index & bit) != 0, rolled(rows, -bit), rows)
    return rolled(jnp.sum(rows, axis=0, keepdims=True), span)


def stream_products(wanted, streams, name, limit):
    span, width = streams[0].shape
    hw = width // 2
    kinds = sorted({kind[0] for kind in wanted}, reverse=True)

    def body(k_ref, v_ref, q_ref, g_ref, *rest):
        outs, (held, sems) = rest[:-2], rest[-2:]
        core = core_of()

        def copies(place, at, pair):
            half = 1 - core if at == 0 else core
            columns = pl.ds(pl.multiple_of(half * hw, 128), hw)
            return [
                pltpu.make_async_copy(ref.at[:, columns], held.at[place, at, i], sems.at[place, at, i])
                for i, ref in enumerate(pair)
            ]

        for place, kind in enumerate(kinds):
            mixed_core = 0 if kind == "P" else 1
            for is_mixed, pair in ((True, (k_ref, v_ref)), (False, (g_ref, q_ref))):

                @pl.when((core == mixed_core) == is_mixed)
                def _():
                    for at in range(2):
                        for copy in copies(place, at, pair):
                            copy.start()

        for place, kind in enumerate(kinds):
            for at in range(2):
                for copy in copies(place, at, (k_ref, v_ref)):
                    copy.wait()
                product = (held[place, at, 0].astype(F32) * held[place, at, 1].astype(F32)).astype(BF16)
                for out_ref, name in zip(outs, wanted):
                    if name == kind:
                        out_ref[at] = product
                    elif name == f"{kind}{at}":
                        out_ref[...] = product

    shapes = [jax.ShapeDtypeStruct((2, span, hw) if len(n) == 1 else (span, hw), BF16) for n in wanted]
    return call(
        body,
        name,
        shapes,
        [HBM] * 4,
        [VMEM] * len(shapes),
        [pltpu.VMEM((len(kinds), 2, 2, span, hw), BF16), pltpu.SemaphoreType.DMA((len(kinds), 2, 2))],
        limit=limit,
    )(*streams)


def short_lag(lag_ref, group, slots):
    lag = lag_ref[group * slots]
    for slot in range(1, slots):
        lag = jnp.minimum(lag, lag_ref[group * slots + slot])
    return lag


def toeplitz_matrices(lags, far_taps, near_taps, span, width, bw):
    groups, slots, doubled = far_taps.shape
    nb = width // 2 // bw

    def body(lag_ref, far_ref, near_ref, out_ref, near_rows):
        core = core_of()
        near_rows[...] = near_ref[...].astype(F32)
        for frame in range(2):
            half = core if frame == 0 else 1 - core
            for b in range(nb):
                group = block_group(half, b, width, bw)
                far = far_ref[group].astype(F32)
                near = near_rows[pl.ds(group, 1), :]
                short = last = jnp.zeros((1, doubled), F32)
                for slot in range(slots):
                    is_last = lag_ref[group * slots + slot] == WIN - 1
                    taps = far[slot : slot + 1]
                    short = jnp.where(is_last, short, taps)
                    last = jnp.where(is_last, taps, last)
                near = jnp.concatenate([jnp.zeros((1, span), F32), near], axis=1)
                for at, taps in enumerate((near, short, last)):
                    matrix = skew(taps, span)
                    out_ref[1 - core, frame * nb + b, at] = matrix.astype(BF16)
                    out_ref[core, frame * nb + b, at] = matrix.T.astype(BF16)

    return call(
        body,
        "toeplitz",
        jax.ShapeDtypeStruct((2, 2 * nb, 3, span, span), BF16),
        [SMEM, VMEM, VMEM],
        VMEM,
        [pltpu.VMEM((groups, span), F32)],
    )(lags, far_taps, near_taps)


def outer(mixed, gated):
    return lax.dot_general(mixed, gated, (((1,), (1,)), ((), ())), preferred_element_type=F32)


def by_core(body):
    core = core_of()

    @pl.when(core == 0)
    def _():
        body(outer)

    @pl.when(core != 0)
    def _():
        body(lambda p, q: outer(q, p))


def correlate_near(p_own, q_own):
    span, hw = p_own[0].shape
    bw = min(GSIZE, hw)
    nb = hw // bw

    def body(p0, p1, q0, q1, rows_ref):
        def run(pair):
            for frame in range(2):
                for b in range(nb):
                    at = pl.ds(b * bw, bw)
                    matrix = pair((p0, p1)[frame][:, at], (q0, q1)[frame][:, at])
                    rows_ref[frame, pl.ds(b, 1), :] = diagonal_sums(matrix, span)

        by_core(run)

    return call(
        body,
        "correlate_near",
        jax.ShapeDtypeStruct((2, nb, 2 * span), F32),
        [VMEM] * 4,
        VMEM,
    )(*p_own, *q_own)


def correlate_one(p_own, q_own, r1, x0):
    span, hw = p_own[0].shape
    bw = min(GSIZE, hw)
    nb = hw // bw

    def body(p_ref, q_ref, r1_ref, x0_ref, rows_ref):
        def run(pair):
            for b in range(nb):
                at = pl.ds(b * bw, bw)
                matrix = pair(r1_ref[0, :, at], q_ref[:, at]) + pair(p_ref[:, at], x0_ref[:, at])
                rows_ref[pl.ds(b, 1), :] = diagonal_sums(matrix, span)

        by_core(run)

    return call(
        body,
        "correlate_one",
        jax.ShapeDtypeStruct((nb, 2 * span), F32),
        [VMEM] * 4,
        VMEM,
    )(p_own[0], q_own[0], r1, x0[0])


def correlate_far(lags, slots, near, ones, p_own, r1, x1, r2):
    span, hw = r2.shape
    bw = min(GSIZE, hw)
    nb = hw // bw

    def body(lag_ref, near_ref, ones_ref, p0, p1, r1_ref, x1_ref, r2_ref, out_ref):
        core = core_of()

        def run(pair):
            for b in range(nb):
                at = pl.ds(b * bw, bw)
                p, x = p0[:, at], x1_ref[1, :, at]
                last = diagonal_sums(pair(r1_ref[0, :, at], x) + pair(p, r2_ref[:, at]), span)
                twos = [
                    diagonal_sums(pair(p, x), span),
                    diagonal_sums(pair(p1[:, at], x1_ref[0, :, at]), span),
                ]
                for frame in range(2):
                    half = core if frame == 0 else 1 - core
                    group = block_group(half, b, 2 * hw, bw)
                    place = half * nb + b
                    is_two = short_lag(lag_ref, group, slots) == 2
                    empty = jnp.zeros_like(last)
                    one = ones_ref[pl.ds(b, 1), :] if frame == 0 else empty
                    short = jnp.where(is_two, twos[frame], one)
                    distant = last if frame == 0 else empty
                    out_ref[place, pl.ds(0, 1), :] = near_ref[frame, pl.ds(b, 1), :]
                    for slot in range(slots):
                        is_last = lag_ref[group * slots + slot] == WIN - 1
                        out_ref[place, pl.ds(1 + slot, 1), :] = jnp.where(is_last, distant, short)

        by_core(run)

    return call(
        body,
        "correlate_far",
        jax.ShapeDtypeStruct((2 * nb, slots + 1, 2 * span), F32),
        [SMEM] + [VMEM] * 7,
        VMEM,
    )(lags, near, ones, *p_own, r1, x1, r2)


def partial_sums(lags, slots, toeplitz, p_own, r1, x2):
    span, hw = p_own[0].shape
    bw = min(GSIZE, hw)
    nb = hw // bw

    def body(lag_ref, t_ref, p0, p1, r1_ref, x20, x21, out_ref):
        core = core_of()
        for frame in range(2):
            half = core if frame == 0 else 1 - core
            for b in range(nb):
                at = pl.ds(b * bw, bw)
                group = block_group(half, b, 2 * hw, bw)
                is_one = short_lag(lag_ref, group, slots) == 1
                panel = jnp.where(is_one, r1_ref[frame, :, at], (x20, x21)[frame][:, at])
                total = jnp.dot(t_ref[0, frame * nb + b, 0], (p0, p1)[frame][:, at], preferred_element_type=F32)
                total += jnp.dot(t_ref[0, frame * nb + b, 1], panel, preferred_element_type=F32)
                out_ref[frame, :, at] = total

    return call(
        body,
        "partial_sums",
        jax.ShapeDtypeStruct((2, span, hw), F32),
        [SMEM] + [VMEM] * 6,
        VMEM,
    )(lags, toeplitz, *p_own, r1, *x2)


def gated_output(role, panels, total_of, key, query, results):
    span, width = key.shape
    hw = width // 2
    bw = min(GSIZE, hw)
    nb = hw // bw
    role_at = 0 if role == "P" else 1
    count = len(panels)

    def body(*refs):
        lag_ref, panel_refs, key_ref, query_ref = refs[0], refs[1:count], refs[count], refs[count + 1]
        block_ref, values_ref, gate, held, sems = refs[-5:]
        core = core_of()
        to_block = core == role_at

        def load(ref):
            return pltpu.make_async_copy(ref, gate, sems.at[2 * nb])

        def store(at, columns, ref):
            return pltpu.make_async_copy(held.at[at], ref.at[:, columns], sems.at[at])

        @pl.when(to_block)
        def _():
            load(query_ref).start()

        @pl.when(jnp.logical_not(to_block))
        def _():
            load(key_ref).start()

        for frame in range(2):
            half = core if frame == 0 else 1 - core
            for b in range(nb):
                at = frame * nb + b
                group = block_group(half, b, width, bw)
                total = total_of(lag_ref, group, frame, b, at, pl.ds(b * bw, bw), *panel_refs)
                if at == 0:
                    load(key_ref).wait()
                columns = pl.ds(pl.multiple_of(half * hw + b * bw, 128), bw)
                held[at] = (total * gate[:, columns].astype(F32)).astype(BF16)

                @pl.when(to_block)
                def _():
                    store(at, columns, block_ref).start()

                @pl.when(jnp.logical_not(to_block))
                def _():
                    store(at, columns, values_ref).start()

        for at in range(2 * nb):
            store(at, pl.ds(0, bw), block_ref).wait()

    shape = jax.ShapeDtypeStruct((span, width), BF16)
    return call(
        body,
        f"out_{role.lower()}",
        [shape, shape],
        [SMEM] + [VMEM] * (count - 1) + [HBM] * (2 + len(results)),
        [HBM, HBM],
        [
            pltpu.VMEM((span, width), BF16),
            pltpu.VMEM((2 * nb, span, bw), BF16),
            pltpu.SemaphoreType.DMA((2 * nb + 1,)),
        ],
        {count + 2: 0, count + 3: 1} if results else None,
    )(*panels, key, query, *results)


def q_output(lags, slots, toeplitz, q_own, x0, x1, r2, key, query):
    def total_of(lag_ref, group, frame, b, place, at, t_ref, q0, q1, x00, x01, x1_ref, r20, r21):
        is_one = short_lag(lag_ref, group, slots) == 1
        panel = jnp.where(is_one, (x00, x01)[frame][:, at], x1_ref[1 - frame, :, at])
        total = jnp.dot(t_ref[1, place, 0], (q0, q1)[frame][:, at], preferred_element_type=F32)
        total += jnp.dot(t_ref[1, place, 1], panel, preferred_element_type=F32)
        return total + jnp.dot(t_ref[1, place, 2], (r20, r21)[frame][:, at], preferred_element_type=F32)

    return gated_output("Q", (lags, toeplitz, *q_own, *x0, x1, *r2), total_of, key, query, ())


def p_output(lags, toeplitz, sums, r3, key, query, results):
    def total_of(lag_ref, group, frame, b, place, at, t_ref, sums_ref, r3_ref):
        last = jnp.dot(t_ref[0, place, 2], r3_ref[frame, :, at], preferred_element_type=F32)
        return sums_ref[frame, :, at] + last

    return gated_output("P", (lags, toeplitz, sums, r3), total_of, key, query, results)


def after(value, *others):
    return lax.optimization_barrier((value,) + others)[0]


def plain_sum(a, b):
    def body(a_ref, b_ref, out_ref):
        out_ref[...] = a_ref[...] + b_ref[...]

    return call(body, "add_rows", jax.ShapeDtypeStruct(a.shape, F32), [VMEM, VMEM], VMEM)(a, b)


def sum_over_chips(rows):
    count = lax.axis_size("ctx")
    if count & (count - 1):
        return lax.psum(rows, "ctx")
    bit = 2
    while bit < count:
        rows = plain_sum(rows, lax.ppermute(rows, "ctx", [(i, i ^ bit) for i in range(count)]))
        bit *= 2
    return rows


def sum_over_cores(rows):
    count = lax.axis_size("ctx")
    if count & (count - 1):
        return rows
    return plain_sum(rows, lax.ppermute(rows, "ctx", [(i, i ^ 1) for i in range(count)]))


def joined(first, second, bit):
    def body(first_ref, second_ref, out_ref):
        length = first_ref.shape[0]
        here = lax.rem(lax.div(lax.axis_index("chan"), bit), 2)
        out_ref[pl.ds(here * length, length)] = first_ref[...]
        out_ref[pl.ds((1 - here) * length, length)] = second_ref[...]

    shape = jax.ShapeDtypeStruct((2 * first.shape[0],) + first.shape[1:], F32)
    return call(body, "join_rows", shape, [VMEM] * 2, VMEM)(first, second)


def filter_gradients(rows, groups, span, scale):
    count = lax.axis_size("chan")
    _, rows_per, doubled = rows.shape
    slots = rows_per - 1
    if count & (count - 1):
        rows = lax.all_gather(rows, "chan", axis=0, tiled=True)
    else:
        bit = 1
        while bit < count:
            other = lax.ppermute(rows, "chan", [(i, i ^ bit) for i in range(count)])
            rows = joined(rows, other, bit)
            bit *= 2
    repeat = rows.shape[0] // groups

    def body(rows_ref, far_ref, near_ref):
        for group in range(groups):
            total = rows_ref[group * repeat]
            for at in range(1, repeat):
                total = total + rows_ref[group * repeat + at]
            far_ref[group] = total[1:] * scale
            near_ref[pl.ds(group, 1), :] = total[:1, span:] * scale

    return call(
        body,
        "filter_gradients",
        [
            jax.ShapeDtypeStruct((groups, slots, doubled), F32),
            jax.ShapeDtypeStruct((groups, span), F32),
        ],
        [VMEM],
        [VMEM, VMEM],
    )(rows)


def per_device(
    key_stream, value_stream, query_stream, grad_out, distant_lag_taps, near_taps, lag_blocks
):
    span, width = key_stream.shape
    groups = distant_lag_taps.shape[0]
    count = lax.axis_size("ctx")
    hw = width // 2
    bw = min(GSIZE, hw)

    def keep(moves):
        return [(a, b) for a, b in moves if 0 <= b < count]

    swap = [(i, i ^ 1) for i in range(count)]
    to_near = keep([(i, i + 1 if i % 2 else i - 1) for i in range(count)])
    to_far = keep([(i, i - 3 if i % 2 else i + 3) for i in range(count)])
    onward = keep([(i, i - 2 if i % 2 else i + 2) for i in range(count)])

    def send(value, moves):
        return lax.ppermute(value, "ctx", moves)

    slots = lag_blocks.shape[1]
    streams = (key_stream, value_stream, query_stream, grad_out)
    (q_sent,) = stream_products(("Q",), streams, "q_stream", FIRST_LIMIT)
    r1 = send(q_sent, to_near)
    *late, far_taps, near_taps, lags, _ = lax.optimization_barrier(
        streams + (distant_lag_taps, near_taps, lag_blocks, q_sent)
    )
    lags = lags.reshape(-1)
    qa, qb, pa, pb = stream_products(("Q0", "Q1", "P0", "P1"), late, "streams", SECOND_LIMIT)
    q_own, p_own = (qb, qa), (pb, pa)
    x0 = (send(pa, swap), send(pb, swap))
    toeplitz = toeplitz_matrices(lags, far_taps, near_taps, span, width, bw)
    near = correlate_near(p_own, q_own)

    r1, x0 = lax.optimization_barrier((r1, x0, toeplitz, near))[:2]
    r2a = send(after(pa, r1), to_far)
    x1 = send(r1, swap)
    ones = correlate_one(p_own, q_own, r1, x0)
    r2b = send(after(pb, x1), to_far)
    rows = sum_over_chips(correlate_far(lags, slots, near, ones, p_own, r1, x1, r2a))
    r1_late, r2a_late, r2b, rows = lax.optimization_barrier((r1, r2a, r2b, rows))
    r3 = send(r1_late, onward)
    x2 = (send(r2b, swap), send(r2a_late, swap))
    results = q_output(lags, slots, toeplitz, q_own, x0, x1, (r2a, r2b), key_stream, query_stream)
    rows = sum_over_cores(rows)
    sums = partial_sums(lags, slots, toeplitz, p_own, r1, x2)
    results = p_output(lags, toeplitz, sums, r3, key_stream, query_stream, results)

    scale = 1.0 / math.sqrt(span * count * GSIZE)
    far, near = filter_gradients(rows, groups, span, scale)
    return (results[0], results[1], far, near)


def solution(mesh):
    streams = P("ctx", "chan")
    return jax.shard_map(
        per_device,
        mesh=mesh,
        in_specs=(streams, streams, streams, streams, P(), P(), P()),
        out_specs=(streams, streams, P(), P()),
        check_vma=False,
    )
```

profile of v0, /device:TPU:0, one launch (start us, length us, event | category | flops | bytes accessed | tf_op | source)
XLA Modules:
  0.0 66.5 jit_solution(7748871823327777254)
XLA Ops:
  0.7 2.8 %q_stream.1 = bf16[2,256,1024]{2,1,0:T(8,128)(2,1)} custom-call(bf16[256,2048]{1,0:T(8,128)(2,1)} %refs_4_.1, bf16[256,2048]{1,0:T(8,128)(2,1)} %v_ref.2, bf16[256,2048]{1,0:T(8,128)(2,1)} %refs_5_.1, bf16[256,2048]{1,0:T(8,128)(2,1)} %g_ref.2), custom_call_target="tpu_custom_call" | custom-call | flops 1 | bytes 163840 | tf_op jit(solution)/shard_map/q_stream/pallas_call | solution.py:32
  3.5 0.7 %collective-permute-start = (bf16[2,256,1024]{2,1,0:T(8,128)(2,1)}, bf16[2,256,1024]{2,1,0:T(8,128)(2,1)S(1)}, u32[]{:S(2)}, u32[]{:S(2)}) collective-permute-start(bf16[2,256,1024]{2,1,0:T(8,128)(2,1)} %q_stream.1), channel_id=1, source_target_pairs={{4,8},{8,4},{12,16},{16,12},{20,24},{24,20},{5,9},{9,5},{13,17},{1... | collective-permute-start | bytes 3145736 | tf_op jit(solution)/shard_map/ppermute | solution.py:486
  4.2 1.2 %copy-done.4 = bf16[256,2048]{1,0:T(8,128)(2,1)S(1)} copy-done((bf16[256,2048]{1,0:T(8,128)(2,1)S(1)}, bf16[256,2048]{1,0:T(8,128)(2,1)}, u32[]{:S(2)}) %copy-start.4) | copy-done | bytes 1048600
  5.4 1.2 %copy-done.5 = bf16[256,2048]{1,0:T(8,128)(2,1)S(1)} copy-done((bf16[256,2048]{1,0:T(8,128)(2,1)S(1)}, bf16[256,2048]{1,0:T(8,128)(2,1)}, u32[]{:S(2)}) %copy-start.5) | copy-done | bytes 1048600
  6.7 1.8 %streams.1 = (bf16[256,1024]{1,0:T(8,128)(2,1)S(1)}, bf16[256,1024]{1,0:T(8,128)(2,1)S(1)}, bf16[256,1024]{1,0:T(8,128)(2,1)}, bf16[256,1024]{1,0:T(8,128)(2,1)}) custom-call(bf16[256,2048]{1,0:T(8,128)(2,1)S(1)} %copy-done, bf16[256,2048]{1,0:T(8,128)(2,1)S(1)} %copy-done.4, bf16[256,2048]{1,0:T(8,128)(2,1)S(1)} %copy-done.1, bf16[256,2048]{1,0:T(8,128)(2,1)S(1)} %copy-done.5), custom_call_target="tpu_custom_call" | custom-call | flops 1 | bytes 196608 | tf_op jit(solution)/shard_map/streams/pallas_call | solution.py:32
  8.5 4.4 %collective-permute-start.1 = (bf16[256,1024]{1,0:T(8,128)(2,1)}, bf16[256,1024]{1,0:T(8,128)(2,1)}, u32[]{:S(2)}, u32[]{:S(2)}) collective-permute-start(bf16[256,1024]{1,0:T(8,128)(2,1)} %get-tuple-element.42.p1), channel_id=1, source_target_pairs={{0,4},{4,0},{8,12},{12,8},{16,20},{20,16},{24,28},{28,24},{1,5},{5... | collective-permute-start | bytes 1572872 | tf_op jit(solution)/shard_map/ppermute | solution.py:486
  13.0 2.2 %correlate_near.1.near_ref = f32[2,2,512]{2,1,0:T(2,128)S(1)} custom-call(bf16[256,1024]{1,0:T(8,128)(2,1)} %get-tuple-element.43.p0.p_ref, bf16[256,1024]{1,0:T(8,128)(2,1)} %get-tuple-element.42.p1, bf16[256,1024]{1,0:T(8,128)(2,1)S(1)} %get-tuple-element.39.q0.q_ref.refs_2_, bf16[256,1024]{1,0:T(8,128)(2,1)S(1)} %get-tuple-element.40.q1.refs_3_), custom_call_target="tpu_custom_call" | custom-call | flops 1 | bytes 65792 | tf_op jit(solution)/shard_map/correlate_near/pallas_call | solution.py:32
  15.2 0.8 %copy-done.2 = bf16[256,1024]{1,0:T(8,128)(2,1)} copy-done((bf16[256,1024]{1,0:T(8,128)(2,1)}, bf16[256,1024]{1,0:T(8,128)(2,1)S(1)}, u32[]{:S(2)}) %copy-start.2) | copy-done | bytes 524312
  16.0 0.8 %copy-done.6 = bf16[256,1024]{1,0:T(8,128)(2,1)} copy-done((bf16[256,1024]{1,0:T(8,128)(2,1)}, bf16[256,1024]{1,0:T(8,128)(2,1)S(1)}, u32[]{:S(2)}) %copy-start.6) | copy-done | bytes 524312
  16.9 0.1 reshape.11.lag_ref.refs_0_
  17.0 3.7 %toeplitz.1.t_ref.refs_1_ = bf16[2,4,3,256,256]{4,3,2,1,0:T(8,128)(2,1)S(1)} custom-call(s32[32]{0:T(128)S(1)} %reshape.11.lag_ref.refs_0_, bf16[16,2,512]{2,1,0:T(2,128)(2,1)S(1)} %copy-done.8, bf16[16,256]{1,0:T(8,128)(2,1)S(1)} %copy-done.9), custom_call_target="tpu_custom_call" | custom-call | flops 1 | bytes 99588 | tf_op jit(solution)/shard_map/toeplitz/pallas_call | solution.py:32
  20.7 0.5 collective-permute-start.4
  21.2 3.6 %collective-permute-start.3 = (bf16[256,1024]{1,0:T(8,128)(2,1)}, bf16[256,1024]{1,0:T(8,128)(2,1)S(1)}, u32[]{:S(2)}, u32[]{:S(2)}) collective-permute-start(bf16[256,1024]{1,0:T(8,128)(2,1)} %get-tuple-element.42.p1), channel_id=1, source_target_pairs={{0,12},{8,20},{12,0},{16,28},{20,8},{28,16},{1,13},{9,21},{13,1},{... | collective-permute-start | bytes 1572872 | tf_op jit(solution)/shard_map/ppermute | solution.py:486
  24.8 2.3 %collective-permute-start.5 = (bf16[256,1024]{1,0:T(8,128)(2,1)}, bf16[256,1024]{1,0:T(8,128)(2,1)S(1)}, u32[]{:S(2)}, u32[]{:S(2)}) collective-permute-start(bf16[256,1024]{1,0:T(8,128)(2,1)} %get-tuple-element.43.p0.p_ref), channel_id=1, source_target_pairs={{0,12},{8,20},{12,0},{16,28},{20,8},{28,16},{1,13},{9,21},{13,1},{... | collective-permute-start | bytes 1572872 | tf_op jit(solution)/shard_map/ppermute | solution.py:486
  27.1 2.2 %correlate_one.1.ones_ref = f32[2,512]{1,0:T(2,128)S(1)} custom-call(bf16[256,1024]{1,0:T(8,128)(2,1)} %get-tuple-element.43.p0.p_ref, bf16[256,1024]{1,0:T(8,128)(2,1)S(1)} %copy-done.3, bf16[2,256,1024]{2,1,0:T(8,128)(2,1)S(1)} %collective-permute-done.r1_ref, bf16[256,1024]{1,0:T(8,128)(2,1)} %collective-permute-done.1.x0_ref.refs_4_), custom_call_target="tpu_custom_call" | custom-call | flops 1 | bytes 82048 | tf_op jit(solution)/shard_map/correlate_one/pallas_call | solution.py:32
  29.3 2.6 %collective-permute-done.3.r2_ref.refs_7_ = bf16[256,1024]{1,0:T(8,128)(2,1)S(1)} collective-permute-done((bf16[256,1024]{1,0:T(8,128)(2,1)}, bf16[256,1024]{1,0:T(8,128)(2,1)S(1)}, u32[]{:S(2)}, u32[]{:S(2)}) %collective-permute-start.3) | collective-permute-done | bytes 524320 | tf_op jit(solution)/shard_map/ppermute | solution.py:486
  31.9 2.5 %correlate_far.1.a_ref = f32[4,3,512]{2,1,0:T(4,128)S(1)} custom-call(s32[32]{0:T(128)S(1)} %reshape.11.lag_ref.refs_0_, f32[2,2,512]{2,1,0:T(2,128)S(1)} %correlate_near.1.near_ref, f32[2,512]{1,0:T(2,128)S(1)} %correlate_one.1.ones_ref, bf16[256,1024]{1,0:T(8,128)(2,1)} %get-tuple-element.43.p0.p_ref, bf16[256,1024]{1,0:T(8,128)(2,1)} %get-tuple-element.42.p1, ...), custom_call_target="tpu_custom_call" | custom-call | flops 1 | bytes 115844 | tf_op jit(solution)/shard_map/correlate_far/pallas_call | solution.py:32
  34.4 1.8 %collective-permute-start.6 = (f32[4,3,512]{2,1,0:T(4,128)S(1)}, f32[4,3,512]{2,1,0:T(4,128)S(1)}, u32[]{:S(2)}, u32[]{:S(2)}) collective-permute-start(f32[4,3,512]{2,1,0:T(4,128)S(1)} %correlate_far.1.a_ref), channel_id=1, source_target_pairs={{0,8},{4,12},{8,0},{12,4},{16,24},{20,28},{24,16},{28,20},{1,9},{5... | collective-permute-start | bytes 73736 | tf_op jit(solution)/shard_map/ppermute | solution.py:411
  36.2 2.2 %collective-permute-done.6.b_ref = f32[4,3,512]{2,1,0:T(4,128)S(1)} collective-permute-done((f32[4,3,512]{2,1,0:T(4,128)S(1)}, f32[4,3,512]{2,1,0:T(4,128)S(1)}, u32[]{:S(2)}, u32[]{:S(2)}) %collective-permute-start.6) | collective-permute-done | bytes 24608 | tf_op jit(solution)/shard_map/ppermute | solution.py:411
  38.5 2.8 %collective-permute-start.7 = (f32[4,3,512]{2,1,0:T(4,128)S(1)}, f32[4,3,512]{2,1,0:T(4,128)S(1)}, u32[]{:S(2)}, u32[]{:S(2)}) collective-permute-start(f32[4,3,512]{2,1,0:T(4,128)S(1)} %add_rows.3.a_ref), channel_id=1, source_target_pairs={{0,16},{4,20},{8,24},{12,28},{16,0},{20,4},{24,8},{28,12},{1,17},{... | collective-permute-start | bytes 73736 | tf_op jit(solution)/shard_map/ppermute | solution.py:411
  41.2 2.1 %collective-permute-done.7.b_ref = f32[4,3,512]{2,1,0:T(4,128)S(1)} collective-permute-done((f32[4,3,512]{2,1,0:T(4,128)S(1)}, f32[4,3,512]{2,1,0:T(4,128)S(1)}, u32[]{:S(2)}, u32[]{:S(2)}) %collective-permute-start.7) | collective-permute-done | bytes 24608 | tf_op jit(solution)/shard_map/ppermute | solution.py:411
  43.3 4.0 %collective-permute-start.10 = (bf16[2,256,1024]{2,1,0:T(8,128)(2,1)S(1)}, bf16[2,256,1024]{2,1,0:T(8,128)(2,1)S(1)}, u32[]{:S(2)}, u32[]{:S(2)}) collective-permute-start(bf16[2,256,1024]{2,1,0:T(8,128)(2,1)S(1)} %collective-permute-done.r1_ref), channel_id=1, source_target_pairs={{0,8},{8,16},{12,4},{16,24},{20,12},{28,20},{1,9},{9,17},{13,5},{1... | collective-permute-start | bytes 3145736 | tf_op jit(solution)/shard_map/ppermute | solution.py:486
  47.4 0.5 collective-permute-start.8
  48.0 2.1 %collective-permute-done.11.b_ref = f32[4,3,512]{2,1,0:T(4,128)S(1)} collective-permute-done((f32[4,3,512]{2,1,0:T(4,128)S(1)}, f32[4,3,512]{2,1,0:T(4,128)S(1)}, u32[]{:S(2)}, u32[]{:S(2)}) %collective-permute-start.11) | collective-permute-done | bytes 24608 | tf_op jit(solution)/shard_map/ppermute | solution.py:420
  50.1 1.5 %collective-permute-start.12 = (f32[4,3,512]{2,1,0:T(4,128)S(1)}, f32[4,3,512]{2,1,0:T(4,128)S(1)}, u32[]{:S(2)}, u32[]{:S(2)}) collective-permute-start(f32[4,3,512]{2,1,0:T(4,128)S(1)} %add_rows.5.first_ref), channel_id=1, source_target_pairs={{0,1},{1,0},{2,3},{3,2},{4,5},{5,4},{6,7},{7,6},{8,9},{9,8},{10,11... | collective-permute-start | bytes 73736 | tf_op jit(solution)/shard_map/ppermute | solution.py:443
  51.6 2.4 %collective-permute-done.12.second_ref = f32[4,3,512]{2,1,0:T(4,128)S(1)} collective-permute-done((f32[4,3,512]{2,1,0:T(4,128)S(1)}, f32[4,3,512]{2,1,0:T(4,128)S(1)}, u32[]{:S(2)}, u32[]{:S(2)}) %collective-permute-start.12) | collective-permute-done | bytes 24608 | tf_op jit(solution)/shard_map/ppermute | solution.py:443
  54.0 1.6 %collective-permute-start.13 = (f32[8,3,512]{2,1,0:T(4,128)S(1)}, f32[8,3,512]{2,1,0:T(4,128)S(1)}, u32[]{:S(2)}, u32[]{:S(2)}) collective-permute-start(f32[8,3,512]{2,1,0:T(4,128)S(1)} %join_rows.2.first_ref), channel_id=1, source_target_pairs={{0,2},{1,3},{2,0},{3,1},{4,6},{5,7},{6,4},{7,5},{8,10},{9,11},{10,... | collective-permute-start | bytes 147464 | tf_op jit(solution)/shard_map/ppermute | solution.py:443
  55.6 2.7 %collective-permute-done.13.second_ref = f32[8,3,512]{2,1,0:T(4,128)S(1)} collective-permute-done((f32[8,3,512]{2,1,0:T(4,128)S(1)}, f32[8,3,512]{2,1,0:T(4,128)S(1)}, u32[]{:S(2)}, u32[]{:S(2)}) %collective-permute-start.13) | collective-permute-done | bytes 49184 | tf_op jit(solution)/shard_map/ppermute | solution.py:443
  58.4 3.3 %out_q.1 = (bf16[256,2048]{1,0:T(8,128)(2,1)}, bf16[256,2048]{1,0:T(8,128)(2,1)}) custom-call(s32[32]{0:T(128)S(1)} %reshape.11.lag_ref.refs_0_, bf16[2,4,3,256,256]{4,3,2,1,0:T(8,128)(2,1)S(1)} %toeplitz.1.t_ref.refs_1_, bf16[256,1024]{1,0:T(8,128)(2,1)S(1)} %copy-done.3, bf16[256,1024]{1,0:T(8,128)(2,1)S(1)} %copy-done.7, ...), custom_call_target="tpu_custom_call" | custom-call | flops 1 | bytes 360452 | tf_op jit(solution)/shard_map/out_q/pallas_call | solution.py:32
  61.7 0.7 %filter_gradients.1 = (f32[16,2,512]{2,1,0:T(2,128)}, f32[16,256]{1,0:T(8,128)}) custom-call(f32[16,3,512]{2,1,0:T(4,128)S(1)} %join_rows.3.rows_ref), custom_call_target="tpu_custom_call" | custom-call | flops 1 | bytes 5632 | tf_op jit(solution)/shard_map/filter_gradients/pallas_call | solution.py:32
  62.4 2.0 %partial_sums.1.refs_2_ = f32[2,256,1024]{2,1,0:T(8,128)S(1)} custom-call(s32[32]{0:T(128)S(1)} %reshape.11.lag_ref.refs_0_, bf16[2,4,3,256,256]{4,3,2,1,0:T(8,128)(2,1)S(1)} %toeplitz.1.t_ref.refs_1_, bf16[256,1024]{1,0:T(8,128)(2,1)} %get-tuple-element.43.p0.p_ref, bf16[256,1024]{1,0:T(8,128)(2,1)} %get-tuple-element.42.p1, ...), custom_call_target="tpu_custom_call" | custom-call | flops 1 | bytes 262148 | tf_op jit(solution)/shard_map/partial_sums/pallas_call | solution.py:32
  64.4 2.1 %out_p.1 = (bf16[256,2048]{1,0:T(8,128)(2,1)}, bf16[256,2048]{1,0:T(8,128)(2,1)}) custom-call(s32[32]{0:T(128)S(1)} %reshape.11.lag_ref.refs_0_, bf16[2,4,3,256,256]{4,3,2,1,0:T(8,128)(2,1)S(1)} %toeplitz.1.t_ref.refs_1_, f32[2,256,1024]{2,1,0:T(8,128)S(1)} %partial_sums.1.refs_2_, ...), custom_call_target="tpu_custom_call", output_to_operand_aliasing={{0}: (6, {}), {1}: (7, {})} | custom-call | flops 1 | bytes 393220 | tf_op jit(solution)/shard_map/out_p/pallas_call | solution.py:32
  (35 shorter events, 0.4 us)
Async XLA Ops:
  0.6 3.6 %copy-start.1 = (bf16[256,2048]{1,0:T(8,128)(2,1)S(1)}, bf16[256,2048]{1,0:T(8,128)(2,1)}, u32[]{:S(2)}) copy-start(bf16[256,2048]{1,0:T(8,128)(2,1)} %refs_5_.1) | copy-start | bytes 3145732
  0.6 3.6 %copy-start = (bf16[256,2048]{1,0:T(8,128)(2,1)S(1)}, bf16[256,2048]{1,0:T(8,128)(2,1)}, u32[]{:S(2)}) copy-start(bf16[256,2048]{1,0:T(8,128)(2,1)} %refs_4_.1) | copy-start | bytes 3145732
  3.5 17.2 %collective-permute-start = (bf16[2,256,1024]{2,1,0:T(8,128)(2,1)}, bf16[2,256,1024]{2,1,0:T(8,128)(2,1)S(1)}, u32[]{:S(2)}, u32[]{:S(2)}) collective-permute-start(bf16[2,256,1024]{2,1,0:T(8,128)(2,1)} %q_stream.1), channel_id=1, source_target_pairs={{4,8},{8,4},{12,16},{16,12},{20,24},{24,20},{5,9},{9,5},{13,17},{1... | collective-permute-start | bytes 3145736 | tf_op jit(solution)/shard_map/ppermute | solution.py:486
  4.2 1.2 %copy-start.4 = (bf16[256,2048]{1,0:T(8,128)(2,1)S(1)}, bf16[256,2048]{1,0:T(8,128)(2,1)}, u32[]{:S(2)}) copy-start(bf16[256,2048]{1,0:T(8,128)(2,1)} %v_ref.2) | copy-start | bytes 3145732
  5.4 1.2 %copy-start.5 = (bf16[256,2048]{1,0:T(8,128)(2,1)S(1)}, bf16[256,2048]{1,0:T(8,128)(2,1)}, u32[]{:S(2)}) copy-start(bf16[256,2048]{1,0:T(8,128)(2,1)} %g_ref.2) | copy-start | bytes 3145732
  6.7 10.1 %copy-start.10 = (s32[16,2]{0,1:T(2,128)S(1)}, s32[16,2]{0,1:T(2,128)}, u32[]{:S(2)}) copy-start(s32[16,2]{0,1:T(2,128)} %param.13) | copy-start | bytes 388
  6.7 10.3 %copy-start.8 = (bf16[16,2,512]{2,1,0:T(2,128)(2,1)S(1)}, bf16[16,2,512]{2,1,0:T(2,128)(2,1)}, u32[]{:S(2)}) copy-start(bf16[16,2,512]{2,1,0:T(2,128)(2,1)} %far_ref) | copy-start | bytes 98308
  6.7 10.3 %copy-start.9 = (bf16[16,256]{1,0:T(8,128)(2,1)S(1)}, bf16[16,256]{1,0:T(8,128)(2,1)}, u32[]{:S(2)}) copy-start(bf16[16,256]{1,0:T(8,128)(2,1)} %near_ref) | copy-start | bytes 24580
  8.5 12.2 %collective-permute-start.1 = (bf16[256,1024]{1,0:T(8,128)(2,1)}, bf16[256,1024]{1,0:T(8,128)(2,1)}, u32[]{:S(2)}, u32[]{:S(2)}) collective-permute-start(bf16[256,1024]{1,0:T(8,128)(2,1)} %get-tuple-element.42.p1), channel_id=1, source_target_pairs={{0,4},{4,0},{8,12},{12,8},{16,20},{20,16},{24,28},{28,24},{1,5},{5... | collective-permute-start | bytes 1572872 | tf_op jit(solution)/shard_map/ppermute | solution.py:486
  12.9 7.8 %collective-permute-start.2 = (bf16[256,1024]{1,0:T(8,128)(2,1)}, bf16[256,1024]{1,0:T(8,128)(2,1)}, u32[]{:S(2)}, u32[]{:S(2)}) collective-permute-start(bf16[256,1024]{1,0:T(8,128)(2,1)} %get-tuple-element.43.p0.p_ref), channel_id=1, source_target_pairs={{0,4},{4,0},{8,12},{12,8},{16,20},{20,16},{24,28},{28,24},{1,5},{5... | collective-permute-start | bytes 1572872 | tf_op jit(solution)/shard_map/ppermute | solution.py:486
  15.2 0.8 %copy-start.2 = (bf16[256,1024]{1,0:T(8,128)(2,1)}, bf16[256,1024]{1,0:T(8,128)(2,1)S(1)}, u32[]{:S(2)}) copy-start(bf16[256,1024]{1,0:T(8,128)(2,1)S(1)} %get-tuple-element.39.q0.q_ref.refs_2_) | copy-start | bytes 1572868
  16.0 0.8 %copy-start.6 = (bf16[256,1024]{1,0:T(8,128)(2,1)}, bf16[256,1024]{1,0:T(8,128)(2,1)S(1)}, u32[]{:S(2)}) copy-start(bf16[256,1024]{1,0:T(8,128)(2,1)S(1)} %get-tuple-element.40.q1.refs_3_) | copy-start | bytes 1572868
  17.0 10.1 %copy-start.3 = (bf16[256,1024]{1,0:T(8,128)(2,1)S(1)}, bf16[256,1024]{1,0:T(8,128)(2,1)}, u32[]{:S(2)}) copy-start(bf16[256,1024]{1,0:T(8,128)(2,1)} %copy-done.2) | copy-start | bytes 1572868
  20.7 37.7 %copy-start.7 = (bf16[256,1024]{1,0:T(8,128)(2,1)S(1)}, bf16[256,1024]{1,0:T(8,128)(2,1)}, u32[]{:S(2)}) copy-start(bf16[256,1024]{1,0:T(8,128)(2,1)} %copy-done.6) | copy-start | bytes 1572868
  20.7 4.1 %collective-permute-start.4 = (bf16[2,256,1024]{2,1,0:T(8,128)(2,1)S(1)}, bf16[2,256,1024]{2,1,0:T(8,128)(2,1)S(1)}, u32[]{:S(2)}, u32[]{:S(2)}) collective-permute-start(bf16[2,256,1024]{2,1,0:T(8,128)(2,1)S(1)} %collective-permute-done.r1_ref), channel_id=1, source_target_pairs={{0,4},{4,0},{8,12},{12,8},{16,20},{20,16},{24,28},{28,24},{1,5},{5... | collective-permute-start | bytes 3145736 | tf_op jit(solution)/shard_map/ppermute | solution.py:486
  21.2 10.7 %collective-permute-start.3 = (bf16[256,1024]{1,0:T(8,128)(2,1)}, bf16[256,1024]{1,0:T(8,128)(2,1)S(1)}, u32[]{:S(2)}, u32[]{:S(2)}) collective-permute-start(bf16[256,1024]{1,0:T(8,128)(2,1)} %get-tuple-element.42.p1), channel_id=1, source_target_pairs={{0,12},{8,20},{12,0},{16,28},{20,8},{28,16},{1,13},{9,21},{13,1},{... | collective-permute-start | bytes 1572872 | tf_op jit(solution)/shard_map/ppermute | solution.py:486
  24.8 18.4 %collective-permute-start.5 = (bf16[256,1024]{1,0:T(8,128)(2,1)}, bf16[256,1024]{1,0:T(8,128)(2,1)S(1)}, u32[]{:S(2)}, u32[]{:S(2)}) collective-permute-start(bf16[256,1024]{1,0:T(8,128)(2,1)} %get-tuple-element.43.p0.p_ref), channel_id=1, source_target_pairs={{0,12},{8,20},{12,0},{16,28},{20,8},{28,16},{1,13},{9,21},{13,1},{... | collective-permute-start | bytes 1572872 | tf_op jit(solution)/shard_map/ppermute | solution.py:486
  34.4 4.0 %collective-permute-start.6 = (f32[4,3,512]{2,1,0:T(4,128)S(1)}, f32[4,3,512]{2,1,0:T(4,128)S(1)}, u32[]{:S(2)}, u32[]{:S(2)}) collective-permute-start(f32[4,3,512]{2,1,0:T(4,128)S(1)} %correlate_far.1.a_ref), channel_id=1, source_target_pairs={{0,8},{4,12},{8,0},{12,4},{16,24},{20,28},{24,16},{28,20},{1,9},{5... | collective-permute-start | bytes 73736 | tf_op jit(solution)/shard_map/ppermute | solution.py:411
  38.5 4.8 %collective-permute-start.7 = (f32[4,3,512]{2,1,0:T(4,128)S(1)}, f32[4,3,512]{2,1,0:T(4,128)S(1)}, u32[]{:S(2)}, u32[]{:S(2)}) collective-permute-start(f32[4,3,512]{2,1,0:T(4,128)S(1)} %add_rows.3.a_ref), channel_id=1, source_target_pairs={{0,16},{4,20},{8,24},{12,28},{16,0},{20,4},{24,8},{28,12},{1,17},{... | collective-permute-start | bytes 73736 | tf_op jit(solution)/shard_map/ppermute | solution.py:411
  43.3 21.1 %collective-permute-start.10 = (bf16[2,256,1024]{2,1,0:T(8,128)(2,1)S(1)}, bf16[2,256,1024]{2,1,0:T(8,128)(2,1)S(1)}, u32[]{:S(2)}, u32[]{:S(2)}) collective-permute-start(bf16[2,256,1024]{2,1,0:T(8,128)(2,1)S(1)} %collective-permute-done.r1_ref), channel_id=1, source_target_pairs={{0,8},{8,16},{12,4},{16,24},{20,12},{28,20},{1,9},{9,17},{13,5},{1... | collective-permute-start | bytes 3145736 | tf_op jit(solution)/shard_map/ppermute | solution.py:486
  47.3 15.1 %collective-permute-start.9 = (bf16[256,1024]{1,0:T(8,128)(2,1)S(1)}, bf16[256,1024]{1,0:T(8,128)(2,1)S(1)}, u32[]{:S(2)}, u32[]{:S(2)}) collective-permute-start(bf16[256,1024]{1,0:T(8,128)(2,1)S(1)} %collective-permute-done.3.r2_ref.refs_7_), channel_id=1, source_target_pairs={{0,4},{4,0},{8,12},{12,8},{16,20},{20,16},{24,28},{28,24},{1,5},{5... | collective-permute-start | bytes 1572872 | tf_op jit(solution)/shard_map/ppermute | solution.py:486
  47.4 15.0 %collective-permute-start.8 = (bf16[256,1024]{1,0:T(8,128)(2,1)S(1)}, bf16[256,1024]{1,0:T(8,128)(2,1)S(1)}, u32[]{:S(2)}, u32[]{:S(2)}) collective-permute-start(bf16[256,1024]{1,0:T(8,128)(2,1)S(1)} %collective-permute-done.5.refs_8_), channel_id=1, source_target_pairs={{0,4},{4,0},{8,12},{12,8},{16,20},{20,16},{24,28},{28,24},{1,5},{5... | collective-permute-start | bytes 1572872 | tf_op jit(solution)/shard_map/ppermute | solution.py:486
  47.9 2.2 %collective-permute-start.11 = (f32[4,3,512]{2,1,0:T(4,128)S(1)}, f32[4,3,512]{2,1,0:T(4,128)S(1)}, u32[]{:S(2)}, u32[]{:S(2)}) collective-permute-start(f32[4,3,512]{2,1,0:T(4,128)S(1)} %add_rows.4.a_ref), channel_id=1, source_target_pairs={{0,4},{4,0},{8,12},{12,8},{16,20},{20,16},{24,28},{28,24},{1,5},{5... | collective-permute-start | bytes 73736 | tf_op jit(solution)/shard_map/ppermute | solution.py:420
  50.1 3.9 %collective-permute-start.12 = (f32[4,3,512]{2,1,0:T(4,128)S(1)}, f32[4,3,512]{2,1,0:T(4,128)S(1)}, u32[]{:S(2)}, u32[]{:S(2)}) collective-permute-start(f32[4,3,512]{2,1,0:T(4,128)S(1)} %add_rows.5.first_ref), channel_id=1, source_target_pairs={{0,1},{1,0},{2,3},{3,2},{4,5},{5,4},{6,7},{7,6},{8,9},{9,8},{10,11... | collective-permute-start | bytes 73736 | tf_op jit(solution)/shard_map/ppermute | solution.py:443
  54.0 4.3 %collective-permute-start.13 = (f32[8,3,512]{2,1,0:T(4,128)S(1)}, f32[8,3,512]{2,1,0:T(4,128)S(1)}, u32[]{:S(2)}, u32[]{:S(2)}) collective-permute-start(f32[8,3,512]{2,1,0:T(4,128)S(1)} %join_rows.2.first_ref), channel_id=1, source_target_pairs={{0,2},{1,3},{2,0},{3,1},{4,6},{5,7},{6,4},{7,5},{8,10},{9,11},{10,... | collective-permute-start | bytes 147464 | tf_op jit(solution)/shard_map/ppermute | solution.py:443
where the time goes:
time: 66.9 us; the launch traced here: 66.5 us
  starting transfers between devices  23.9 us (36%)
  Pallas kernels  23.2 us (35%)
  waiting for transfers between devices  14.2 us (21%)
  local copies, waits for them, and re-layouts  4.24 us (6%)
  between operations  0.89 us (1%)
    pallas_call x15, Pallas kernels, run(): pl.pallas_call(body, in_specs=in_specs, out_specs=out_specs, out_shape=ou...  23.2 us
    ppermute x9, starting transfers between devices, send(): return lax.ppermute(value, 'ctx', moves)  16.2 us
    ppermute x2, waiting for transfers between devices, filter_gradients(): other = lax.ppermute(rows, 'chan', [(i, i ^ bit) for i in range(count)])  5.17 us
    ppermute x2, starting transfers between devices, sum_over_chips(): lax.ppermute(rows, 'ctx', [(i, i ^ bit) for i in range(count)])  4.55 us
    ppermute x2, waiting for transfers between devices, sum_over_chips(): lax.ppermute(rows, 'ctx', [(i, i ^ bit) for i in range(count)])  4.31 us
    unnamed x22, local copies, waits for them, and re-layouts  4.07 us
    ppermute x2, starting transfers between devices, filter_gradients(): other = lax.ppermute(rows, 'chan', [(i, i ^ bit) for i in range(count)])  3.08 us
    ppermute x9, waiting for transfers between devices, send(): return lax.ppermute(value, 'ctx', moves)  2.61 us
  transfers between devices with their start and end apart: 14, of which 6 were waited for; matrix products, arithmetic and copies ran while one was open for 0% of the time, Pallas kernels for 28%

commit v1 on v0

v1 whole, which is shorter than its diff:
```python
import functools
import math

import jax
import jax.numpy as jnp
from jax import lax
from jax.experimental import pallas as pl
from jax.experimental.pallas import tpu as pltpu
from jax.sharding import PartitionSpec as P

GSIZE = 512
WIN = 4
VMEM_LIMIT = 16 * 1024 * 1024
SCALE = 1
BF16 = jnp.bfloat16
F32 = jnp.float32

VMEM = pl.BlockSpec(memory_space=pltpu.VMEM)
SMEM = pl.BlockSpec(memory_space=pltpu.SMEM)
HBM = pl.BlockSpec(memory_space=pltpu.HBM)


def core_of():
    return lax.rem(lax.axis_index("ctx"), 2)


def call(body, name, out_shape, in_specs, out_specs, scratch=(), aliases=None, limit=VMEM_LIMIT, flops=1):
    def run(*args):
        moved = sum(a.size * a.dtype.itemsize for a in args + tuple(jax.tree.leaves(out_shape)))
        return pl.pallas_call(
            body,
            in_specs=in_specs,
            out_specs=out_specs,
            out_shape=out_shape,
            scratch_shapes=scratch,
            input_output_aliases=aliases or {},
            compiler_params=pltpu.CompilerParams(vmem_limit_bytes=limit),
            cost_estimate=pl.CostEstimate(flops=flops, bytes_accessed=max(1, moved // SCALE), transcendentals=0),
            name=name,
        )(*args)

    return run


def block_group(half, block, width, bw):
    first = lax.axis_index("chan") * width + half * (width // 2) + block * bw
    return lax.div(first, GSIZE)


def rolled(value, shift):
    shift %= value.shape[1]
    if shift % 128 == 0:
        return value if shift == 0 else jnp.concatenate([value[:, -shift:], value[:, :-shift]], axis=1)
    return pltpu.roll(value, shift, 1)


def skew(taps, span):
    width = 2 * span
    row = rolled(jnp.broadcast_to(taps, (8, width)), span)
    index = lax.broadcasted_iota(jnp.int32, (8, width), 0)
    for bit in (1, 2, 4):
        row = jnp.where((index & bit) != 0, rolled(row, bit), row)
    filled = 8
    while filled < span:
        row = jnp.concatenate([row, rolled(row, filled)], axis=0)
        filled *= 2
    return row[:, :span]


def diagonal_sums(matrix, span):
    width = 2 * span
    rows = jnp.concatenate([matrix, jnp.zeros((span, span), F32)], axis=1)
    half = span // 2
    while half >= 8:
        rows = rows[:half] + rolled(rows[half:], -half)
        half //= 2
    index = lax.broadcasted_iota(jnp.int32, (8, width), 0)
    for bit in (1, 2, 4):
        rows = jnp.where((index & bit) != 0, rolled(rows, -bit), rows)
    return rolled(jnp.sum(rows, axis=0, keepdims=True), span)


def stream_products(wanted, streams, name):
    span, width = streams[0].shape
    hw = width // 2
    count = len(wanted)

    def body(k_ref, v_ref, q_ref, g_ref, *rest):
        outs, (held, sems) = rest[:-2], rest[-2:]
        core = core_of()

        def copies(at, pair):
            half = 1 - core if wanted[at][1] == "0" else core
            columns = pl.ds(pl.multiple_of(half * hw, 128), hw)
            return [
                pltpu.make_async_copy(ref.at[:, columns], held.at[at, i], sems.at[at, i])
                for i, ref in enumerate(pair)
            ]

        for at, kind in enumerate(wanted):
            mixed_core = 0 if kind[0] == "P" else 1
            for is_mixed, pair in ((True, (k_ref, v_ref)), (False, (g_ref, q_ref))):

                @pl.when((core == mixed_core) == is_mixed)
                def _():
                    for copy in copies(at, pair):
                        copy.start()

        for at in range(count):
            for copy in copies(at, (k_ref, v_ref)):
                copy.wait()
            product = (held[at, 0].astype(F32) * held[at, 1].astype(F32)).astype(BF16)
            outs[at][...] = product

    return call(
        body,
        name,
        [jax.ShapeDtypeStruct((span, hw), BF16)] * count,
        [HBM] * 4,
        [VMEM] * count,
        [pltpu.VMEM((count, 2, span, hw), BF16), pltpu.SemaphoreType.DMA((count, 2))],
    )(*streams)


def short_lag(lag_ref, group, slots):
    lag = lag_ref[group * slots]
    for slot in range(1, slots):
        lag = jnp.minimum(lag, lag_ref[group * slots + slot])
    return lag


def toeplitz_matrices(lags, far_taps, near_taps, span, width, bw):
    groups, slots, doubled = far_taps.shape
    nb = width // 2 // bw

    def body(lag_ref, far_ref, near_ref, out_ref, near_rows):
        core = core_of()
        near_rows[...] = near_ref[...].astype(F32)
        for frame in range(2):
            half = core if frame == 0 else 1 - core
            for b in range(nb):
                group = block_group(half, b, width, bw)
                far = far_ref[group].astype(F32)
                near = near_rows[pl.ds(group, 1), :]
                short = last = jnp.zeros((1, doubled), F32)
                for slot in range(slots):
                    is_last = lag_ref[group * slots + slot] == WIN - 1
                    taps = far[slot : slot + 1]
                    short = jnp.where(is_last, short, taps)
                    last = jnp.where(is_last, taps, last)
                near = jnp.concatenate([jnp.zeros((1, span), F32), near], axis=1)
                for at, taps in enumerate((near, short, last)):
                    matrix = skew(taps, span)
                    out_ref[1 - core, frame * nb + b, at] = matrix.astype(BF16)
                    out_ref[core, frame * nb + b, at] = matrix.T.astype(BF16)

    return call(
        body,
        "toeplitz",
        jax.ShapeDtypeStruct((2, 2 * nb, 3, span, span), BF16),
        [SMEM, VMEM, VMEM],
        VMEM,
        [pltpu.VMEM((groups, span), F32)],
    )(lags, far_taps, near_taps)


def outer(mixed, gated):
    return lax.dot_general(mixed, gated, (((1,), (1,)), ((), ())), preferred_element_type=F32)


def by_core(body):
    core = core_of()

    @pl.when(core == 0)
    def _():
        body(outer)

    @pl.when(core != 0)
    def _():
        body(lambda p, q: outer(q, p))


def correlate_near(p_own, q_own):
    span, hw = p_own[0].shape
    bw = min(GSIZE, hw)
    nb = hw // bw

    def body(p0, p1, q0, q1, rows_ref):
        def run(pair):
            for frame in range(2):
                for b in range(nb):
                    at = pl.ds(b * bw, bw)
                    matrix = pair((p0, p1)[frame][:, at], (q0, q1)[frame][:, at])
                    rows_ref[frame, pl.ds(b, 1), :] = diagonal_sums(matrix, span)

        by_core(run)

    return call(
        body,
        "correlate_near",
        jax.ShapeDtypeStruct((2, nb, 2 * span), F32),
        [VMEM] * 4,
        VMEM,
    )(*p_own, *q_own)


def correlate_far(lags, slots, near, p_own, q_own, r1, x0, x1, r2):
    span, hw = r2.shape
    bw = min(GSIZE, hw)
    nb = hw // bw

    def body(lag_ref, near_ref, p0, p1, q_ref, r1_ref, x0_ref, x10, x11, r2_ref, out_ref):
        core = core_of()

        def run(pair):
            for b in range(nb):
                at = pl.ds(b * bw, bw)
                p, x, r = p0[:, at], x10[:, at], r1_ref[:, at]
                is_one = short_lag(lag_ref, block_group(core, b, 2 * hw, bw), slots) == 1
                short = pair(jnp.where(is_one, r, p), jnp.where(is_one, q_ref[:, at], x))
                short += pair(p, jnp.where(is_one, x0_ref[:, at], jnp.zeros_like(p)))
                last = pair(r, x) + pair(p, r2_ref[:, at])
                other = pair(p1[:, at], x11[:, at])
                rows = [diagonal_sums(matrix, span) for matrix in (short, last, other)]
                empty = jnp.zeros_like(rows[0])
                for frame in range(2):
                    half = core if frame == 0 else 1 - core
                    group = block_group(half, b, 2 * hw, bw)
                    place = half * nb + b
                    if frame == 0:
                        close, distant = rows[0], rows[1]
                    else:
                        close = jnp.where(short_lag(lag_ref, group, slots) == 2, rows[2], empty)
                        distant = empty
                    out_ref[place, pl.ds(0, 1), :] = near_ref[frame, pl.ds(b, 1), :]
                    for slot in range(slots):
                        is_last = lag_ref[group * slots + slot] == WIN - 1
                        out_ref[place, pl.ds(1 + slot, 1), :] = jnp.where(is_last, distant, close)

        by_core(run)

    return call(
        body,
        "correlate_far",
        jax.ShapeDtypeStruct((2 * nb, slots + 1, 2 * span), F32),
        [SMEM] + [VMEM] * 9,
        VMEM,
    )(lags, near, *p_own, q_own[0], r1, x0, *x1, r2)


def partial_sums(lags, slots, toeplitz, p_own, r1, x2, key, query):
    span, hw = p_own[0].shape
    bw = min(GSIZE, hw)
    nb = hw // bw

    def body(lag_ref, t_ref, p0, p1, r10, r11, x20, x21, key_ref, query_ref, gate_ref, out_ref, sem):
        core = core_of()

        def load(ref):
            return pltpu.make_async_copy(ref, gate_ref, sem)

        @pl.when(core == 0)
        def _():
            load(query_ref).start()

        @pl.when(core != 0)
        def _():
            load(key_ref).start()

        for frame in range(2):
            half = core if frame == 0 else 1 - core
            for b in range(nb):
                at = pl.ds(b * bw, bw)
                group = block_group(half, b, 2 * hw, bw)
                is_one = short_lag(lag_ref, group, slots) == 1
                panel = jnp.where(is_one, (r10, r11)[frame][:, at], (x20, x21)[frame][:, at])
                total = jnp.dot(t_ref[0, frame * nb + b, 0], (p0, p1)[frame][:, at], preferred_element_type=F32)
                total += jnp.dot(t_ref[0, frame * nb + b, 1], panel, preferred_element_type=F32)
                out_ref[frame, :, at] = total
        load(key_ref).wait()

    return call(
        body,
        "partial_sums",
        [jax.ShapeDtypeStruct((span, 2 * hw), BF16), jax.ShapeDtypeStruct((2, span, hw), F32)],
        [SMEM] + [VMEM] * 7 + [HBM] * 2,
        [VMEM, VMEM],
        [pltpu.SemaphoreType.DMA],
    )(lags, toeplitz, *p_own, *r1, *x2, key, query)


def gated_output(role, panels, total_of, gates, results):
    span, width = gates[0].shape
    hw = width // 2
    bw = min(GSIZE, hw)
    nb = hw // bw
    role_at = 0 if role == "P" else 1
    count = len(panels)
    loads = len(gates) == 2

    def body(*refs):
        lag_ref, panel_refs, gate_refs = refs[0], refs[1:count], refs[count : count + len(gates)]
        block_ref, values_ref, held, sems = refs[-4 - loads : len(refs) - loads]
        core = core_of()
        to_block = core == role_at
        gate = refs[-1] if loads else gate_refs[0]

        def load(ref):
            return pltpu.make_async_copy(ref, gate, sems.at[2 * nb])

        def store(at, columns, ref):
            return pltpu.make_async_copy(held.at[at], ref.at[:, columns], sems.at[at])

        if loads:

            @pl.when(to_block)
            def _():
                load(gate_refs[1]).start()

            @pl.when(jnp.logical_not(to_block))
            def _():
                load(gate_refs[0]).start()

        for frame in range(2):
            half = core if frame == 0 else 1 - core
            for b in range(nb):
                at = frame * nb + b
                group = block_group(half, b, width, bw)
                total = total_of(lag_ref, group, frame, b, at, pl.ds(b * bw, bw), *panel_refs)
                if at == 0 and loads:
                    load(gate_refs[0]).wait()
                columns = pl.ds(pl.multiple_of(half * hw + b * bw, 128), bw)
                held[at] = (total * gate[:, columns].astype(F32)).astype(BF16)

                @pl.when(to_block)
                def _():
                    store(at, columns, block_ref).start()

                @pl.when(jnp.logical_not(to_block))
                def _():
                    store(at, columns, values_ref).start()

        for at in range(2 * nb):
            store(at, pl.ds(0, bw), block_ref).wait()

    shape = jax.ShapeDtypeStruct((span, width), BF16)
    scratch = [pltpu.VMEM((2 * nb, span, bw), BF16), pltpu.SemaphoreType.DMA((2 * nb + 1,))]
    if loads:
        scratch.append(pltpu.VMEM((span, width), BF16))
    first = count + len(gates)
    return call(
        body,
        f"out_{role.lower()}",
        [shape, shape],
        [SMEM] + [VMEM] * (count - 1) + [HBM if loads else VMEM] * len(gates) + [HBM] * len(results),
        [HBM, HBM],
        scratch,
        {first: 0, first + 1: 1} if results else None,
    )(*panels, *gates, *results)


def q_output(lags, slots, toeplitz, q_own, x0, x1, r2, key, query):
    def total_of(lag_ref, group, frame, b, place, at, t_ref, q0, q1, x00, x01, x10, x11, r20, r21):
        is_one = short_lag(lag_ref, group, slots) == 1
        panel = jnp.where(is_one, (x00, x01)[frame][:, at], (x10, x11)[frame][:, at])
        total = jnp.dot(t_ref[1, place, 0], (q0, q1)[frame][:, at], preferred_element_type=F32)
        total += jnp.dot(t_ref[1, place, 1], panel, preferred_element_type=F32)
        return total + jnp.dot(t_ref[1, place, 2], (r20, r21)[frame][:, at], preferred_element_type=F32)

    return gated_output("Q", (lags, toeplitz, *q_own, *x0, *x1, *r2), total_of, (key, query), ())


def p_output(lags, toeplitz, sums, r3, gate, results):
    def total_of(lag_ref, group, frame, b, place, at, t_ref, sums_ref, r3_ref):
        last = jnp.dot(t_ref[0, place, 2], r3_ref[frame, :, at], preferred_element_type=F32)
        return sums_ref[frame, :, at] + last

    return gated_output("P", (lags, toeplitz, sums, r3), total_of, (gate,), results)


def after(value, *others):
    return lax.optimization_barrier((value,) + others)[0]


def stacked(parts):
    def body(*refs):
        for i, ref in enumerate(refs[:-1]):
            refs[-1][i] = ref[...]

    shape = jax.ShapeDtypeStruct((len(parts),) + parts[0].shape, parts[0].dtype)
    return call(body, "stack", shape, [VMEM] * len(parts), VMEM)(*parts)


def added(parts):
    def body(*refs):
        terms = [ref[...] for ref in refs[:-1]]
        while len(terms) > 1:
            terms = [a + b for a, b in zip(terms[::2], terms[1::2])]
        refs[-1][...] = terms[0]

    shape = jax.ShapeDtypeStruct(parts[0].shape, F32)
    return call(body, "add_rows", shape, [VMEM] * len(parts), VMEM)(*parts)


def sum_over_chips(rows, work):
    count = lax.axis_size("ctx")
    if count & (count - 1):
        return lax.psum(rows, "ctx")
    bit = 2
    while bit < count:
        steps = [k * bit for k in range(1, 4) if k * bit < count]
        others = [lax.ppermute(rows, "ctx", [(i, i ^ step) for i in range(count)]) for step in steps]
        if bit == 2:
            others = lax.optimization_barrier((others, work))[0]
        rows = added([rows] + others)
        bit *= 4
    return rows


def sum_over_cores(rows):
    count = lax.axis_size("ctx")
    if count & (count - 1):
        return rows
    return added([rows, lax.ppermute(rows, "ctx", [(i, i ^ 1) for i in range(count)])])


def joined(first, second, bit):
    def body(first_ref, second_ref, out_ref):
        length = first_ref.shape[0]
        here = lax.rem(lax.div(lax.axis_index("chan"), bit), 2)
        out_ref[pl.ds(here * length, length)] = first_ref[...]
        out_ref[pl.ds((1 - here) * length, length)] = second_ref[...]

    shape = jax.ShapeDtypeStruct((2 * first.shape[0],) + first.shape[1:], F32)
    return call(body, "join_rows", shape, [VMEM] * 2, VMEM)(first, second)


def gather_over_chan(rows, work):
    count = lax.axis_size("chan")
    if count & (count - 1):
        return lax.all_gather(rows, "chan", axis=0, tiled=True)
    bit = 1
    while bit < count:
        other = lax.ppermute(rows, "chan", [(i, i ^ bit) for i in range(count)])
        if bit == 1:
            other = after(other, work)
        rows = joined(rows, other, bit)
        bit *= 2
    return rows


def filter_gradients(rows, groups, span, scale):
    _, rows_per, doubled = rows.shape
    slots = rows_per - 1
    repeat = rows.shape[0] // groups

    def body(rows_ref, far_ref, near_ref):
        for group in range(groups):
            total = rows_ref[group * repeat]
            for at in range(1, repeat):
                total = total + rows_ref[group * repeat + at]
            far_ref[group] = total[1:] * scale
            near_ref[pl.ds(group, 1), :] = total[:1, span:] * scale

    return call(
        body,
        "filter_gradients",
        [
            jax.ShapeDtypeStruct((groups, slots, doubled), F32),
            jax.ShapeDtypeStruct((groups, span), F32),
        ],
        [VMEM],
        [VMEM, VMEM],
    )(rows)


def per_device(
    key_stream, value_stream, query_stream, grad_out, distant_lag_taps, near_taps, lag_blocks
):
    span, width = key_stream.shape
    groups = distant_lag_taps.shape[0]
    count = lax.axis_size("ctx")
    hw = width // 2
    bw = min(GSIZE, hw)

    def keep(moves):
        return [(a, b) for a, b in moves if 0 <= b < count]

    swap = [(i, i ^ 1) for i in range(count)]
    to_near = keep([(i, i + 1 if i % 2 else i - 1) for i in range(count)])
    to_far = keep([(i, i - 3 if i % 2 else i + 3) for i in range(count)])
    onward = keep([(i, i - 2 if i % 2 else i + 2) for i in range(count)])

    def send(value, moves):
        return lax.ppermute(value, "ctx", moves)

    slots = lag_blocks.shape[1]
    streams = (key_stream, value_stream, query_stream, grad_out)
    streams = tuple(pltpu.with_memory_space_constraint(x, pltpu.HBM) for x in streams)
    qa, qb = stream_products(("Q0", "Q1"), streams, "q_stream")
    r1a, r1b = send(qa, to_near), send(qb, to_near)
    *late, far_taps, near_taps, lags, _ = lax.optimization_barrier(
        streams + (distant_lag_taps, near_taps, lag_blocks, qb)
    )
    lags = lags.reshape(-1)
    pa, pb = stream_products(("P0", "P1"), late, "p_stream")
    q_own, p_own = (qb, qa), (pb, pa)
    toeplitz = toeplitz_matrices(lags, far_taps, near_taps, span, width, bw)
    near = correlate_near(p_own, q_own)

    r2a = send(after(pa, near, toeplitz), to_far)
    r1 = lax.optimization_barrier(((r1a, r1b), toeplitz, near))[0]
    x1 = (send(r1[1], swap), send(r1[0], swap))
    x0a = send(after(pa, r1), swap)
    r2b = send(after(pb, r1), to_far)
    both, r1 = lax.optimization_barrier((stacked(r1), r1))
    rows = correlate_far(lags, slots, near, p_own, q_own, r1[0], x0a, x1, r2a)
    x0b = send(after(pb, rows), swap)

    gates = (key_stream, query_stream)
    results = q_output(lags, slots, toeplitz, q_own, (x0a, x0b), x1, (r2a, r2b), *gates)
    rows = sum_over_chips(rows, results[0])
    both, r2_late, rows = lax.optimization_barrier((both, (r2a, r2b), rows))
    r3 = send(both, onward)
    x2 = (send(r2_late[1], swap), send(r2_late[0], swap))
    rows = sum_over_cores(rows)
    gate, sums = partial_sums(lags, slots, toeplitz, p_own, r1, x2, *gates)
    rows = gather_over_chan(rows, sums)
    scale = 1.0 / math.sqrt(span * count * GSIZE)
    far, near = filter_gradients(rows, groups, span, scale)
    results = p_output(lags, toeplitz, sums, r3, gate, results)
    return (results[0], results[1], far, near)


def solution(mesh):
    streams = P("ctx", "chan")
    return jax.shard_map(
        per_device,
        mesh=mesh,
        in_specs=(streams, streams, streams, streams, P(), P(), P()),
        out_specs=(streams, streams, P(), P()),
        check_vma=False,
    )
```

time: 66.9 us -> 54 us (0.81)
  Pallas kernels: 23.2 us -> 16.6 us
  local copies, waits for them, and re-layouts: 4.24 us -> 0.2 us
  waiting for transfers between devices: 14.2 us -> 10.2 us
  starting transfers between devices: 23.9 us -> 25.8 us
    pallas_call x15 -> x14, Pallas kernels: 23.2 us -> 16.6 us  [run(): pl.pallas_call(body, in_specs=in_specs, out_specs=out_specs, out_shape=ou...]
    unnamed x22 -> x10, local copies, waits for them, and re-layouts: 4.07 us -> 0.03 us
    ppermute x4 -> x5, waiting for transfers between devices: 9.48 us -> 5.5 us  [the longest x2 3.75 us: gather_over_chan(): other = lax.ppermute(rows, 'chan', [(i, i ^ bit) for i in range(count)])]
    ppermute x9 -> x11, starting transfers between devices: 16.2 us -> 17.7 us  [send(): return lax.ppermute(value, 'ctx', moves)]
    ppermute x4 -> x5, starting transfers between devices: 7.63 us -> 8 us  [the longest x3 4.92 us: sum_over_chips(): lax.ppermute(rows, 'ctx', [(i, i ^ step) for i in range(count)])]
    ppermute x9 -> x11, waiting for transfers between devices: 2.61 us -> 2.6 us  [send(): return lax.ppermute(value, 'ctx', moves)]
  transfers between devices with their start and end apart: 14 -> 17, of which waited for: 6 -> 7; matrix products, arithmetic and copies ran while one was open for 0% -> 0% of each run, Pallas kernels for 28% -> 24%
where the time goes in v1:
time: 54 us; the launch traced here: 53.7 us
  starting transfers between devices  25.8 us (48%)
  Pallas kernels  16.6 us (31%)
  waiting for transfers between devices  10.2 us (19%)
  between operations  0.87 us (2%)
    ppermute x11, starting transfers between devices, send(): return lax.ppermute(value, 'ctx', moves)  17.7 us
    pallas_call x14, Pallas kernels, run(): pl.pallas_call(body, in_specs=in_specs, out_specs=out_specs, out_shape=ou...  16.6 us
    ppermute x3, starting transfers between devices, sum_over_chips(): lax.ppermute(rows, 'ctx', [(i, i ^ step) for i in range(count)])  4.92 us
    ppermute x2, waiting for transfers between devices, gather_over_chan(): other = lax.ppermute(rows, 'chan', [(i, i ^ bit) for i in range(count)])  3.75 us
    ppermute x2, starting transfers between devices, gather_over_chan(): other = lax.ppermute(rows, 'chan', [(i, i ^ bit) for i in range(count)])  3.08 us
    ppermute x11, waiting for transfers between devices, send(): return lax.ppermute(value, 'ctx', moves)  2.6 us
    ppermute x1, waiting for transfers between devices, sum_over_cores(): lax.ppermute(rows, 'ctx', [(i, i ^ 1) for i in range(count)])  2.12 us
    ppermute x3, waiting for transfers between devices, sum_over_chips(): lax.ppermute(rows, 'ctx', [(i, i ^ step) for i in range(count)])  1.74 us
  transfers between devices with their start and end apart: 17, of which 7 were waited for; matrix products, arithmetic and copies ran while one was open for 0% of the time, Pallas kernels for 24%

profile of v1, /device:TPU:0, one launch (start us, length us, event | category | flops | bytes accessed | tf_op | source)
XLA Modules:
  0.0 53.7 jit_solution(6743970670911682007)
XLA Ops:
  0.6 1.7 %q_stream.1 = (bf16[256,1024]{1,0:T(8,128)(2,1)S(1)}, bf16[256,1024]{1,0:T(8,128)(2,1)S(1)}) custom-call(bf16[256,2048]{1,0:T(8,128)(2,1)} %key_ref.1, bf16[256,2048]{1,0:T(8,128)(2,1)} %v_ref.2, bf16[256,2048]{1,0:T(8,128)(2,1)} %query_ref.1, bf16[256,2048]{1,0:T(8,128)(2,1)} %g_ref.2), custom_call_target="tpu_custom_call" | custom-call | flops 1 | bytes 5242880 | tf_op jit(solution)/shard_map/q_stream/pallas_call | solution.py:30
  2.3 0.7 %collective-permute-start.1 = (bf16[256,1024]{1,0:T(8,128)(2,1)S(1)}, bf16[256,1024]{1,0:T(8,128)(2,1)S(1)}, u32[]{:S(2)}, u32[]{:S(2)}) collective-permute-start(bf16[256,1024]{1,0:T(8,128)(2,1)S(1)} %get-tuple-element.40.q0.q_ref.refs_2_), channel_id=1, source_target_pairs={{4,8},{8,4},{12,16},{16,12},{20,24},{24,20},{5,9},{9,5},{13,17},{1... | collective-permute-start | bytes 1572872 | tf_op jit(solution)/shard_map/ppermute | solution.py:495
  3.1 0.8 %collective-permute-start = (bf16[256,1024]{1,0:T(8,128)(2,1)S(1)}, bf16[256,1024]{1,0:T(8,128)(2,1)S(1)}, u32[]{:S(2)}, u32[]{:S(2)}) collective-permute-start(bf16[256,1024]{1,0:T(8,128)(2,1)S(1)} %get-tuple-element.50.q1.refs_3_), channel_id=1, source_target_pairs={{4,8},{8,4},{12,16},{16,12},{20,24},{24,20},{5,9},{9,5},{13,17},{1... | collective-permute-start | bytes 1572872 | tf_op jit(solution)/shard_map/ppermute | solution.py:495
  3.9 1.7 %p_stream.1 = (bf16[256,1024]{1,0:T(8,128)(2,1)S(1)}, bf16[256,1024]{1,0:T(8,128)(2,1)S(1)}) custom-call(bf16[256,2048]{1,0:T(8,128)(2,1)} %key_ref.1, bf16[256,2048]{1,0:T(8,128)(2,1)} %v_ref.2, bf16[256,2048]{1,0:T(8,128)(2,1)} %query_ref.1, bf16[256,2048]{1,0:T(8,128)(2,1)} %g_ref.2), custom_call_target="tpu_custom_call" | custom-call | flops 1 | bytes 5242880 | tf_op jit(solution)/shard_map/p_stream/pallas_call | solution.py:30
  5.6 1.0 %correlate_near.1.near_ref = f32[2,2,512]{2,1,0:T(2,128)S(1)} custom-call(bf16[256,1024]{1,0:T(8,128)(2,1)S(1)} %get-tuple-element.59.p0, bf16[256,1024]{1,0:T(8,128)(2,1)S(1)} %get-tuple-element.58.p1, bf16[256,1024]{1,0:T(8,128)(2,1)S(1)} %get-tuple-element.40.q0.q_ref.refs_2_, bf16[256,1024]{1,0:T(8,128)(2,1)S(1)} %get-tuple-element.50.q1.refs_3_), custom_call_target="tpu_custom_call" | custom-call | flops 1 | bytes 2105344 | tf_op jit(solution)/shard_map/correlate_near/pallas_call | solution.py:30
  6.6 0.1 copy.14
  6.7 0.1 reshape.11.lag_ref.refs_0_
  6.8 3.7 %toeplitz.1.refs_1_.t_ref = bf16[2,4,3,256,256]{4,3,2,1,0:T(8,128)(2,1)S(1)} custom-call(s32[32]{0:T(128)S(1)} %reshape.11.lag_ref.refs_0_, bf16[16,2,512]{2,1,0:T(2,128)(2,1)S(1)} %copy-done.2, bf16[16,256]{1,0:T(8,128)(2,1)S(1)} %copy-done.3), custom_call_target="tpu_custom_call" | custom-call | flops 1 | bytes 3186816 | tf_op jit(solution)/shard_map/toeplitz/pallas_call | solution.py:30
  10.5 8.8 %collective-permute-start.2 = (bf16[256,1024]{1,0:T(8,128)(2,1)S(1)}, bf16[256,1024]{1,0:T(8,128)(2,1)S(1)}, u32[]{:S(2)}, u32[]{:S(2)}) collective-permute-start(bf16[256,1024]{1,0:T(8,128)(2,1)S(1)} %get-tuple-element.58.p1), channel_id=1, source_target_pairs={{0,12},{8,20},{12,0},{16,28},{20,8},{28,16},{1,13},{9,21},{13,1},{... | collective-permute-start | bytes 1572872 | tf_op jit(solution)/shard_map/ppermute | solution.py:495
  19.3 0.5 collective-permute-start.4
  19.9 0.5 collective-permute-start.6
  20.4 3.6 %collective-permute-start.3 = (bf16[256,1024]{1,0:T(8,128)(2,1)S(1)}, bf16[256,1024]{1,0:T(8,128)(2,1)S(1)}, u32[]{:S(2)}, u32[]{:S(2)}) collective-permute-start(bf16[256,1024]{1,0:T(8,128)(2,1)S(1)} %get-tuple-element.59.p0), channel_id=1, source_target_pairs={{0,12},{8,20},{12,0},{16,28},{20,8},{28,16},{1,13},{9,21},{13,1},{... | collective-permute-start | bytes 1572872 | tf_op jit(solution)/shard_map/ppermute | solution.py:495
  24.1 2.1 %collective-permute-done.2.r2_ref.refs_8_ = bf16[256,1024]{1,0:T(8,128)(2,1)S(1)} collective-permute-done((bf16[256,1024]{1,0:T(8,128)(2,1)S(1)}, bf16[256,1024]{1,0:T(8,128)(2,1)S(1)}, u32[]{:S(2)}, u32[]{:S(2)}) %collective-permute-start.2) | collective-permute-done | bytes 524320 | tf_op jit(solution)/shard_map/ppermute | solution.py:495
  26.2 2.0 %correlate_far.1.refs_0_ = f32[4,3,512]{2,1,0:T(4,128)S(1)} custom-call(s32[32]{0:T(128)S(1)} %reshape.11.lag_ref.refs_0_, f32[2,2,512]{2,1,0:T(2,128)S(1)} %correlate_near.1.near_ref, bf16[256,1024]{1,0:T(8,128)(2,1)S(1)} %get-tuple-element.59.p0, bf16[256,1024]{1,0:T(8,128)(2,1)S(1)} %get-tuple-element.58.p1, ...), custom_call_target="tpu_custom_call" | custom-call | flops 1 | bytes 4227200 | tf_op jit(solution)/shard_map/correlate_far/pallas_call | solution.py:30
  28.3 2.4 %collective-permute-start.7 = (f32[4,3,512]{2,1,0:T(4,128)S(1)}, f32[4,3,512]{2,1,0:T(4,128)S(1)}, u32[]{:S(2)}, u32[]{:S(2)}) collective-permute-start(f32[4,3,512]{2,1,0:T(4,128)S(1)} %correlate_far.1.refs_0_), channel_id=1, source_target_pairs={{0,8},{4,12},{8,0},{12,4},{16,24},{20,28},{24,16},{28,20},{1,9},{5... | collective-permute-start | bytes 73736 | tf_op jit(solution)/shard_map/ppermute | solution.py:412
  30.7 1.2 %collective-permute-start.8 = (f32[4,3,512]{2,1,0:T(4,128)S(1)}, f32[4,3,512]{2,1,0:T(4,128)S(1)}, u32[]{:S(2)}, u32[]{:S(2)}) collective-permute-start(f32[4,3,512]{2,1,0:T(4,128)S(1)} %correlate_far.1.refs_0_), channel_id=1, source_target_pairs={{0,16},{4,20},{8,24},{12,28},{16,0},{20,4},{24,8},{28,12},{1,17},{... | collective-permute-start | bytes 73736 | tf_op jit(solution)/shard_map/ppermute | solution.py:412
  31.9 1.3 %collective-permute-start.9 = (f32[4,3,512]{2,1,0:T(4,128)S(1)}, f32[4,3,512]{2,1,0:T(4,128)S(1)}, u32[]{:S(2)}, u32[]{:S(2)}) collective-permute-start(f32[4,3,512]{2,1,0:T(4,128)S(1)} %correlate_far.1.refs_0_), channel_id=1, source_target_pairs={{0,24},{4,28},{8,16},{12,20},{16,8},{20,12},{24,0},{28,4},{1,25},{... | collective-permute-start | bytes 73736 | tf_op jit(solution)/shard_map/ppermute | solution.py:412
  33.2 2.6 %out_q.1 = (bf16[256,2048]{1,0:T(8,128)(2,1)}, bf16[256,2048]{1,0:T(8,128)(2,1)}) custom-call(s32[32]{0:T(128)S(1)} %reshape.11.lag_ref.refs_0_, bf16[2,4,3,256,256]{4,3,2,1,0:T(8,128)(2,1)S(1)} %toeplitz.1.refs_1_.t_ref, bf16[256,1024]{1,0:T(8,128)(2,1)S(1)} %get-tuple-element.40.q0.q_ref.refs_2_, bf16[256,1024]{1,0:T(8,128)(2,1)S(1)} %get-tuple-element.50.q1.refs_3_, ...), custom_call_target="tpu_custom_call" | custom-call | flops 1 | bytes 11534464 | tf_op jit(solution)/shard_map/out_q/pallas_call | solution.py:30
  35.9 0.7 %collective-permute-done.8.refs_2_ = f32[4,3,512]{2,1,0:T(4,128)S(1)} collective-permute-done((f32[4,3,512]{2,1,0:T(4,128)S(1)}, f32[4,3,512]{2,1,0:T(4,128)S(1)}, u32[]{:S(2)}, u32[]{:S(2)}) %collective-permute-start.8) | collective-permute-done | bytes 24608 | tf_op jit(solution)/shard_map/ppermute | solution.py:412
  36.5 1.0 %collective-permute-done.9.refs_3_ = f32[4,3,512]{2,1,0:T(4,128)S(1)} collective-permute-done((f32[4,3,512]{2,1,0:T(4,128)S(1)}, f32[4,3,512]{2,1,0:T(4,128)S(1)}, u32[]{:S(2)}, u32[]{:S(2)}) %collective-permute-start.9) | collective-permute-done | bytes 24608 | tf_op jit(solution)/shard_map/ppermute | solution.py:412
  37.6 2.0 %collective-permute-start.13 = (bf16[2,256,1024]{2,1,0:T(8,128)(2,1)S(1)}, bf16[2,256,1024]{2,1,0:T(8,128)(2,1)S(1)}, u32[]{:S(2)}, u32[]{:S(2)}) collective-permute-start(bf16[2,256,1024]{2,1,0:T(8,128)(2,1)S(1)} %stack.1), channel_id=1, source_target_pairs={{0,8},{8,16},{12,4},{16,24},{20,12},{28,20},{1,9},{9,17},{13,5},{1... | collective-permute-start | bytes 3145736 | tf_op jit(solution)/shard_map/ppermute | solution.py:495
  39.7 0.5 collective-permute-start.12
  40.2 0.1 collective-permute-start.14
  40.3 2.1 %collective-permute-done.14.refs_1_ = f32[4,3,512]{2,1,0:T(4,128)S(1)} collective-permute-done((f32[4,3,512]{2,1,0:T(4,128)S(1)}, f32[4,3,512]{2,1,0:T(4,128)S(1)}, u32[]{:S(2)}, u32[]{:S(2)}) %collective-permute-start.14) | collective-permute-done | bytes 24608 | tf_op jit(solution)/shard_map/ppermute | solution.py:424
  42.4 1.5 %collective-permute-start.15 = (f32[4,3,512]{2,1,0:T(4,128)S(1)}, f32[4,3,512]{2,1,0:T(4,128)S(1)}, u32[]{:S(2)}, u32[]{:S(2)}) collective-permute-start(f32[4,3,512]{2,1,0:T(4,128)S(1)} %add_rows.3.first_ref), channel_id=1, source_target_pairs={{0,1},{1,0},{2,3},{3,2},{4,5},{5,4},{6,7},{7,6},{8,9},{9,8},{10,11... | collective-permute-start | bytes 73736 | tf_op jit(solution)/shard_map/ppermute | solution.py:444
  43.9 1.4 %partial_sums.1 = (bf16[256,2048]{1,0:T(8,128)(2,1)S(1)}, f32[2,256,1024]{2,1,0:T(8,128)S(1)}) custom-call(s32[32]{0:T(128)S(1)} %reshape.11.lag_ref.refs_0_, bf16[2,4,3,256,256]{4,3,2,1,0:T(8,128)(2,1)S(1)} %toeplitz.1.refs_1_.t_ref, bf16[256,1024]{1,0:T(8,128)(2,1)S(1)} %get-tuple-element.59.p0, bf16[256,1024]{1,0:T(8,128)(2,1)S(1)} %get-tuple-element.58.p1, ...), custom_call_target="tpu_custom_call" | custom-call | flops 1 | bytes 11534464 | tf_op jit(solution)/shard_map/partial_sums/pallas_call | solution.py:30
  45.3 1.0 %collective-permute-done.15.second_ref = f32[4,3,512]{2,1,0:T(4,128)S(1)} collective-permute-done((f32[4,3,512]{2,1,0:T(4,128)S(1)}, f32[4,3,512]{2,1,0:T(4,128)S(1)}, u32[]{:S(2)}, u32[]{:S(2)}) %collective-permute-start.15) | collective-permute-done | bytes 24608 | tf_op jit(solution)/shard_map/ppermute | solution.py:444
  46.4 1.6 %collective-permute-start.16 = (f32[8,3,512]{2,1,0:T(4,128)S(1)}, f32[8,3,512]{2,1,0:T(4,128)S(1)}, u32[]{:S(2)}, u32[]{:S(2)}) collective-permute-start(f32[8,3,512]{2,1,0:T(4,128)S(1)} %join_rows.2.first_ref), channel_id=1, source_target_pairs={{0,2},{1,3},{2,0},{3,1},{4,6},{5,7},{6,4},{7,5},{8,10},{9,11},{10,... | collective-permute-start | bytes 147464 | tf_op jit(solution)/shard_map/ppermute | solution.py:444
  47.9 2.7 %collective-permute-done.16.second_ref = f32[8,3,512]{2,1,0:T(4,128)S(1)} collective-permute-done((f32[8,3,512]{2,1,0:T(4,128)S(1)}, f32[8,3,512]{2,1,0:T(4,128)S(1)}, u32[]{:S(2)}, u32[]{:S(2)}) %collective-permute-start.16) | collective-permute-done | bytes 49184 | tf_op jit(solution)/shard_map/ppermute | solution.py:444
  50.7 0.7 %filter_gradients.1 = (f32[16,2,512]{2,1,0:T(2,128)}, f32[16,256]{1,0:T(8,128)}) custom-call(f32[16,3,512]{2,1,0:T(4,128)S(1)} %join_rows.3.rows_ref), custom_call_target="tpu_custom_call" | custom-call | flops 1 | bytes 180224 | tf_op jit(solution)/shard_map/filter_gradients/pallas_call | solution.py:30
  51.4 0.5 collective-permute-done.13.refs_3_
  51.9 1.8 %out_p.1 = (bf16[256,2048]{1,0:T(8,128)(2,1)}, bf16[256,2048]{1,0:T(8,128)(2,1)}) custom-call(s32[32]{0:T(128)S(1)} %reshape.11.lag_ref.refs_0_, bf16[2,4,3,256,256]{4,3,2,1,0:T(8,128)(2,1)S(1)} %toeplitz.1.refs_1_.t_ref, f32[2,256,1024]{2,1,0:T(8,128)S(1)} %get-tuple-element.66.refs_2_, ...), custom_call_target="tpu_custom_call", output_to_operand_aliasing={{0}: (5, {}), {1}: (6, {})} | custom-call | flops 1 | bytes 11534464 | tf_op jit(solution)/shard_map/out_p/pallas_call | solution.py:30
  (28 shorter events, 0.4 us)
Async XLA Ops:
  2.3 17.0 %collective-permute-start.1 = (bf16[256,1024]{1,0:T(8,128)(2,1)S(1)}, bf16[256,1024]{1,0:T(8,128)(2,1)S(1)}, u32[]{:S(2)}, u32[]{:S(2)}) collective-permute-start(bf16[256,1024]{1,0:T(8,128)(2,1)S(1)} %get-tuple-element.40.q0.q_ref.refs_2_), channel_id=1, source_target_pairs={{4,8},{8,4},{12,16},{16,12},{20,24},{24,20},{5,9},{9,5},{13,17},{1... | collective-permute-start | bytes 1572872 | tf_op jit(solution)/shard_map/ppermute | solution.py:495
  3.0 3.6 %copy-start.4 = (s32[16,2]{0,1:T(2,128)S(1)}, s32[16,2]{0,1:T(2,128)}, u32[]{:S(2)}) copy-start(s32[16,2]{0,1:T(2,128)} %param.13) | copy-start | bytes 388
  3.0 3.8 %copy-start.2 = (bf16[16,2,512]{2,1,0:T(2,128)(2,1)S(1)}, bf16[16,2,512]{2,1,0:T(2,128)(2,1)}, u32[]{:S(2)}) copy-start(bf16[16,2,512]{2,1,0:T(2,128)(2,1)} %far_ref) | copy-start | bytes 98308
  3.1 3.8 %copy-start.3 = (bf16[16,256]{1,0:T(8,128)(2,1)S(1)}, bf16[16,256]{1,0:T(8,128)(2,1)}, u32[]{:S(2)}) copy-start(bf16[16,256]{1,0:T(8,128)(2,1)} %near_ref) | copy-start | bytes 24580
  3.1 16.3 %collective-permute-start = (bf16[256,1024]{1,0:T(8,128)(2,1)S(1)}, bf16[256,1024]{1,0:T(8,128)(2,1)S(1)}, u32[]{:S(2)}, u32[]{:S(2)}) collective-permute-start(bf16[256,1024]{1,0:T(8,128)(2,1)S(1)} %get-tuple-element.50.q1.refs_3_), channel_id=1, source_target_pairs={{4,8},{8,4},{12,16},{16,12},{20,24},{24,20},{5,9},{9,5},{13,17},{1... | collective-permute-start | bytes 1572872 | tf_op jit(solution)/shard_map/ppermute | solution.py:495
  10.5 22.7 %copy-start = (bf16[256,2048]{1,0:T(8,128)(2,1)S(1)}, bf16[256,2048]{1,0:T(8,128)(2,1)}, u32[]{:S(2)}) copy-start(bf16[256,2048]{1,0:T(8,128)(2,1)} %key_ref.1) | copy-start | bytes 3145732
  10.5 22.7 %copy-start.1 = (bf16[256,2048]{1,0:T(8,128)(2,1)S(1)}, bf16[256,2048]{1,0:T(8,128)(2,1)}, u32[]{:S(2)}) copy-start(bf16[256,2048]{1,0:T(8,128)(2,1)} %query_ref.1) | copy-start | bytes 3145732
  10.5 15.7 %collective-permute-start.2 = (bf16[256,1024]{1,0:T(8,128)(2,1)S(1)}, bf16[256,1024]{1,0:T(8,128)(2,1)S(1)}, u32[]{:S(2)}, u32[]{:S(2)}) collective-permute-start(bf16[256,1024]{1,0:T(8,128)(2,1)S(1)} %get-tuple-element.58.p1), channel_id=1, source_target_pairs={{0,12},{8,20},{12,0},{16,28},{20,8},{28,16},{1,13},{9,21},{13,1},{... | collective-permute-start | bytes 1572872 | tf_op jit(solution)/shard_map/ppermute | solution.py:495
  19.3 6.8 %collective-permute-start.4 = (bf16[256,1024]{1,0:T(8,128)(2,1)S(1)}, bf16[256,1024]{1,0:T(8,128)(2,1)S(1)}, u32[]{:S(2)}, u32[]{:S(2)}) collective-permute-start(bf16[256,1024]{1,0:T(8,128)(2,1)S(1)} %get-tuple-element.58.p1), channel_id=1, source_target_pairs={{0,4},{4,0},{8,12},{12,8},{16,20},{20,16},{24,28},{28,24},{1,5},{5... | collective-permute-start | bytes 1572872 | tf_op jit(solution)/shard_map/ppermute | solution.py:495
  19.9 6.3 %collective-permute-start.5 = (bf16[256,1024]{1,0:T(8,128)(2,1)S(1)}, bf16[256,1024]{1,0:T(8,128)(2,1)S(1)}, u32[]{:S(2)}, u32[]{:S(2)}) collective-permute-start(bf16[256,1024]{1,0:T(8,128)(2,1)S(1)} %collective-permute-done.1.refs_1_.r11), channel_id=1, source_target_pairs={{0,4},{4,0},{8,12},{12,8},{16,20},{20,16},{24,28},{28,24},{1,5},{5... | collective-permute-start | bytes 1572872 | tf_op jit(solution)/shard_map/ppermute | solution.py:495
  19.9 6.3 %collective-permute-start.6 = (bf16[256,1024]{1,0:T(8,128)(2,1)S(1)}, bf16[256,1024]{1,0:T(8,128)(2,1)S(1)}, u32[]{:S(2)}, u32[]{:S(2)}) collective-permute-start(bf16[256,1024]{1,0:T(8,128)(2,1)S(1)} %collective-permute-done.refs_0_.r1_ref.r10), channel_id=1, source_target_pairs={{0,4},{4,0},{8,12},{12,8},{16,20},{20,16},{24,28},{28,24},{1,5},{5... | collective-permute-start | bytes 1572872 | tf_op jit(solution)/shard_map/ppermute | solution.py:495
  20.4 12.8 %collective-permute-start.3 = (bf16[256,1024]{1,0:T(8,128)(2,1)S(1)}, bf16[256,1024]{1,0:T(8,128)(2,1)S(1)}, u32[]{:S(2)}, u32[]{:S(2)}) collective-permute-start(bf16[256,1024]{1,0:T(8,128)(2,1)S(1)} %get-tuple-element.59.p0), channel_id=1, source_target_pairs={{0,12},{8,20},{12,0},{16,28},{20,8},{28,16},{1,13},{9,21},{13,1},{... | collective-permute-start | bytes 1572872 | tf_op jit(solution)/shard_map/ppermute | solution.py:495
  28.2 5.0 %collective-permute-start.10 = (bf16[256,1024]{1,0:T(8,128)(2,1)S(1)}, bf16[256,1024]{1,0:T(8,128)(2,1)S(1)}, u32[]{:S(2)}, u32[]{:S(2)}) collective-permute-start(bf16[256,1024]{1,0:T(8,128)(2,1)S(1)} %get-tuple-element.59.p0), channel_id=1, source_target_pairs={{0,4},{4,0},{8,12},{12,8},{16,20},{20,16},{24,28},{28,24},{1,5},{5... | collective-permute-start | bytes 1572872 | tf_op jit(solution)/shard_map/ppermute | solution.py:495
  28.3 7.6 %collective-permute-start.7 = (f32[4,3,512]{2,1,0:T(4,128)S(1)}, f32[4,3,512]{2,1,0:T(4,128)S(1)}, u32[]{:S(2)}, u32[]{:S(2)}) collective-permute-start(f32[4,3,512]{2,1,0:T(4,128)S(1)} %correlate_far.1.refs_0_), channel_id=1, source_target_pairs={{0,8},{4,12},{8,0},{12,4},{16,24},{20,28},{24,16},{28,20},{1,9},{5... | collective-permute-start | bytes 73736 | tf_op jit(solution)/shard_map/ppermute | solution.py:412
  30.7 5.8 %collective-permute-start.8 = (f32[4,3,512]{2,1,0:T(4,128)S(1)}, f32[4,3,512]{2,1,0:T(4,128)S(1)}, u32[]{:S(2)}, u32[]{:S(2)}) collective-permute-start(f32[4,3,512]{2,1,0:T(4,128)S(1)} %correlate_far.1.refs_0_), channel_id=1, source_target_pairs={{0,16},{4,20},{8,24},{12,28},{16,0},{20,4},{24,8},{28,12},{1,17},{... | collective-permute-start | bytes 73736 | tf_op jit(solution)/shard_map/ppermute | solution.py:412
  31.9 5.7 %collective-permute-start.9 = (f32[4,3,512]{2,1,0:T(4,128)S(1)}, f32[4,3,512]{2,1,0:T(4,128)S(1)}, u32[]{:S(2)}, u32[]{:S(2)}) collective-permute-start(f32[4,3,512]{2,1,0:T(4,128)S(1)} %correlate_far.1.refs_0_), channel_id=1, source_target_pairs={{0,24},{4,28},{8,16},{12,20},{16,8},{20,12},{24,0},{28,4},{1,25},{... | collective-permute-start | bytes 73736 | tf_op jit(solution)/shard_map/ppermute | solution.py:412
  37.6 14.3 %collective-permute-start.13 = (bf16[2,256,1024]{2,1,0:T(8,128)(2,1)S(1)}, bf16[2,256,1024]{2,1,0:T(8,128)(2,1)S(1)}, u32[]{:S(2)}, u32[]{:S(2)}) collective-permute-start(bf16[2,256,1024]{2,1,0:T(8,128)(2,1)S(1)} %stack.1), channel_id=1, source_target_pairs={{0,8},{8,16},{12,4},{16,24},{20,12},{28,20},{1,9},{9,17},{13,5},{1... | collective-permute-start | bytes 3145736 | tf_op jit(solution)/shard_map/ppermute | solution.py:495
  39.7 4.3 %collective-permute-start.11 = (bf16[256,1024]{1,0:T(8,128)(2,1)S(1)}, bf16[256,1024]{1,0:T(8,128)(2,1)S(1)}, u32[]{:S(2)}, u32[]{:S(2)}) collective-permute-start(bf16[256,1024]{1,0:T(8,128)(2,1)S(1)} %collective-permute-done.3.refs_9_), channel_id=1, source_target_pairs={{0,4},{4,0},{8,12},{12,8},{16,20},{20,16},{24,28},{28,24},{1,5},{5... | collective-permute-start | bytes 1572872 | tf_op jit(solution)/shard_map/ppermute | solution.py:495
  39.7 4.2 %collective-permute-start.12 = (bf16[256,1024]{1,0:T(8,128)(2,1)S(1)}, bf16[256,1024]{1,0:T(8,128)(2,1)S(1)}, u32[]{:S(2)}, u32[]{:S(2)}) collective-permute-start(bf16[256,1024]{1,0:T(8,128)(2,1)S(1)} %collective-permute-done.2.r2_ref.refs_8_), channel_id=1, source_target_pairs={{0,4},{4,0},{8,12},{12,8},{16,20},{20,16},{24,28},{28,24},{1,5},{5... | collective-permute-start | bytes 1572872 | tf_op jit(solution)/shard_map/ppermute | solution.py:495
  40.2 2.2 %collective-permute-start.14 = (f32[4,3,512]{2,1,0:T(4,128)S(1)}, f32[4,3,512]{2,1,0:T(4,128)S(1)}, u32[]{:S(2)}, u32[]{:S(2)}) collective-permute-start(f32[4,3,512]{2,1,0:T(4,128)S(1)} %add_rows.2.refs_0_), channel_id=1, source_target_pairs={{0,4},{4,0},{8,12},{12,8},{16,20},{20,16},{24,28},{28,24},{1,5},{5... | collective-permute-start | bytes 73736 | tf_op jit(solution)/shard_map/ppermute | solution.py:424
  42.4 3.9 %collective-permute-start.15 = (f32[4,3,512]{2,1,0:T(4,128)S(1)}, f32[4,3,512]{2,1,0:T(4,128)S(1)}, u32[]{:S(2)}, u32[]{:S(2)}) collective-permute-start(f32[4,3,512]{2,1,0:T(4,128)S(1)} %add_rows.3.first_ref), channel_id=1, source_target_pairs={{0,1},{1,0},{2,3},{3,2},{4,5},{5,4},{6,7},{7,6},{8,9},{9,8},{10,11... | collective-permute-start | bytes 73736 | tf_op jit(solution)/shard_map/ppermute | solution.py:444
  46.4 4.3 %collective-permute-start.16 = (f32[8,3,512]{2,1,0:T(4,128)S(1)}, f32[8,3,512]{2,1,0:T(4,128)S(1)}, u32[]{:S(2)}, u32[]{:S(2)}) collective-permute-start(f32[8,3,512]{2,1,0:T(4,128)S(1)} %join_rows.2.first_ref), channel_id=1, source_target_pairs={{0,2},{1,3},{2,0},{3,1},{4,6},{5,7},{6,4},{7,5},{8,10},{9,11},{10,... | collective-permute-start | bytes 147464 | tf_op jit(solution)/shard_map/ppermute | solution.py:444

commit v2 on v1

--- a/solution.py
+++ b/solution.py
@@ -10,6 +10,8 @@
 
 GSIZE = 512
 WIN = 4
+
+Q_OUTPUT_FLOPS = 46 * 10**8
 VMEM_LIMIT = 16 * 1024 * 1024
 SCALE = 1
 BF16 = jnp.bfloat16
@@ -40,6 +42,16 @@
         )(*args)
 
     return run
+
+
+def valid(stream, lag):
+    place = lax.axis_index("ctx")
+    earlier, later = place >= lag, place + lag < lax.axis_size("ctx")
+    return jnp.where(core_of() == (0 if stream == "P" else 1), earlier, later)
+
+
+def kept(panel, exists):
+    return jnp.where(exists, panel, jnp.zeros_like(panel))
 
 
 def block_group(half, block, width, bw):
@@ -215,12 +227,12 @@
         def run(pair):
             for b in range(nb):
                 at = pl.ds(b * bw, bw)
-                p, x, r = p0[:, at], x10[:, at], r1_ref[:, at]
+                p, x, r = p0[:, at], kept(x10[:, at], valid("Q", 2)), kept(r1_ref[:, at], valid("P", 1))
                 is_one = short_lag(lag_ref, block_group(core, b, 2 * hw, bw), slots) == 1
                 short = pair(jnp.where(is_one, r, p), jnp.where(is_one, q_ref[:, at], x))
                 short += pair(p, jnp.where(is_one, x0_ref[:, at], jnp.zeros_like(p)))
-                last = pair(r, x) + pair(p, r2_ref[:, at])
-                other = pair(p1[:, at], x11[:, at])
+                last = pair(r, x) + pair(p, kept(r2_ref[:, at], valid("Q", 3)))
+                other = pair(p1[:, at], kept(x11[:, at], valid("Q", 2)))
                 rows = [diagonal_sums(matrix, span) for matrix in (short, last, other)]
                 empty = jnp.zeros_like(rows[0])
                 for frame in range(2):
@@ -248,12 +260,35 @@
     )(lags, near, *p_own, q_own[0], r1, x0, *x1, r2)
 
 
-def partial_sums(lags, slots, toeplitz, p_own, r1, x2, key, query):
+def near_sums(toeplitz, p_own, q_own):
     span, hw = p_own[0].shape
     bw = min(GSIZE, hw)
     nb = hw // bw
 
-    def body(lag_ref, t_ref, p0, p1, r10, r11, x20, x21, key_ref, query_ref, gate_ref, out_ref, sem):
+    def body(t_ref, p0, p1, q0, q1, out_ref):
+        for role, panels in enumerate(((p0, p1), (q0, q1))):
+            for frame in range(2):
+                for b in range(nb):
+                    at = pl.ds(b * bw, bw)
+                    out_ref[role, frame, :, at] = jnp.dot(
+                        t_ref[role, frame * nb + b, 0], panels[frame][:, at], preferred_element_type=F32
+                    )
+
+    return call(
+        body,
+        "near_sums",
+        jax.ShapeDtypeStruct((2, 2, span, hw), F32),
+        [VMEM] * 5,
+        VMEM,
+    )(toeplitz, *p_own, *q_own)
+
+
+def partial_sums(lags, slots, toeplitz, sums, r1, x2, key, query):
+    span, hw = r1[0].shape
+    bw = min(GSIZE, hw)
+    nb = hw // bw
+
+    def body(lag_ref, t_ref, sums_ref, r10, r11, x20, x21, key_ref, query_ref, gate_ref, out_ref, sem):
         core = core_of()
 
         def load(ref):
@@ -274,7 +309,8 @@
                 group = block_group(half, b, 2 * hw, bw)
                 is_one = short_lag(lag_ref, group, slots) == 1
                 panel = jnp.where(is_one, (r10, r11)[frame][:, at], (x20, x21)[frame][:, at])
-                total = jnp.dot(t_ref[0, frame * nb + b, 0], (p0, p1)[frame][:, at], preferred_element_type=F32)
+                panel = kept(panel, jnp.where(is_one, valid("P", 1), valid("P", 2)))
+                total = sums_ref[0, frame, :, at]
                 total += jnp.dot(t_ref[0, frame * nb + b, 1], panel, preferred_element_type=F32)
                 out_ref[frame, :, at] = total
         load(key_ref).wait()
@@ -283,10 +319,10 @@
         body,
         "partial_sums",
         [jax.ShapeDtypeStruct((span, 2 * hw), BF16), jax.ShapeDtypeStruct((2, span, hw), F32)],
-        [SMEM] + [VMEM] * 7 + [HBM] * 2,
+        [SMEM] + [VMEM] * 6 + [HBM] * 2,
         [VMEM, VMEM],
         [pltpu.SemaphoreType.DMA],
-    )(lags, toeplitz, *p_own, *r1, *x2, key, query)
+    )(lags, toeplitz, sums, *r1, *x2, key, query)
 
 
 def gated_output(role, panels, total_of, gates, results):
@@ -356,23 +392,26 @@
         [HBM, HBM],
         scratch,
         {first: 0, first + 1: 1} if results else None,
+        flops=Q_OUTPUT_FLOPS if role == "Q" else 1,
     )(*panels, *gates, *results)
 
 
-def q_output(lags, slots, toeplitz, q_own, x0, x1, r2, key, query):
-    def total_of(lag_ref, group, frame, b, place, at, t_ref, q0, q1, x00, x01, x10, x11, r20, r21):
+def q_output(lags, slots, toeplitz, sums, x0, x1, r2, key, query):
+    def total_of(lag_ref, group, frame, b, place, at, t_ref, sums_ref, x00, x01, x10, x11, r20, r21):
         is_one = short_lag(lag_ref, group, slots) == 1
         panel = jnp.where(is_one, (x00, x01)[frame][:, at], (x10, x11)[frame][:, at])
-        total = jnp.dot(t_ref[1, place, 0], (q0, q1)[frame][:, at], preferred_element_type=F32)
+        panel = kept(panel, jnp.logical_or(is_one, valid("Q", 2)))
+        last = kept((r20, r21)[frame][:, at], valid("Q", 3))
+        total = sums_ref[1, frame, :, at]
         total += jnp.dot(t_ref[1, place, 1], panel, preferred_element_type=F32)
-        return total + jnp.dot(t_ref[1, place, 2], (r20, r21)[frame][:, at], preferred_element_type=F32)
-
-    return gated_output("Q", (lags, toeplitz, *q_own, *x0, *x1, *r2), total_of, (key, query), ())
+        return total + jnp.dot(t_ref[1, place, 2], last, preferred_element_type=F32)
+
+    return gated_output("Q", (lags, toeplitz, sums, *x0, *x1, *r2), total_of, (key, query), ())
 
 
 def p_output(lags, toeplitz, sums, r3, gate, results):
     def total_of(lag_ref, group, frame, b, place, at, t_ref, sums_ref, r3_ref):
-        last = jnp.dot(t_ref[0, place, 2], r3_ref[frame, :, at], preferred_element_type=F32)
+        last = jnp.dot(t_ref[0, place, 2], kept(r3_ref[frame, :, at], valid("P", 3)), preferred_element_type=F32)
         return sums_ref[frame, :, at] + last
 
     return gated_output("P", (lags, toeplitz, sums, r3), total_of, (gate,), results)
@@ -402,17 +441,15 @@
     return call(body, "add_rows", shape, [VMEM] * len(parts), VMEM)(*parts)
 
 
-def sum_over_chips(rows, work):
+def sum_over_chips(rows):
     count = lax.axis_size("ctx")
     if count & (count - 1):
         return lax.psum(rows, "ctx")
     bit = 2
     while bit < count:
-        steps = [k * bit for k in range(1, 4) if k * bit < count]
+        steps = [k * bit for k in (3, 2, 1) if k * bit < count]
         others = [lax.ppermute(rows, "ctx", [(i, i ^ step) for i in range(count)]) for step in steps]
-        if bit == 2:
-            others = lax.optimization_barrier((others, work))[0]
-        rows = added([rows] + others)
+        rows = added(others + [rows])
         bit *= 4
     return rows
 
@@ -435,15 +472,16 @@
     return call(body, "join_rows", shape, [VMEM] * 2, VMEM)(first, second)
 
 
-def gather_over_chan(rows, work):
+def gather_over_chan(rows, works):
     count = lax.axis_size("chan")
     if count & (count - 1):
         return lax.all_gather(rows, "chan", axis=0, tiled=True)
     bit = 1
     while bit < count:
         other = lax.ppermute(rows, "chan", [(i, i ^ bit) for i in range(count)])
-        if bit == 1:
-            other = after(other, work)
+        if works:
+            other = after(other, works[0])
+            works = works[1:]
         rows = joined(rows, other, bit)
         bit *= 2
     return rows
@@ -483,16 +521,24 @@
     hw = width // 2
     bw = min(GSIZE, hw)
 
-    def keep(moves):
-        return [(a, b) for a, b in moves if 0 <= b < count]
-
-    swap = [(i, i ^ 1) for i in range(count)]
-    to_near = keep([(i, i + 1 if i % 2 else i - 1) for i in range(count)])
-    to_far = keep([(i, i - 3 if i % 2 else i + 3) for i in range(count)])
-    onward = keep([(i, i - 2 if i % 2 else i + 2) for i in range(count)])
+    def along(moves):
+        chans = lax.axis_size("chan")
+        moves = [(a, b) for a, b in moves if 0 <= b < count]
+        sources, targets = {a for a, _ in moves}, {b for _, b in moves}
+        moves += [(a, a ^ 1) for a in targets - sources if (a ^ 1) in sources - targets]
+        pairs = [(a * chans + c, b * chans + c) for a, b in moves for c in range(chans)]
+        if chans % 2 == 0:
+            idle = set(range(count)) - sources - targets
+            pairs += [(a * chans + c, a * chans + (c ^ 1)) for a in sorted(idle) for c in range(chans)]
+        return sorted(pairs)
+
+    swap = along([(i, i ^ 1) for i in range(count)])
+    to_near = along([(i, i + 1 if i % 2 else i - 1) for i in range(count)])
+    to_far = along([(i, i - 3 if i % 2 else i + 3) for i in range(count)])
+    onward = along([(i, i - 2 if i % 2 else i + 2) for i in range(count)])
 
     def send(value, moves):
-        return lax.ppermute(value, "ctx", moves)
+        return lax.ppermute(value, ("ctx", "chan"), moves)
 
     slots = lag_blocks.shape[1]
     streams = (key_stream, value_stream, query_stream, grad_out)
@@ -508,27 +554,27 @@
     toeplitz = toeplitz_matrices(lags, far_taps, near_taps, span, width, bw)
     near = correlate_near(p_own, q_own)
 
-    r2a = send(after(pa, near, toeplitz), to_far)
-    r1 = lax.optimization_barrier(((r1a, r1b), toeplitz, near))[0]
+    sums = near_sums(toeplitz, p_own, q_own)
+
+    r2a = send(after(pa, near, sums), to_far)
+    r1 = lax.optimization_barrier(((r1a, r1b), sums, near))[0]
     x1 = (send(r1[1], swap), send(r1[0], swap))
     x0a = send(after(pa, r1), swap)
     r2b = send(after(pb, r1), to_far)
     both, r1 = lax.optimization_barrier((stacked(r1), r1))
     rows = correlate_far(lags, slots, near, p_own, q_own, r1[0], x0a, x1, r2a)
-    x0b = send(after(pb, rows), swap)
-
+    r3 = send(after(both, rows), onward)
+    rows = sum_over_cores(sum_over_chips(rows))
+    pb_late, r2_late, rows = lax.optimization_barrier((pb, (r2a, r2b), rows))
+    x0b = send(pb_late, swap)
+    x2 = (send(r2_late[1], swap), send(r2_late[0], swap))
     gates = (key_stream, query_stream)
-    results = q_output(lags, slots, toeplitz, q_own, (x0a, x0b), x1, (r2a, r2b), *gates)
-    rows = sum_over_chips(rows, results[0])
-    both, r2_late, rows = lax.optimization_barrier((both, (r2a, r2b), rows))
-    r3 = send(both, onward)
-    x2 = (send(r2_late[1], swap), send(r2_late[0], swap))
-    rows = sum_over_cores(rows)
-    gate, sums = partial_sums(lags, slots, toeplitz, p_own, r1, x2, *gates)
-    rows = gather_over_chan(rows, sums)
+    results = q_output(lags, slots, toeplitz, sums, (x0a, x0b), x1, (r2a, r2b), *gates)
+    gate, sums = partial_sums(lags, slots, toeplitz, sums, r1, x2, *gates)
+    rows = gather_over_chan(rows, [results[0], sums])
+    results = p_output(lags, toeplitz, sums, r3, gate, results)
     scale = 1.0 / math.sqrt(span * count * GSIZE)
     far, near = filter_gradients(rows, groups, span, scale)
-    results = p_output(lags, toeplitz, sums, r3, gate, results)
     return (results[0], results[1], far, near)
 
 

time: 54 us -> 49.2 us (0.911)
  starting transfers between devices: 25.8 us -> 14.8 us
  waiting for transfers between devices: 10.2 us -> 16.3 us
    ppermute x11, starting transfers between devices: 17.7 us -> 7.25 us  [send(): return lax.ppermute(value, ('ctx', 'chan'), moves)]
    ppermute x11, waiting for transfers between devices: 2.6 us -> 8.3 us  [send(): return lax.ppermute(value, ('ctx', 'chan'), moves)]
    ppermute x3, waiting for transfers between devices: 1.74 us -> 5.17 us  [sum_over_chips(): lax.ppermute(rows, 'ctx', [(i, i ^ step) for i in range(count)])]
    ppermute x2, waiting for transfers between devices: 3.75 us -> 1.6 us  [gather_over_chan(): other = lax.ppermute(rows, 'chan', [(i, i ^ bit) for i in range(count)])]
    ppermute x1, waiting for transfers between devices: 2.12 us -> 1.19 us  [sum_over_cores(): lax.ppermute(rows, 'ctx', [(i, i ^ 1) for i in range(count)])]
    pallas_call x14 -> x15, Pallas kernels: 16.6 us -> 16.9 us  [run(): pl.pallas_call(body, in_specs=in_specs, out_specs=out_specs, out_shape=ou...]
  transfers between devices with their start and end apart: 17 -> 17, of which waited for: 7 -> 7; matrix products, arithmetic and copies ran while one was open for 0% -> 0% of each run, Pallas kernels for 24% -> 27%
where the time goes in v2:
time: 49.2 us; the launch traced here: 49 us
  Pallas kernels  16.9 us (34%)
  waiting for transfers between devices  16.3 us (33%)
  starting transfers between devices  14.8 us (30%)
  between operations  0.8 us (2%)
    pallas_call x15, Pallas kernels, run(): pl.pallas_call(body, in_specs=in_specs, out_specs=out_specs, out_shape=ou...  16.9 us
    ppermute x11, waiting for transfers between devices, send(): return lax.ppermute(value, ('ctx', 'chan'), moves)  8.3 us
    ppermute x11, starting transfers between devices, send(): return lax.ppermute(value, ('ctx', 'chan'), moves)  7.25 us
    ppermute x3, waiting for transfers between devices, sum_over_chips(): lax.ppermute(rows, 'ctx', [(i, i ^ step) for i in range(count)])  5.17 us
    ppermute x3, starting transfers between devices, sum_over_chips(): lax.ppermute(rows, 'ctx', [(i, i ^ step) for i in range(count)])  4.45 us
    ppermute x2, starting transfers between devices, gather_over_chan(): other = lax.ppermute(rows, 'chan', [(i, i ^ bit) for i in range(count)])  3.06 us
    ppermute x2, waiting for transfers between devices, gather_over_chan(): other = lax.ppermute(rows, 'chan', [(i, i ^ bit) for i in range(count)])  1.6 us
    ppermute x1, waiting for transfers between devices, sum_over_cores(): lax.ppermute(rows, 'ctx', [(i, i ^ 1) for i in range(count)])  1.19 us
  transfers between devices with their start and end apart: 17, of which 7 were waited for; matrix products, arithmetic and copies ran while one was open for 0% of the time, Pallas kernels for 27%

profile of v2, /device:TPU:0, one launch (start us, length us, event | category | flops | bytes accessed | tf_op | source)
XLA Modules:
  0.0 49.0 jit_solution(2078187651740657182)
XLA Ops:
  0.7 1.7 %q_stream.1 = (bf16[256,1024]{1,0:T(8,128)(2,1)S(1)}, bf16[256,1024]{1,0:T(8,128)(2,1)S(1)}) custom-call(bf16[256,2048]{1,0:T(8,128)(2,1)} %refs_9_.1, bf16[256,2048]{1,0:T(8,128)(2,1)} %v_ref.2, bf16[256,2048]{1,0:T(8,128)(2,1)} %refs_10_.1, bf16[256,2048]{1,0:T(8,128)(2,1)} %g_ref.2), custom_call_target="tpu_custom_call" | custom-call | flops 1 | bytes 5242880 | tf_op jit(solution)/shard_map/q_stream/pallas_call | solution.py:32
  2.4 3.0 %collective-permute-start = (bf16[256,1024]{1,0:T(8,128)(2,1)S(1)}, bf16[256,1024]{1,0:T(8,128)(2,1)S(1)}, u32[]{:S(2)}, u32[]{:S(2)}) collective-permute-start(bf16[256,1024]{1,0:T(8,128)(2,1)S(1)} %get-tuple-element.48.q1), channel_id=1, source_target_pairs={{0,1},{1,0},{2,3},{3,2},{4,8},{5,9},{6,10},{7,11},{8,4},{9,5},{10,... | collective-permute-start | bytes 1572872 | tf_op jit(solution)/shard_map/ppermute | solution.py:541
  5.4 0.1 copy.14
  5.5 0.1 reshape.11.lag_ref.refs_0_
  5.6 3.7 %toeplitz.1.t_ref.refs_1_ = bf16[2,4,3,256,256]{4,3,2,1,0:T(8,128)(2,1)S(1)} custom-call(s32[32]{0:T(128)S(1)} %reshape.11.lag_ref.refs_0_, bf16[16,2,512]{2,1,0:T(2,128)(2,1)S(1)} %copy-done.2, bf16[16,256]{1,0:T(8,128)(2,1)S(1)} %copy-done.3), custom_call_target="tpu_custom_call" | custom-call | flops 1 | bytes 3186816 | tf_op jit(solution)/shard_map/toeplitz/pallas_call | solution.py:32
  9.3 1.7 %p_stream.1 = (bf16[256,1024]{1,0:T(8,128)(2,1)S(1)}, bf16[256,1024]{1,0:T(8,128)(2,1)S(1)}) custom-call(bf16[256,2048]{1,0:T(8,128)(2,1)} %refs_9_.1, bf16[256,2048]{1,0:T(8,128)(2,1)} %v_ref.2, bf16[256,2048]{1,0:T(8,128)(2,1)} %refs_10_.1, bf16[256,2048]{1,0:T(8,128)(2,1)} %g_ref.2), custom_call_target="tpu_custom_call" | custom-call | flops 1 | bytes 5242880 | tf_op jit(solution)/shard_map/p_stream/pallas_call | solution.py:32
  11.0 1.0 %correlate_near.1.near_ref = f32[2,2,512]{2,1,0:T(2,128)S(1)} custom-call(bf16[256,1024]{1,0:T(8,128)(2,1)S(1)} %get-tuple-element.62.p0, bf16[256,1024]{1,0:T(8,128)(2,1)S(1)} %get-tuple-element.55.p1, bf16[256,1024]{1,0:T(8,128)(2,1)S(1)} %get-tuple-element.38.q0.q_ref, bf16[256,1024]{1,0:T(8,128)(2,1)S(1)} %get-tuple-element.48.q1), custom_call_target="tpu_custom_call" | custom-call | flops 1 | bytes 2105344 | tf_op jit(solution)/shard_map/correlate_near/pallas_call | solution.py:32
  12.0 0.7 %near_sums.1.sums_ref.refs_2_ = f32[2,2,256,1024]{3,2,1,0:T(8,128)S(1)} custom-call(bf16[2,4,3,256,256]{4,3,2,1,0:T(8,128)(2,1)S(1)} %toeplitz.1.t_ref.refs_1_, bf16[256,1024]{1,0:T(8,128)(2,1)S(1)} %get-tuple-element.62.p0, bf16[256,1024]{1,0:T(8,128)(2,1)S(1)} %get-tuple-element.55.p1, bf16[256,1024]{1,0:T(8,128)(2,1)S(1)} %get-tuple-element.38.q0.q_ref, ...), custom_call_target="tpu_custom_call" | custom-call | flops 1 | bytes 9437184 | tf_op jit(solution)/shard_map/near_sums/pallas_call | solution.py:32
  12.8 1.4 %collective-permute-start.2 = (bf16[256,1024]{1,0:T(8,128)(2,1)S(1)}, bf16[256,1024]{1,0:T(8,128)(2,1)S(1)}, u32[]{:S(2)}, u32[]{:S(2)}) collective-permute-start(bf16[256,1024]{1,0:T(8,128)(2,1)S(1)} %get-tuple-element.55.p1), channel_id=1, source_target_pairs={{0,12},{1,13},{2,14},{3,15},{4,5},{5,4},{6,7},{7,6},{8,20},{9,21},... | collective-permute-start | bytes 1572872 | tf_op jit(solution)/shard_map/ppermute | solution.py:541
  14.2 6.5 %collective-permute-done.1.refs_1_.r11 = bf16[256,1024]{1,0:T(8,128)(2,1)S(1)} collective-permute-done((bf16[256,1024]{1,0:T(8,128)(2,1)S(1)}, bf16[256,1024]{1,0:T(8,128)(2,1)S(1)}, u32[]{:S(2)}, u32[]{:S(2)}) %collective-permute-start.1) | collective-permute-done | bytes 524320 | tf_op jit(solution)/shard_map/ppermute | solution.py:541
  20.7 0.5 %collective-permute-start.6 = (bf16[256,1024]{1,0:T(8,128)(2,1)S(1)}, bf16[256,1024]{1,0:T(8,128)(2,1)S(1)}, u32[]{:S(2)}, u32[]{:S(2)}) collective-permute-start(bf16[256,1024]{1,0:T(8,128)(2,1)S(1)} %collective-permute-done.refs_0_.r1_ref.r10), channel_id=1, source_target_pairs={{0,4},{1,5},{2,6},{3,7},{4,0},{5,1},{6,2},{7,3},{8,12},{9,13},{10,... | collective-permute-start | bytes 1572872 | tf_op jit(solution)/shard_map/ppermute | solution.py:541
  21.2 1.0 %collective-permute-start.3 = (bf16[256,1024]{1,0:T(8,128)(2,1)S(1)}, bf16[256,1024]{1,0:T(8,128)(2,1)S(1)}, u32[]{:S(2)}, u32[]{:S(2)}) collective-permute-start(bf16[256,1024]{1,0:T(8,128)(2,1)S(1)} %get-tuple-element.62.p0), channel_id=1, source_target_pairs={{0,12},{1,13},{2,14},{3,15},{4,5},{5,4},{6,7},{7,6},{8,20},{9,21},... | collective-permute-start | bytes 1572872 | tf_op jit(solution)/shard_map/ppermute | solution.py:541
  22.3 1.6 %collective-permute-done.2.r2_ref.refs_7_ = bf16[256,1024]{1,0:T(8,128)(2,1)S(1)} collective-permute-done((bf16[256,1024]{1,0:T(8,128)(2,1)S(1)}, bf16[256,1024]{1,0:T(8,128)(2,1)S(1)}, u32[]{:S(2)}, u32[]{:S(2)}) %collective-permute-start.2) | collective-permute-done | bytes 524320 | tf_op jit(solution)/shard_map/ppermute | solution.py:541
  23.8 0.2 collective-permute-done.5.x10.refs_5_
  24.1 2.0 %correlate_far.1.refs_3_ = f32[4,3,512]{2,1,0:T(4,128)S(1)} custom-call(s32[32]{0:T(128)S(1)} %reshape.11.lag_ref.refs_0_, f32[2,2,512]{2,1,0:T(2,128)S(1)} %correlate_near.1.near_ref, bf16[256,1024]{1,0:T(8,128)(2,1)S(1)} %get-tuple-element.62.p0, bf16[256,1024]{1,0:T(8,128)(2,1)S(1)} %get-tuple-element.55.p1, ...), custom_call_target="tpu_custom_call" | custom-call | flops 1 | bytes 4227200 | tf_op jit(solution)/shard_map/correlate_far/pallas_call | solution.py:32
  26.1 1.4 %collective-permute-start.9 = (f32[4,3,512]{2,1,0:T(4,128)S(1)}, f32[4,3,512]{2,1,0:T(4,128)S(1)}, u32[]{:S(2)}, u32[]{:S(2)}) collective-permute-start(f32[4,3,512]{2,1,0:T(4,128)S(1)} %correlate_far.1.refs_3_), channel_id=1, source_target_pairs={{0,8},{4,12},{8,0},{12,4},{16,24},{20,28},{24,16},{28,20},{1,9},{5... | collective-permute-start | bytes 73736 | tf_op jit(solution)/shard_map/ppermute | solution.py:451
  27.5 2.5 %collective-permute-start.8 = (f32[4,3,512]{2,1,0:T(4,128)S(1)}, f32[4,3,512]{2,1,0:T(4,128)S(1)}, u32[]{:S(2)}, u32[]{:S(2)}) collective-permute-start(f32[4,3,512]{2,1,0:T(4,128)S(1)} %correlate_far.1.refs_3_), channel_id=1, source_target_pairs={{0,16},{4,20},{8,24},{12,28},{16,0},{20,4},{24,8},{28,12},{1,17},{... | collective-permute-start | bytes 73736 | tf_op jit(solution)/shard_map/ppermute | solution.py:451
  30.0 0.5 collective-permute-start.7
  30.5 0.5 collective-permute-start.13
  31.0 2.2 %collective-permute-done.8.refs_1_ = f32[4,3,512]{2,1,0:T(4,128)S(1)} collective-permute-done((f32[4,3,512]{2,1,0:T(4,128)S(1)}, f32[4,3,512]{2,1,0:T(4,128)S(1)}, u32[]{:S(2)}, u32[]{:S(2)}) %collective-permute-start.8) | collective-permute-done | bytes 24608 | tf_op jit(solution)/shard_map/ppermute | solution.py:451
  33.2 2.9 %collective-permute-done.7.refs_0_ = f32[4,3,512]{2,1,0:T(4,128)S(1)} collective-permute-done((f32[4,3,512]{2,1,0:T(4,128)S(1)}, f32[4,3,512]{2,1,0:T(4,128)S(1)}, u32[]{:S(2)}, u32[]{:S(2)}) %collective-permute-start.7) | collective-permute-done | bytes 24608 | tf_op jit(solution)/shard_map/ppermute | solution.py:451
  36.3 1.2 %collective-permute-done.10.refs_1_ = f32[4,3,512]{2,1,0:T(4,128)S(1)} collective-permute-done((f32[4,3,512]{2,1,0:T(4,128)S(1)}, f32[4,3,512]{2,1,0:T(4,128)S(1)}, u32[]{:S(2)}, u32[]{:S(2)}) %collective-permute-start.10) | collective-permute-done | bytes 24608 | tf_op jit(solution)/shard_map/ppermute | solution.py:461
  37.5 0.2 collective-permute-start.14
  37.7 0.3 collective-permute-start.11
  38.0 0.2 collective-permute-start.12
  38.2 1.5 %collective-permute-start.15 = (f32[4,3,512]{2,1,0:T(4,128)S(1)}, f32[4,3,512]{2,1,0:T(4,128)S(1)}, u32[]{:S(2)}, u32[]{:S(2)}) collective-permute-start(f32[4,3,512]{2,1,0:T(4,128)S(1)} %add_rows.3.first_ref), channel_id=1, source_target_pairs={{0,1},{1,0},{2,3},{3,2},{4,5},{5,4},{6,7},{7,6},{8,9},{9,8},{10,11... | collective-permute-start | bytes 73736 | tf_op jit(solution)/shard_map/ppermute | solution.py:481
  39.7 2.4 %out_q.1 = (bf16[256,2048]{1,0:T(8,128)(2,1)}, bf16[256,2048]{1,0:T(8,128)(2,1)}) custom-call(s32[32]{0:T(128)S(1)} %reshape.11.lag_ref.refs_0_, bf16[2,4,3,256,256]{4,3,2,1,0:T(8,128)(2,1)S(1)} %toeplitz.1.t_ref.refs_1_, f32[2,2,256,1024]{3,2,1,0:T(8,128)S(1)} %near_sums.1.sums_ref.refs_2_, bf16[256,1024]{1,0:T(8,128)(2,1)S(1)} %collective-permute-done.4.x0_ref.refs_3_, ...), custom_call_target="tpu_custom_call" | custom-call | flops 4600000000 | bytes 14680192 | tf_op jit(solution)/shard_map/out_q/pallas_call | solution.py:32
  42.2 1.6 %collective-permute-start.16 = (f32[8,3,512]{2,1,0:T(4,128)S(1)}, f32[8,3,512]{2,1,0:T(4,128)S(1)}, u32[]{:S(2)}, u32[]{:S(2)}) collective-permute-start(f32[8,3,512]{2,1,0:T(4,128)S(1)} %join_rows.2.first_ref), channel_id=1, source_target_pairs={{0,2},{1,3},{2,0},{3,1},{4,6},{5,7},{6,4},{7,5},{8,10},{9,11},{10,... | collective-permute-start | bytes 147464 | tf_op jit(solution)/shard_map/ppermute | solution.py:481
  43.8 1.1 %partial_sums.1 = (bf16[256,2048]{1,0:T(8,128)(2,1)S(1)}, f32[2,256,1024]{2,1,0:T(8,128)S(1)}) custom-call(s32[32]{0:T(128)S(1)} %reshape.11.lag_ref.refs_0_, bf16[2,4,3,256,256]{4,3,2,1,0:T(8,128)(2,1)S(1)} %toeplitz.1.t_ref.refs_1_, f32[2,2,256,1024]{3,2,1,0:T(8,128)S(1)} %near_sums.1.sums_ref.refs_2_, ...), custom_call_target="tpu_custom_call" | custom-call | flops 1 | bytes 14680192 | tf_op jit(solution)/shard_map/partial_sums/pallas_call | solution.py:32
  44.9 1.6 %collective-permute-done.16.second_ref = f32[8,3,512]{2,1,0:T(4,128)S(1)} collective-permute-done((f32[8,3,512]{2,1,0:T(4,128)S(1)}, f32[8,3,512]{2,1,0:T(4,128)S(1)}, u32[]{:S(2)}, u32[]{:S(2)}) %collective-permute-start.16) | collective-permute-done | bytes 49184 | tf_op jit(solution)/shard_map/ppermute | solution.py:481
  46.5 0.7 %filter_gradients.1 = (f32[16,2,512]{2,1,0:T(2,128)}, f32[16,256]{1,0:T(8,128)}) custom-call(f32[16,3,512]{2,1,0:T(4,128)S(1)} %join_rows.3.rows_ref), custom_call_target="tpu_custom_call" | custom-call | flops 1 | bytes 180224 | tf_op jit(solution)/shard_map/filter_gradients/pallas_call | solution.py:32
  47.2 1.8 %out_p.1 = (bf16[256,2048]{1,0:T(8,128)(2,1)}, bf16[256,2048]{1,0:T(8,128)(2,1)}) custom-call(s32[32]{0:T(128)S(1)} %reshape.11.lag_ref.refs_0_, bf16[2,4,3,256,256]{4,3,2,1,0:T(8,128)(2,1)S(1)} %toeplitz.1.t_ref.refs_1_, f32[2,256,1024]{2,1,0:T(8,128)S(1)} %get-tuple-element.58.refs_2_, ...), custom_call_target="tpu_custom_call", output_to_operand_aliasing={{0}: (5, {}), {1}: (6, {})} | custom-call | flops 1 | bytes 11534464 | tf_op jit(solution)/shard_map/out_p/pallas_call | solution.py:32
  (29 shorter events, 0.4 us)
Async XLA Ops:
  0.6 4.8 %copy-start.4 = (s32[16,2]{0,1:T(2,128)S(1)}, s32[16,2]{0,1:T(2,128)}, u32[]{:S(2)}) copy-start(s32[16,2]{0,1:T(2,128)} %param.13) | copy-start | bytes 388
  0.6 5.0 %copy-start.3 = (bf16[16,256]{1,0:T(8,128)(2,1)S(1)}, bf16[16,256]{1,0:T(8,128)(2,1)}, u32[]{:S(2)}) copy-start(bf16[16,256]{1,0:T(8,128)(2,1)} %near_ref) | copy-start | bytes 24580
  0.7 5.0 %copy-start.2 = (bf16[16,2,512]{2,1,0:T(2,128)(2,1)S(1)}, bf16[16,2,512]{2,1,0:T(2,128)(2,1)}, u32[]{:S(2)}) copy-start(bf16[16,2,512]{2,1,0:T(2,128)(2,1)} %far_ref) | copy-start | bytes 98308
  2.4 11.8 %collective-permute-start = (bf16[256,1024]{1,0:T(8,128)(2,1)S(1)}, bf16[256,1024]{1,0:T(8,128)(2,1)S(1)}, u32[]{:S(2)}, u32[]{:S(2)}) collective-permute-start(bf16[256,1024]{1,0:T(8,128)(2,1)S(1)} %get-tuple-element.48.q1), channel_id=1, source_target_pairs={{0,1},{1,0},{2,3},{3,2},{4,8},{5,9},{6,10},{7,11},{8,4},{9,5},{10,... | collective-permute-start | bytes 1572872 | tf_op jit(solution)/shard_map/ppermute | solution.py:541
  5.4 15.3 %collective-permute-start.1 = (bf16[256,1024]{1,0:T(8,128)(2,1)S(1)}, bf16[256,1024]{1,0:T(8,128)(2,1)S(1)}, u32[]{:S(2)}, u32[]{:S(2)}) collective-permute-start(bf16[256,1024]{1,0:T(8,128)(2,1)S(1)} %get-tuple-element.38.q0.q_ref), channel_id=1, source_target_pairs={{0,1},{1,0},{2,3},{3,2},{4,8},{5,9},{6,10},{7,11},{8,4},{9,5},{10,... | collective-permute-start | bytes 1572872 | tf_op jit(solution)/shard_map/ppermute | solution.py:541
  12.7 27.0 %copy-start = (bf16[256,2048]{1,0:T(8,128)(2,1)S(1)}, bf16[256,2048]{1,0:T(8,128)(2,1)}, u32[]{:S(2)}) copy-start(bf16[256,2048]{1,0:T(8,128)(2,1)} %refs_9_.1) | copy-start | bytes 3145732
  12.7 27.0 %copy-start.1 = (bf16[256,2048]{1,0:T(8,128)(2,1)S(1)}, bf16[256,2048]{1,0:T(8,128)(2,1)}, u32[]{:S(2)}) copy-start(bf16[256,2048]{1,0:T(8,128)(2,1)} %refs_10_.1) | copy-start | bytes 3145732
  12.8 11.1 %collective-permute-start.2 = (bf16[256,1024]{1,0:T(8,128)(2,1)S(1)}, bf16[256,1024]{1,0:T(8,128)(2,1)S(1)}, u32[]{:S(2)}, u32[]{:S(2)}) collective-permute-start(bf16[256,1024]{1,0:T(8,128)(2,1)S(1)} %get-tuple-element.55.p1), channel_id=1, source_target_pairs={{0,12},{1,13},{2,14},{3,15},{4,5},{5,4},{6,7},{7,6},{8,20},{9,21},... | collective-permute-start | bytes 1572872 | tf_op jit(solution)/shard_map/ppermute | solution.py:541
  20.7 3.2 %collective-permute-start.4 = (bf16[256,1024]{1,0:T(8,128)(2,1)S(1)}, bf16[256,1024]{1,0:T(8,128)(2,1)S(1)}, u32[]{:S(2)}, u32[]{:S(2)}) collective-permute-start(bf16[256,1024]{1,0:T(8,128)(2,1)S(1)} %get-tuple-element.55.p1), channel_id=1, source_target_pairs={{0,4},{1,5},{2,6},{3,7},{4,0},{5,1},{6,2},{7,3},{8,12},{9,13},{10,... | collective-permute-start | bytes 1572872 | tf_op jit(solution)/shard_map/ppermute | solution.py:541
  20.7 3.2 %collective-permute-start.6 = (bf16[256,1024]{1,0:T(8,128)(2,1)S(1)}, bf16[256,1024]{1,0:T(8,128)(2,1)S(1)}, u32[]{:S(2)}, u32[]{:S(2)}) collective-permute-start(bf16[256,1024]{1,0:T(8,128)(2,1)S(1)} %collective-permute-done.refs_0_.r1_ref.r10), channel_id=1, source_target_pairs={{0,4},{1,5},{2,6},{3,7},{4,0},{5,1},{6,2},{7,3},{8,12},{9,13},{10,... | collective-permute-start | bytes 1572872 | tf_op jit(solution)/shard_map/ppermute | solution.py:541
  21.2 2.9 %collective-permute-start.5 = (bf16[256,1024]{1,0:T(8,128)(2,1)S(1)}, bf16[256,1024]{1,0:T(8,128)(2,1)S(1)}, u32[]{:S(2)}, u32[]{:S(2)}) collective-permute-start(bf16[256,1024]{1,0:T(8,128)(2,1)S(1)} %collective-permute-done.1.refs_1_.r11), channel_id=1, source_target_pairs={{0,4},{1,5},{2,6},{3,7},{4,0},{5,1},{6,2},{7,3},{8,12},{9,13},{10,... | collective-permute-start | bytes 1572872 | tf_op jit(solution)/shard_map/ppermute | solution.py:541
  21.2 16.3 %collective-permute-start.3 = (bf16[256,1024]{1,0:T(8,128)(2,1)S(1)}, bf16[256,1024]{1,0:T(8,128)(2,1)S(1)}, u32[]{:S(2)}, u32[]{:S(2)}) collective-permute-start(bf16[256,1024]{1,0:T(8,128)(2,1)S(1)} %get-tuple-element.62.p0), channel_id=1, source_target_pairs={{0,12},{1,13},{2,14},{3,15},{4,5},{5,4},{6,7},{7,6},{8,20},{9,21},... | collective-permute-start | bytes 1572872 | tf_op jit(solution)/shard_map/ppermute | solution.py:541
  26.1 4.9 %collective-permute-start.9 = (f32[4,3,512]{2,1,0:T(4,128)S(1)}, f32[4,3,512]{2,1,0:T(4,128)S(1)}, u32[]{:S(2)}, u32[]{:S(2)}) collective-permute-start(f32[4,3,512]{2,1,0:T(4,128)S(1)} %correlate_far.1.refs_3_), channel_id=1, source_target_pairs={{0,8},{4,12},{8,0},{12,4},{16,24},{20,28},{24,16},{28,20},{1,9},{5... | collective-permute-start | bytes 73736 | tf_op jit(solution)/shard_map/ppermute | solution.py:451
  27.5 5.7 %collective-permute-start.8 = (f32[4,3,512]{2,1,0:T(4,128)S(1)}, f32[4,3,512]{2,1,0:T(4,128)S(1)}, u32[]{:S(2)}, u32[]{:S(2)}) collective-permute-start(f32[4,3,512]{2,1,0:T(4,128)S(1)} %correlate_far.1.refs_3_), channel_id=1, source_target_pairs={{0,16},{4,20},{8,24},{12,28},{16,0},{20,4},{24,8},{28,12},{1,17},{... | collective-permute-start | bytes 73736 | tf_op jit(solution)/shard_map/ppermute | solution.py:451
  30.0 6.1 %collective-permute-start.7 = (f32[4,3,512]{2,1,0:T(4,128)S(1)}, f32[4,3,512]{2,1,0:T(4,128)S(1)}, u32[]{:S(2)}, u32[]{:S(2)}) collective-permute-start(f32[4,3,512]{2,1,0:T(4,128)S(1)} %correlate_far.1.refs_3_), channel_id=1, source_target_pairs={{0,24},{4,28},{8,16},{12,20},{16,8},{20,12},{24,0},{28,4},{1,25},{... | collective-permute-start | bytes 73736 | tf_op jit(solution)/shard_map/ppermute | solution.py:451
  30.5 16.7 %collective-permute-start.13 = (bf16[2,256,1024]{2,1,0:T(8,128)(2,1)S(1)}, bf16[2,256,1024]{2,1,0:T(8,128)(2,1)S(1)}, u32[]{:S(2)}, u32[]{:S(2)}) collective-permute-start(bf16[2,256,1024]{2,1,0:T(8,128)(2,1)S(1)} %stack.1), channel_id=1, source_target_pairs={{0,8},{1,9},{2,10},{3,11},{4,0},{5,1},{6,2},{7,3},{8,16},{9,17},{1... | collective-permute-start | bytes 3145736 | tf_op jit(solution)/shard_map/ppermute | solution.py:541
  36.2 1.3 %collective-permute-start.10 = (f32[4,3,512]{2,1,0:T(4,128)S(1)}, f32[4,3,512]{2,1,0:T(4,128)S(1)}, u32[]{:S(2)}, u32[]{:S(2)}) collective-permute-start(f32[4,3,512]{2,1,0:T(4,128)S(1)} %add_rows.2.refs_0_), channel_id=1, source_target_pairs={{0,4},{4,0},{8,12},{12,8},{16,20},{20,16},{24,28},{28,24},{1,5},{5... | collective-permute-start | bytes 73736 | tf_op jit(solution)/shard_map/ppermute | solution.py:461
  37.5 2.2 %collective-permute-start.14 = (bf16[256,1024]{1,0:T(8,128)(2,1)S(1)}, bf16[256,1024]{1,0:T(8,128)(2,1)S(1)}, u32[]{:S(2)}, u32[]{:S(2)}) collective-permute-start(bf16[256,1024]{1,0:T(8,128)(2,1)S(1)} %get-tuple-element.62.p0), channel_id=1, source_target_pairs={{0,4},{1,5},{2,6},{3,7},{4,0},{5,1},{6,2},{7,3},{8,12},{9,13},{10,... | collective-permute-start | bytes 1572872 | tf_op jit(solution)/shard_map/ppermute | solution.py:541
  37.7 6.1 %collective-permute-start.11 = (bf16[256,1024]{1,0:T(8,128)(2,1)S(1)}, bf16[256,1024]{1,0:T(8,128)(2,1)S(1)}, u32[]{:S(2)}, u32[]{:S(2)}) collective-permute-start(bf16[256,1024]{1,0:T(8,128)(2,1)S(1)} %collective-permute-done.3.refs_8_), channel_id=1, source_target_pairs={{0,4},{1,5},{2,6},{3,7},{4,0},{5,1},{6,2},{7,3},{8,12},{9,13},{10,... | collective-permute-start | bytes 1572872 | tf_op jit(solution)/shard_map/ppermute | solution.py:541
  38.0 5.7 %collective-permute-start.12 = (bf16[256,1024]{1,0:T(8,128)(2,1)S(1)}, bf16[256,1024]{1,0:T(8,128)(2,1)S(1)}, u32[]{:S(2)}, u32[]{:S(2)}) collective-permute-start(bf16[256,1024]{1,0:T(8,128)(2,1)S(1)} %collective-permute-done.2.r2_ref.refs_7_), channel_id=1, source_target_pairs={{0,4},{1,5},{2,6},{3,7},{4,0},{5,1},{6,2},{7,3},{8,12},{9,13},{10,... | collective-permute-start | bytes 1572872 | tf_op jit(solution)/shard_map/ppermute | solution.py:541
  38.2 3.9 %collective-permute-start.15 = (f32[4,3,512]{2,1,0:T(4,128)S(1)}, f32[4,3,512]{2,1,0:T(4,128)S(1)}, u32[]{:S(2)}, u32[]{:S(2)}) collective-permute-start(f32[4,3,512]{2,1,0:T(4,128)S(1)} %add_rows.3.first_ref), channel_id=1, source_target_pairs={{0,1},{1,0},{2,3},{3,2},{4,5},{5,4},{6,7},{7,6},{8,9},{9,8},{10,11... | collective-permute-start | bytes 73736 | tf_op jit(solution)/shard_map/ppermute | solution.py:481
  42.2 4.3 %collective-permute-start.16 = (f32[8,3,512]{2,1,0:T(4,128)S(1)}, f32[8,3,512]{2,1,0:T(4,128)S(1)}, u32[]{:S(2)}, u32[]{:S(2)}) collective-permute-start(f32[8,3,512]{2,1,0:T(4,128)S(1)} %join_rows.2.first_ref), channel_id=1, source_target_pairs={{0,2},{1,3},{2,0},{3,1},{4,6},{5,7},{6,4},{7,5},{8,10},{9,11},{10,... | collective-permute-start | bytes 147464 | tf_op jit(solution)/shard_map/ppermute | solution.py:481

commit v3 on v2

--- a/solution.py
+++ b/solution.py
@@ -10,10 +10,8 @@
 
 GSIZE = 512
 WIN = 4
-
-Q_OUTPUT_FLOPS = 46 * 10**8
+PARTIAL_SUMS_FLOPS = 52 * 10**8
 VMEM_LIMIT = 16 * 1024 * 1024
-SCALE = 1
 BF16 = jnp.bfloat16
 F32 = jnp.float32
 
@@ -37,7 +35,7 @@
             scratch_shapes=scratch,
             input_output_aliases=aliases or {},
             compiler_params=pltpu.CompilerParams(vmem_limit_bytes=limit),
-            cost_estimate=pl.CostEstimate(flops=flops, bytes_accessed=max(1, moved // SCALE), transcendentals=0),
+            cost_estimate=pl.CostEstimate(flops=flops, bytes_accessed=moved, transcendentals=0),
             name=name,
         )(*args)
 
@@ -260,12 +258,27 @@
     )(lags, near, *p_own, q_own[0], r1, x0, *x1, r2)
 
 
-def near_sums(toeplitz, p_own, q_own):
+def near_sums(toeplitz, p_own, q_own, key, query):
     span, hw = p_own[0].shape
     bw = min(GSIZE, hw)
     nb = hw // bw
 
-    def body(t_ref, p0, p1, q0, q1, out_ref):
+    def body(t_ref, p0, p1, q0, q1, key_ref, query_ref, out_ref, p_gate, q_gate, sems):
+        core = core_of()
+
+        def loads(first, second):
+            return (
+                pltpu.make_async_copy(first, p_gate, sems.at[0]),
+                pltpu.make_async_copy(second, q_gate, sems.at[1]),
+            )
+
+        for number, refs in ((0, (query_ref, key_ref)), (1, (key_ref, query_ref))):
+
+            @pl.when(core == number)
+            def _():
+                for load in loads(*refs):
+                    load.start()
+
         for role, panels in enumerate(((p0, p1), (q0, q1))):
             for frame in range(2):
                 for b in range(nb):
@@ -273,35 +286,27 @@
                     out_ref[role, frame, :, at] = jnp.dot(
                         t_ref[role, frame * nb + b, 0], panels[frame][:, at], preferred_element_type=F32
                     )
-
+        for load in loads(key_ref, query_ref):
+            load.wait()
+
+    gate = jax.ShapeDtypeStruct((span, 2 * hw), BF16)
     return call(
         body,
         "near_sums",
-        jax.ShapeDtypeStruct((2, 2, span, hw), F32),
-        [VMEM] * 5,
-        VMEM,
-    )(toeplitz, *p_own, *q_own)
-
-
-def partial_sums(lags, slots, toeplitz, sums, r1, x2, key, query):
+        [jax.ShapeDtypeStruct((2, 2, span, hw), F32), gate, gate],
+        [VMEM] * 5 + [HBM] * 2,
+        [VMEM] * 3,
+        [pltpu.SemaphoreType.DMA((2,))],
+    )(toeplitz, *p_own, *q_own, key, query)
+
+
+def partial_sums(lags, slots, toeplitz, sums, r1, x2):
     span, hw = r1[0].shape
     bw = min(GSIZE, hw)
     nb = hw // bw
 
-    def body(lag_ref, t_ref, sums_ref, r10, r11, x20, x21, key_ref, query_ref, gate_ref, out_ref, sem):
+    def body(lag_ref, t_ref, sums_ref, r10, r11, x20, x21, out_ref):
         core = core_of()
-
-        def load(ref):
-            return pltpu.make_async_copy(ref, gate_ref, sem)
-
-        @pl.when(core == 0)
-        def _():
-            load(query_ref).start()
-
-        @pl.when(core != 0)
-        def _():
-            load(key_ref).start()
-
         for frame in range(2):
             half = core if frame == 0 else 1 - core
             for b in range(nb):
@@ -313,108 +318,86 @@
                 total = sums_ref[0, frame, :, at]
                 total += jnp.dot(t_ref[0, frame * nb + b, 1], panel, preferred_element_type=F32)
                 out_ref[frame, :, at] = total
-        load(key_ref).wait()
 
     return call(
         body,
         "partial_sums",
-        [jax.ShapeDtypeStruct((span, 2 * hw), BF16), jax.ShapeDtypeStruct((2, span, hw), F32)],
-        [SMEM] + [VMEM] * 6 + [HBM] * 2,
-        [VMEM, VMEM],
-        [pltpu.SemaphoreType.DMA],
-    )(lags, toeplitz, sums, *r1, *x2, key, query)
-
-
-def gated_output(role, panels, total_of, gates, results):
-    span, width = gates[0].shape
+        jax.ShapeDtypeStruct((2, span, hw), F32),
+        [SMEM] + [VMEM] * 6,
+        VMEM,
+        flops=PARTIAL_SUMS_FLOPS,
+    )(lags, toeplitz, sums, *r1, *x2)
+
+
+def gated_output(role, frames, panels, total_of, gate, results):
+    span, width = gate.shape
     hw = width // 2
     bw = min(GSIZE, hw)
     nb = hw // bw
     role_at = 0 if role == "P" else 1
     count = len(panels)
-    loads = len(gates) == 2
 
     def body(*refs):
-        lag_ref, panel_refs, gate_refs = refs[0], refs[1:count], refs[count : count + len(gates)]
-        block_ref, values_ref, held, sems = refs[-4 - loads : len(refs) - loads]
+        lag_ref, panel_refs, gate_ref = refs[0], refs[1:count], refs[count]
+        block_ref, values_ref, held, sems = refs[-4:]
         core = core_of()
         to_block = core == role_at
-        gate = refs[-1] if loads else gate_refs[0]
-
-        def load(ref):
-            return pltpu.make_async_copy(ref, gate, sems.at[2 * nb])
 
         def store(at, columns, ref):
             return pltpu.make_async_copy(held.at[at], ref.at[:, columns], sems.at[at])
 
-        if loads:
+        for at in range(len(frames) * nb):
+            frame, b = frames[at // nb], at % nb
+            half = core if frame == 0 else 1 - core
+            group = block_group(half, b, width, bw)
+            total = total_of(lag_ref, group, frame, frame * nb + b, pl.ds(b * bw, bw), *panel_refs)
+            columns = pl.ds(pl.multiple_of(half * hw + b * bw, 128), bw)
+            held[at] = (total * gate_ref[:, columns].astype(F32)).astype(BF16)
 
             @pl.when(to_block)
             def _():
-                load(gate_refs[1]).start()
+                store(at, columns, block_ref).start()
 
             @pl.when(jnp.logical_not(to_block))
             def _():
-                load(gate_refs[0]).start()
-
-        for frame in range(2):
-            half = core if frame == 0 else 1 - core
-            for b in range(nb):
-                at = frame * nb + b
-                group = block_group(half, b, width, bw)
-                total = total_of(lag_ref, group, frame, b, at, pl.ds(b * bw, bw), *panel_refs)
-                if at == 0 and loads:
-                    load(gate_refs[0]).wait()
-                columns = pl.ds(pl.multiple_of(half * hw + b * bw, 128), bw)
-                held[at] = (total * gate[:, columns].astype(F32)).astype(BF16)
-
-                @pl.when(to_block)
-                def _():
-                    store(at, columns, block_ref).start()
-
-                @pl.when(jnp.logical_not(to_block))
-                def _():
-                    store(at, columns, values_ref).start()
-
-        for at in range(2 * nb):
+                store(at, columns, values_ref).start()
+
+        for at in range(len(frames) * nb):
             store(at, pl.ds(0, bw), block_ref).wait()
 
     shape = jax.ShapeDtypeStruct((span, width), BF16)
-    scratch = [pltpu.VMEM((2 * nb, span, bw), BF16), pltpu.SemaphoreType.DMA((2 * nb + 1,))]
-    if loads:
-        scratch.append(pltpu.VMEM((span, width), BF16))
-    first = count + len(gates)
-    return call(
-        body,
-        f"out_{role.lower()}",
+    return call(
+        body,
+        f"out_{role.lower()}" + "".join(map(str, frames)),
         [shape, shape],
-        [SMEM] + [VMEM] * (count - 1) + [HBM if loads else VMEM] * len(gates) + [HBM] * len(results),
+        [SMEM] + [VMEM] * count + [HBM] * len(results),
         [HBM, HBM],
-        scratch,
-        {first: 0, first + 1: 1} if results else None,
-        flops=Q_OUTPUT_FLOPS if role == "Q" else 1,
-    )(*panels, *gates, *results)
-
-
-def q_output(lags, slots, toeplitz, sums, x0, x1, r2, key, query):
-    def total_of(lag_ref, group, frame, b, place, at, t_ref, sums_ref, x00, x01, x10, x11, r20, r21):
+        [
+            pltpu.VMEM((len(frames) * nb, span, bw), BF16),
+            pltpu.SemaphoreType.DMA((len(frames) * nb,)),
+        ],
+        {count + 1: 0, count + 2: 1} if results else None,
+    )(*panels, gate, *results)
+
+
+def q_output(frame, lags, slots, toeplitz, sums, x0, x1, r2, gate, results):
+    def total_of(lag_ref, group, frame, place, at, t_ref, sums_ref, x0_ref, x1_ref, r2_ref):
         is_one = short_lag(lag_ref, group, slots) == 1
-        panel = jnp.where(is_one, (x00, x01)[frame][:, at], (x10, x11)[frame][:, at])
-        panel = kept(panel, jnp.logical_or(is_one, valid("Q", 2)))
-        last = kept((r20, r21)[frame][:, at], valid("Q", 3))
+        panel = kept(jnp.where(is_one, x0_ref[:, at], x1_ref[:, at]), jnp.logical_or(is_one, valid("Q", 2)))
+        last = kept(r2_ref[:, at], valid("Q", 3))
         total = sums_ref[1, frame, :, at]
         total += jnp.dot(t_ref[1, place, 1], panel, preferred_element_type=F32)
         return total + jnp.dot(t_ref[1, place, 2], last, preferred_element_type=F32)
 
-    return gated_output("Q", (lags, toeplitz, sums, *x0, *x1, *r2), total_of, (key, query), ())
+    return gated_output("Q", (frame,), (lags, toeplitz, sums, x0, x1, r2), total_of, gate, results)
 
 
 def p_output(lags, toeplitz, sums, r3, gate, results):
-    def total_of(lag_ref, group, frame, b, place, at, t_ref, sums_ref, r3_ref):
-        last = jnp.dot(t_ref[0, place, 2], kept(r3_ref[frame, :, at], valid("P", 3)), preferred_element_type=F32)
-        return sums_ref[frame, :, at] + last
-
-    return gated_output("P", (lags, toeplitz, sums, r3), total_of, (gate,), results)
+    def total_of(lag_ref, group, frame, place, at, t_ref, sums_ref, r3_ref):
+        last = kept(r3_ref[frame, :, at], valid("P", 3))
+        return sums_ref[frame, :, at] + jnp.dot(t_ref[0, place, 2], last, preferred_element_type=F32)
+
+    return gated_output("P", (0, 1), (lags, toeplitz, sums, r3), total_of, gate, results)
 
 
 def after(value, *others):
@@ -441,7 +424,7 @@
     return call(body, "add_rows", shape, [VMEM] * len(parts), VMEM)(*parts)
 
 
-def sum_over_chips(rows):
+def sum_over_chips(rows, work):
     count = lax.axis_size("ctx")
     if count & (count - 1):
         return lax.psum(rows, "ctx")
@@ -449,6 +432,11 @@
     while bit < count:
         steps = [k * bit for k in (3, 2, 1) if k * bit < count]
         others = [lax.ppermute(rows, "ctx", [(i, i ^ step) for i in range(count)]) for step in steps]
+        if bit == 2:
+            others = list(lax.optimization_barrier((*others, work))[:-1])
+        if len(others) == 3:
+            farthest = added(others[:1])
+            others = [farthest] + list(lax.optimization_barrier((others[1], others[2], farthest))[:2])
         rows = added(others + [rows])
         bit *= 4
     return rows
@@ -472,33 +460,48 @@
     return call(body, "join_rows", shape, [VMEM] * 2, VMEM)(first, second)
 
 
+def crossed(bit):
+    ctxs, chans = lax.axis_size("ctx"), lax.axis_size("chan")
+    core = 1 if ctxs % 2 == 0 else 0
+    return [(i * chans + c, (i ^ core) * chans + (c ^ bit)) for i in range(ctxs) for c in range(chans)]
+
+
 def gather_over_chan(rows, works):
     count = lax.axis_size("chan")
     if count & (count - 1):
-        return lax.all_gather(rows, "chan", axis=0, tiled=True)
-    bit = 1
+        return lax.all_gather(rows, "chan", axis=0, tiled=True), None
+    bit, other = 1, None
     while bit < count:
-        other = lax.ppermute(rows, "chan", [(i, i ^ bit) for i in range(count)])
+        if other is not None:
+            rows = joined(rows, other, bit // 2)
+        other = lax.ppermute(rows, ("ctx", "chan"), crossed(bit))
         if works:
             other = after(other, works[0])
             works = works[1:]
-        rows = joined(rows, other, bit)
         bit *= 2
-    return rows
-
-
-def filter_gradients(rows, groups, span, scale):
-    _, rows_per, doubled = rows.shape
+    return rows, other
+
+
+def filter_gradients(rows, other, groups, span, scale):
+    blocks, rows_per, doubled = rows.shape
     slots = rows_per - 1
-    repeat = rows.shape[0] // groups
-
-    def body(rows_ref, far_ref, near_ref):
-        for group in range(groups):
-            total = rows_ref[group * repeat]
-            for at in range(1, repeat):
-                total = total + rows_ref[group * repeat + at]
-            far_ref[group] = total[1:] * scale
-            near_ref[pl.ds(group, 1), :] = total[:1, span:] * scale
+    lists = [rows] if other is None else [rows, other]
+    repeat = len(lists) * blocks // groups
+    count = lax.axis_size("chan")
+
+    def body(*refs):
+        far_ref, near_ref = refs[-2:]
+        upper = lax.div(2 * lax.axis_index("chan"), count) if len(lists) == 2 else 0
+        for at in range(0, len(lists) * blocks, repeat):
+            source = refs[at // blocks]
+            total = source[at % blocks]
+            for more in range(at % blocks + 1, at % blocks + repeat):
+                total = total + source[more]
+            place = at // repeat
+            if len(lists) == 2:
+                place = lax.rem(place + upper * (groups // 2), groups)
+            far_ref[place] = total[1:] * scale
+            near_ref[pl.ds(place, 1), :] = total[:1, span:] * scale
 
     return call(
         body,
@@ -507,9 +510,9 @@
             jax.ShapeDtypeStruct((groups, slots, doubled), F32),
             jax.ShapeDtypeStruct((groups, span), F32),
         ],
-        [VMEM],
+        [VMEM] * len(lists),
         [VMEM, VMEM],
-    )(rows)
+    )(*lists)
 
 
 def per_device(
@@ -554,7 +557,7 @@
     toeplitz = toeplitz_matrices(lags, far_taps, near_taps, span, width, bw)
     near = correlate_near(p_own, q_own)
 
-    sums = near_sums(toeplitz, p_own, q_own)
+    sums, p_gate, q_gate = near_sums(toeplitz, p_own, q_own, streams[0], streams[2])
 
     r2a = send(after(pa, near, sums), to_far)
     r1 = lax.optimization_barrier(((r1a, r1b), sums, near))[0]
@@ -564,17 +567,18 @@
     both, r1 = lax.optimization_barrier((stacked(r1), r1))
     rows = correlate_far(lags, slots, near, p_own, q_own, r1[0], x0a, x1, r2a)
     r3 = send(after(both, rows), onward)
-    rows = sum_over_cores(sum_over_chips(rows))
-    pb_late, r2_late, rows = lax.optimization_barrier((pb, (r2a, r2b), rows))
-    x0b = send(pb_late, swap)
+    q_sums, pb_late, r2b, _ = lax.optimization_barrier((sums, pb, r2b, rows))
+    results = q_output(0, lags, slots, toeplitz, q_sums, x0a, x1[0], r2a, q_gate, ())
+    x0b = send(after(pb_late, r2b), swap)
+    rows = sum_over_cores(sum_over_chips(rows, results[0]))
+    r2_late, rows = lax.optimization_barrier(((r2a, r2b), rows))
     x2 = (send(r2_late[1], swap), send(r2_late[0], swap))
-    gates = (key_stream, query_stream)
-    results = q_output(lags, slots, toeplitz, sums, (x0a, x0b), x1, (r2a, r2b), *gates)
-    gate, sums = partial_sums(lags, slots, toeplitz, sums, r1, x2, *gates)
-    rows = gather_over_chan(rows, [results[0], sums])
-    results = p_output(lags, toeplitz, sums, r3, gate, results)
+    results = q_output(1, lags, slots, toeplitz, sums, x0b, x1[1], r2b, q_gate, results)
+    sums = partial_sums(lags, slots, toeplitz, sums, r1, x2)
+    rows, other = gather_over_chan(rows, [results[0], sums])
     scale = 1.0 / math.sqrt(span * count * GSIZE)
-    far, near = filter_gradients(rows, groups, span, scale)
+    far, near = filter_gradients(rows, other, groups, span, scale)
+    results = p_output(lags, toeplitz, sums, r3, p_gate, results)
     return (results[0], results[1], far, near)
 
 

time: 49.2 us -> 46.5 us (0.945)
  waiting for transfers between devices: 16.3 us -> 10.8 us
  Pallas kernels: 16.9 us -> 19.3 us
    ppermute x3, waiting for transfers between devices: 5.17 us -> 1.36 us  [sum_over_chips(): lax.ppermute(rows, 'ctx', [(i, i ^ step) for i in range(count)])]
    pallas_call x15 -> x16, Pallas kernels: 16.9 us -> 19.3 us  [run(): pl.pallas_call(body, in_specs=in_specs, out_specs=out_specs, out_shape=ou...]
    ppermute x11, waiting for transfers between devices: 8.3 us -> 6.64 us  [send(): return lax.ppermute(value, ('ctx', 'chan'), moves)]
    ppermute x11, starting transfers between devices: 7.25 us -> 8.04 us  [send(): return lax.ppermute(value, ('ctx', 'chan'), moves)]
    ppermute x1, waiting for transfers between devices: 1.19 us -> 0.7 us  [sum_over_cores(): lax.ppermute(rows, 'ctx', [(i, i ^ 1) for i in range(count)])]
  transfers between devices with their start and end apart: 17 -> 17, of which waited for: 7 -> 6; matrix products, arithmetic and copies ran while one was open for 0% -> 0% of each run, Pallas kernels for 27% -> 34%
where the time goes in v3:
time: 46.5 us; the launch traced here: 46.3 us
  Pallas kernels  19.3 us (42%)
  starting transfers between devices  15.2 us (33%)
  waiting for transfers between devices  10.8 us (23%)
  between operations  0.79 us (2%)
    pallas_call x16, Pallas kernels, run(): pl.pallas_call(body, in_specs=in_specs, out_specs=out_specs, out_shape=ou...  19.3 us
    ppermute x11, starting transfers between devices, send(): return lax.ppermute(value, ('ctx', 'chan'), moves)  8.04 us
    ppermute x11, waiting for transfers between devices, send(): return lax.ppermute(value, ('ctx', 'chan'), moves)  6.64 us
    ppermute x3, starting transfers between devices, sum_over_chips(): lax.ppermute(rows, 'ctx', [(i, i ^ step) for i in range(count)])  4.45 us
    ppermute x2, starting transfers between devices, gather_over_chan(): other = lax.ppermute(rows, ('ctx', 'chan'), crossed(bit))  2.63 us
    ppermute x2, waiting for transfers between devices, gather_over_chan(): other = lax.ppermute(rows, ('ctx', 'chan'), crossed(bit))  2.09 us
    ppermute x3, waiting for transfers between devices, sum_over_chips(): lax.ppermute(rows, 'ctx', [(i, i ^ step) for i in range(count)])  1.36 us
  transfers between devices with their start and end apart: 17, of which 6 were waited for; matrix products, arithmetic and copies ran while one was open for 0% of the time, Pallas kernels for 34%

profile of v3, /device:TPU:0, one launch (start us, length us, event | category | flops | bytes accessed | tf_op | source)
XLA Modules:
  0.0 46.3 jit_solution(9629197216510775483)
XLA Ops:
  0.7 1.7 %q_stream.1 = (bf16[256,1024]{1,0:T(8,128)(2,1)S(1)}, bf16[256,1024]{1,0:T(8,128)(2,1)S(1)}) custom-call(bf16[256,2048]{1,0:T(8,128)(2,1)} %key_ref.1, bf16[256,2048]{1,0:T(8,128)(2,1)} %v_ref.2, bf16[256,2048]{1,0:T(8,128)(2,1)} %query_ref.1, bf16[256,2048]{1,0:T(8,128)(2,1)} %g_ref.2), custom_call_target="tpu_custom_call" | custom-call | flops 1 | bytes 5242880 | tf_op jit(solution)/shard_map/q_stream/pallas_call | solution.py:30
  2.4 3.0 %collective-permute-start = (bf16[256,1024]{1,0:T(8,128)(2,1)S(1)}, bf16[256,1024]{1,0:T(8,128)(2,1)S(1)}, u32[]{:S(2)}, u32[]{:S(2)}) collective-permute-start(bf16[256,1024]{1,0:T(8,128)(2,1)S(1)} %get-tuple-element.59.q1), channel_id=1, source_target_pairs={{0,1},{1,0},{2,3},{3,2},{4,8},{5,9},{6,10},{7,11},{8,4},{9,5},{10,... | collective-permute-start | bytes 1572872 | tf_op jit(solution)/shard_map/ppermute | solution.py:544
  5.4 0.1 collective-permute-start.1
  5.4 0.1 copy.16
  5.5 0.1 reshape.11.lag_ref.refs_0_
  5.6 3.7 %toeplitz.1.t_ref.refs_1_ = bf16[2,4,3,256,256]{4,3,2,1,0:T(8,128)(2,1)S(1)} custom-call(s32[32]{0:T(128)S(1)} %reshape.11.lag_ref.refs_0_, bf16[16,2,512]{2,1,0:T(2,128)(2,1)S(1)} %copy-done, bf16[16,256]{1,0:T(8,128)(2,1)S(1)} %copy-done.1), custom_call_target="tpu_custom_call" | custom-call | flops 1 | bytes 3186816 | tf_op jit(solution)/shard_map/toeplitz/pallas_call | solution.py:30
  9.3 1.7 %p_stream.1 = (bf16[256,1024]{1,0:T(8,128)(2,1)S(1)}, bf16[256,1024]{1,0:T(8,128)(2,1)S(1)}) custom-call(bf16[256,2048]{1,0:T(8,128)(2,1)} %key_ref.1, bf16[256,2048]{1,0:T(8,128)(2,1)} %v_ref.2, bf16[256,2048]{1,0:T(8,128)(2,1)} %query_ref.1, bf16[256,2048]{1,0:T(8,128)(2,1)} %g_ref.2), custom_call_target="tpu_custom_call" | custom-call | flops 1 | bytes 5242880 | tf_op jit(solution)/shard_map/p_stream/pallas_call | solution.py:30
  11.0 1.0 %correlate_near.1.near_ref = f32[2,2,512]{2,1,0:T(2,128)S(1)} custom-call(bf16[256,1024]{1,0:T(8,128)(2,1)S(1)} %get-tuple-element.83.p0, bf16[256,1024]{1,0:T(8,128)(2,1)S(1)} %get-tuple-element.67.p1, bf16[256,1024]{1,0:T(8,128)(2,1)S(1)} %get-tuple-element.49.q0.q_ref, bf16[256,1024]{1,0:T(8,128)(2,1)S(1)} %get-tuple-element.59.q1), custom_call_target="tpu_custom_call" | custom-call | flops 1 | bytes 2105344 | tf_op jit(solution)/shard_map/correlate_near/pallas_call | solution.py:30
  12.0 2.1 %near_sums.1 = (f32[2,2,256,1024]{3,2,1,0:T(8,128)S(1)}, bf16[256,2048]{1,0:T(8,128)(2,1)S(1)}, bf16[256,2048]{1,0:T(8,128)(2,1)S(1)}) custom-call(bf16[2,4,3,256,256]{4,3,2,1,0:T(8,128)(2,1)S(1)} %toeplitz.1.t_ref.refs_1_, bf16[256,1024]{1,0:T(8,128)(2,1)S(1)} %get-tuple-element.83.p0, bf16[256,1024]{1,0:T(8,128)(2,1)S(1)} %get-tuple-element.67.p1, ...), custom_call_target="tpu_custom_call" | custom-call | flops 1 | bytes 13631488 | tf_op jit(solution)/shard_map/near_sums/pallas_call | solution.py:30
  14.2 1.4 %collective-permute-start.2 = (bf16[256,1024]{1,0:T(8,128)(2,1)S(1)}, bf16[256,1024]{1,0:T(8,128)(2,1)S(1)}, u32[]{:S(2)}, u32[]{:S(2)}) collective-permute-start(bf16[256,1024]{1,0:T(8,128)(2,1)S(1)} %get-tuple-element.67.p1), channel_id=1, source_target_pairs={{0,12},{1,13},{2,14},{3,15},{4,5},{5,4},{6,7},{7,6},{8,20},{9,21},... | collective-permute-start | bytes 1572872 | tf_op jit(solution)/shard_map/ppermute | solution.py:544
  15.6 3.6 %collective-permute-done.1.refs_1_.r11 = bf16[256,1024]{1,0:T(8,128)(2,1)S(1)} collective-permute-done((bf16[256,1024]{1,0:T(8,128)(2,1)S(1)}, bf16[256,1024]{1,0:T(8,128)(2,1)S(1)}, u32[]{:S(2)}, u32[]{:S(2)}) %collective-permute-start.1) | collective-permute-done | bytes 524320 | tf_op jit(solution)/shard_map/ppermute | solution.py:544
  19.3 0.5 %collective-permute-start.5 = (bf16[256,1024]{1,0:T(8,128)(2,1)S(1)}, bf16[256,1024]{1,0:T(8,128)(2,1)S(1)}, u32[]{:S(2)}, u32[]{:S(2)}) collective-permute-start(bf16[256,1024]{1,0:T(8,128)(2,1)S(1)} %collective-permute-done.1.refs_1_.r11), channel_id=1, source_target_pairs={{0,4},{1,5},{2,6},{3,7},{4,0},{5,1},{6,2},{7,3},{8,12},{9,13},{10,... | collective-permute-start | bytes 1572872 | tf_op jit(solution)/shard_map/ppermute | solution.py:544
  19.8 1.0 %collective-permute-start.3 = (bf16[256,1024]{1,0:T(8,128)(2,1)S(1)}, bf16[256,1024]{1,0:T(8,128)(2,1)S(1)}, u32[]{:S(2)}, u32[]{:S(2)}) collective-permute-start(bf16[256,1024]{1,0:T(8,128)(2,1)S(1)} %get-tuple-element.83.p0), channel_id=1, source_target_pairs={{0,12},{1,13},{2,14},{3,15},{4,5},{5,4},{6,7},{7,6},{8,20},{9,21},... | collective-permute-start | bytes 1572872 | tf_op jit(solution)/shard_map/ppermute | solution.py:544
  20.9 3.0 %collective-permute-done.2.r2_ref.refs_5_ = bf16[256,1024]{1,0:T(8,128)(2,1)S(1)} collective-permute-done((bf16[256,1024]{1,0:T(8,128)(2,1)S(1)}, bf16[256,1024]{1,0:T(8,128)(2,1)S(1)}, u32[]{:S(2)}, u32[]{:S(2)}) %collective-permute-start.2) | collective-permute-done | bytes 524320 | tf_op jit(solution)/shard_map/ppermute | solution.py:544
  23.9 2.0 %correlate_far.1.refs_3_ = f32[4,3,512]{2,1,0:T(4,128)S(1)} custom-call(s32[32]{0:T(128)S(1)} %reshape.11.lag_ref.refs_0_, f32[2,2,512]{2,1,0:T(2,128)S(1)} %correlate_near.1.near_ref, bf16[256,1024]{1,0:T(8,128)(2,1)S(1)} %get-tuple-element.83.p0, bf16[256,1024]{1,0:T(8,128)(2,1)S(1)} %get-tuple-element.67.p1, ...), custom_call_target="tpu_custom_call" | custom-call | flops 1 | bytes 4227200 | tf_op jit(solution)/shard_map/correlate_far/pallas_call | solution.py:30
  25.9 3.4 %collective-permute-start.7 = (f32[4,3,512]{2,1,0:T(4,128)S(1)}, f32[4,3,512]{2,1,0:T(4,128)S(1)}, u32[]{:S(2)}, u32[]{:S(2)}) collective-permute-start(f32[4,3,512]{2,1,0:T(4,128)S(1)} %correlate_far.1.refs_3_), channel_id=1, source_target_pairs={{0,24},{4,28},{8,16},{12,20},{16,8},{20,12},{24,0},{28,4},{1,25},{... | collective-permute-start | bytes 73736 | tf_op jit(solution)/shard_map/ppermute | solution.py:434
  29.3 1.1 %collective-permute-start.9 = (f32[4,3,512]{2,1,0:T(4,128)S(1)}, f32[4,3,512]{2,1,0:T(4,128)S(1)}, u32[]{:S(2)}, u32[]{:S(2)}) collective-permute-start(f32[4,3,512]{2,1,0:T(4,128)S(1)} %correlate_far.1.refs_3_), channel_id=1, source_target_pairs={{0,8},{4,12},{8,0},{12,4},{16,24},{20,28},{24,16},{28,20},{1,9},{5... | collective-permute-start | bytes 73736 | tf_op jit(solution)/shard_map/ppermute | solution.py:434
  30.3 1.0 %collective-permute-start.13 = (bf16[2,256,1024]{2,1,0:T(8,128)(2,1)S(1)}, bf16[2,256,1024]{2,1,0:T(8,128)(2,1)S(1)}, u32[]{:S(2)}, u32[]{:S(2)}) collective-permute-start(bf16[2,256,1024]{2,1,0:T(8,128)(2,1)S(1)} %stack.1), channel_id=1, source_target_pairs={{0,8},{1,9},{2,10},{3,11},{4,0},{5,1},{6,2},{7,3},{8,16},{9,17},{1... | collective-permute-start | bytes 3145736 | tf_op jit(solution)/shard_map/ppermute | solution.py:544
  31.3 1.8 %out_q0.1 = (bf16[256,2048]{1,0:T(8,128)(2,1)}, bf16[256,2048]{1,0:T(8,128)(2,1)}) custom-call(s32[32]{0:T(128)S(1)} %reshape.11.lag_ref.refs_0_, bf16[2,4,3,256,256]{4,3,2,1,0:T(8,128)(2,1)S(1)} %toeplitz.1.t_ref.refs_1_, f32[2,2,256,1024]{3,2,1,0:T(8,128)S(1)} %get-tuple-element.69.refs_2_.sums_ref, ...), custom_call_target="tpu_custom_call" | custom-call | flops 1 | bytes 12058752 | tf_op jit(solution)/shard_map/out_q0/pallas_call | solution.py:30
  33.1 1.4 %collective-permute-done.8.refs_1_ = f32[4,3,512]{2,1,0:T(4,128)S(1)} collective-permute-done((f32[4,3,512]{2,1,0:T(4,128)S(1)}, f32[4,3,512]{2,1,0:T(4,128)S(1)}, u32[]{:S(2)}, u32[]{:S(2)}) %collective-permute-start.8) | collective-permute-done | bytes 24608 | tf_op jit(solution)/shard_map/ppermute | solution.py:434
  34.5 0.5 %collective-permute-start.14 = (bf16[256,1024]{1,0:T(8,128)(2,1)S(1)}, bf16[256,1024]{1,0:T(8,128)(2,1)S(1)}, u32[]{:S(2)}, u32[]{:S(2)}) collective-permute-start(bf16[256,1024]{1,0:T(8,128)(2,1)S(1)} %get-tuple-element.83.p0), channel_id=1, source_target_pairs={{0,4},{1,5},{2,6},{3,7},{4,0},{5,1},{6,2},{7,3},{8,12},{9,13},{10,... | collective-permute-start | bytes 1572872 | tf_op jit(solution)/shard_map/ppermute | solution.py:544
  35.0 0.7 %collective-permute-done.10.refs_1_ = f32[4,3,512]{2,1,0:T(4,128)S(1)} collective-permute-done((f32[4,3,512]{2,1,0:T(4,128)S(1)}, f32[4,3,512]{2,1,0:T(4,128)S(1)}, u32[]{:S(2)}, u32[]{:S(2)}) %collective-permute-start.10) | collective-permute-done | bytes 24608 | tf_op jit(solution)/shard_map/ppermute | solution.py:449
  35.7 0.2 collective-permute-start.11
  35.9 0.3 collective-permute-start.12
  36.2 1.3 %collective-permute-start.15 = (f32[4,3,512]{2,1,0:T(4,128)S(1)}, f32[4,3,512]{2,1,0:T(4,128)S(1)}, u32[]{:S(2)}, u32[]{:S(2)}) collective-permute-start(f32[4,3,512]{2,1,0:T(4,128)S(1)} %add_rows.5.first_ref), channel_id=1, source_target_pairs={{0,5},{1,4},{2,7},{3,6},{4,1},{5,0},{6,3},{7,2},{8,13},{9,12},{10,... | collective-permute-start | bytes 73736 | tf_op jit(solution)/shard_map/ppermute | solution.py:477
  37.5 1.7 %out_q1.1 = (bf16[256,2048]{1,0:T(8,128)(2,1)}, bf16[256,2048]{1,0:T(8,128)(2,1)}) custom-call(s32[32]{0:T(128)S(1)} %reshape.11.lag_ref.refs_0_, bf16[2,4,3,256,256]{4,3,2,1,0:T(8,128)(2,1)S(1)} %toeplitz.1.t_ref.refs_1_, f32[2,2,256,1024]{3,2,1,0:T(8,128)S(1)} %get-tuple-element.69.refs_2_.sums_ref, ...), custom_call_target="tpu_custom_call", output_to_operand_aliasing={{0}: (7, {}), {1}: (8, {})} | custom-call | flops 1 | bytes 14155904 | tf_op jit(solution)/shard_map/out_q1/pallas_call | solution.py:30
  39.2 0.3 collective-permute-done.15.second_ref
  39.6 1.4 %collective-permute-start.16 = (f32[8,3,512]{2,1,0:T(4,128)S(1)}, f32[8,3,512]{2,1,0:T(4,128)S(1)}, u32[]{:S(2)}, u32[]{:S(2)}) collective-permute-start(f32[8,3,512]{2,1,0:T(4,128)S(1)} %join_rows.1.refs_0_), channel_id=1, source_target_pairs={{0,6},{1,7},{2,4},{3,5},{4,2},{5,3},{6,0},{7,1},{8,14},{9,15},{10,... | collective-permute-start | bytes 147464 | tf_op jit(solution)/shard_map/ppermute | solution.py:477
  41.0 1.1 %partial_sums.1.refs_2_ = f32[2,256,1024]{2,1,0:T(8,128)S(1)} custom-call(s32[32]{0:T(128)S(1)} %reshape.11.lag_ref.refs_0_, bf16[2,4,3,256,256]{4,3,2,1,0:T(8,128)(2,1)S(1)} %toeplitz.1.t_ref.refs_1_, f32[2,2,256,1024]{3,2,1,0:T(8,128)S(1)} %get-tuple-element.69.refs_2_.sums_ref, bf16[256,1024]{1,0:T(8,128)(2,1)S(1)} %collective-permute-done.refs_0_.r1_ref.r10, ...), custom_call_target="tpu_custom_call" | custom-call | flops 5200000000 | bytes 11534464 | tf_op jit(solution)/shard_map/partial_sums/pallas_call | solution.py:30
  42.0 1.8 %collective-permute-done.16.refs_1_ = f32[8,3,512]{2,1,0:T(4,128)S(1)} collective-permute-done((f32[8,3,512]{2,1,0:T(4,128)S(1)}, f32[8,3,512]{2,1,0:T(4,128)S(1)}, u32[]{:S(2)}, u32[]{:S(2)}) %collective-permute-start.16) | collective-permute-done | bytes 49184 | tf_op jit(solution)/shard_map/ppermute | solution.py:477
  43.8 0.7 %filter_gradients.1 = (f32[16,2,512]{2,1,0:T(2,128)}, f32[16,256]{1,0:T(8,128)}) custom-call(f32[8,3,512]{2,1,0:T(4,128)S(1)} %join_rows.1.refs_0_, f32[8,3,512]{2,1,0:T(4,128)S(1)} %collective-permute-done.16.refs_1_), custom_call_target="tpu_custom_call" | custom-call | flops 1 | bytes 180224 | tf_op jit(solution)/shard_map/filter_gradients/pallas_call | solution.py:30
  44.5 1.8 %out_p01.1 = (bf16[256,2048]{1,0:T(8,128)(2,1)}, bf16[256,2048]{1,0:T(8,128)(2,1)}) custom-call(s32[32]{0:T(128)S(1)} %reshape.11.lag_ref.refs_0_, bf16[2,4,3,256,256]{4,3,2,1,0:T(8,128)(2,1)S(1)} %toeplitz.1.t_ref.refs_1_, f32[2,256,1024]{2,1,0:T(8,128)S(1)} %partial_sums.1.refs_2_, ...), custom_call_target="tpu_custom_call", output_to_operand_aliasing={{0}: (5, {}), {1}: (6, {})} | custom-call | flops 1 | bytes 11534464 | tf_op jit(solution)/shard_map/out_p01/pallas_call | solution.py:30
  (26 shorter events, 0.3 us)
Async XLA Ops:
  0.6 5.0 %copy-start = (bf16[16,2,512]{2,1,0:T(2,128)(2,1)S(1)}, bf16[16,2,512]{2,1,0:T(2,128)(2,1)}, u32[]{:S(2)}) copy-start(bf16[16,2,512]{2,1,0:T(2,128)(2,1)} %far_ref) | copy-start | bytes 98308
  0.6 5.0 %copy-start.1 = (bf16[16,256]{1,0:T(8,128)(2,1)S(1)}, bf16[16,256]{1,0:T(8,128)(2,1)}, u32[]{:S(2)}) copy-start(bf16[16,256]{1,0:T(8,128)(2,1)} %near_ref) | copy-start | bytes 24580
  0.7 4.8 %copy-start.2 = (s32[16,2]{0,1:T(2,128)S(1)}, s32[16,2]{0,1:T(2,128)}, u32[]{:S(2)}) copy-start(s32[16,2]{0,1:T(2,128)} %param.13) | copy-start | bytes 388
  2.4 13.3 %collective-permute-start = (bf16[256,1024]{1,0:T(8,128)(2,1)S(1)}, bf16[256,1024]{1,0:T(8,128)(2,1)S(1)}, u32[]{:S(2)}, u32[]{:S(2)}) collective-permute-start(bf16[256,1024]{1,0:T(8,128)(2,1)S(1)} %get-tuple-element.59.q1), channel_id=1, source_target_pairs={{0,1},{1,0},{2,3},{3,2},{4,8},{5,9},{6,10},{7,11},{8,4},{9,5},{10,... | collective-permute-start | bytes 1572872 | tf_op jit(solution)/shard_map/ppermute | solution.py:544
  5.4 13.9 %collective-permute-start.1 = (bf16[256,1024]{1,0:T(8,128)(2,1)S(1)}, bf16[256,1024]{1,0:T(8,128)(2,1)S(1)}, u32[]{:S(2)}, u32[]{:S(2)}) collective-permute-start(bf16[256,1024]{1,0:T(8,128)(2,1)S(1)} %get-tuple-element.49.q0.q_ref), channel_id=1, source_target_pairs={{0,1},{1,0},{2,3},{3,2},{4,8},{5,9},{6,10},{7,11},{8,4},{9,5},{10,... | collective-permute-start | bytes 1572872 | tf_op jit(solution)/shard_map/ppermute | solution.py:544
  14.2 9.7 %collective-permute-start.2 = (bf16[256,1024]{1,0:T(8,128)(2,1)S(1)}, bf16[256,1024]{1,0:T(8,128)(2,1)S(1)}, u32[]{:S(2)}, u32[]{:S(2)}) collective-permute-start(bf16[256,1024]{1,0:T(8,128)(2,1)S(1)} %get-tuple-element.67.p1), channel_id=1, source_target_pairs={{0,12},{1,13},{2,14},{3,15},{4,5},{5,4},{6,7},{7,6},{8,20},{9,21},... | collective-permute-start | bytes 1572872 | tf_op jit(solution)/shard_map/ppermute | solution.py:544
  19.3 4.6 %collective-permute-start.4 = (bf16[256,1024]{1,0:T(8,128)(2,1)S(1)}, bf16[256,1024]{1,0:T(8,128)(2,1)S(1)}, u32[]{:S(2)}, u32[]{:S(2)}) collective-permute-start(bf16[256,1024]{1,0:T(8,128)(2,1)S(1)} %get-tuple-element.67.p1), channel_id=1, source_target_pairs={{0,4},{1,5},{2,6},{3,7},{4,0},{5,1},{6,2},{7,3},{8,12},{9,13},{10,... | collective-permute-start | bytes 1572872 | tf_op jit(solution)/shard_map/ppermute | solution.py:544
  19.3 4.6 %collective-permute-start.5 = (bf16[256,1024]{1,0:T(8,128)(2,1)S(1)}, bf16[256,1024]{1,0:T(8,128)(2,1)S(1)}, u32[]{:S(2)}, u32[]{:S(2)}) collective-permute-start(bf16[256,1024]{1,0:T(8,128)(2,1)S(1)} %collective-permute-done.1.refs_1_.r11), channel_id=1, source_target_pairs={{0,4},{1,5},{2,6},{3,7},{4,0},{5,1},{6,2},{7,3},{8,12},{9,13},{10,... | collective-permute-start | bytes 1572872 | tf_op jit(solution)/shard_map/ppermute | solution.py:544
  19.8 4.1 %collective-permute-start.6 = (bf16[256,1024]{1,0:T(8,128)(2,1)S(1)}, bf16[256,1024]{1,0:T(8,128)(2,1)S(1)}, u32[]{:S(2)}, u32[]{:S(2)}) collective-permute-start(bf16[256,1024]{1,0:T(8,128)(2,1)S(1)} %collective-permute-done.refs_0_.r1_ref.r10), channel_id=1, source_target_pairs={{0,4},{1,5},{2,6},{3,7},{4,0},{5,1},{6,2},{7,3},{8,12},{9,13},{10,... | collective-permute-start | bytes 1572872 | tf_op jit(solution)/shard_map/ppermute | solution.py:544
  19.8 11.5 %collective-permute-start.3 = (bf16[256,1024]{1,0:T(8,128)(2,1)S(1)}, bf16[256,1024]{1,0:T(8,128)(2,1)S(1)}, u32[]{:S(2)}, u32[]{:S(2)}) collective-permute-start(bf16[256,1024]{1,0:T(8,128)(2,1)S(1)} %get-tuple-element.83.p0), channel_id=1, source_target_pairs={{0,12},{1,13},{2,14},{3,15},{4,5},{5,4},{6,7},{7,6},{8,20},{9,21},... | collective-permute-start | bytes 1572872 | tf_op jit(solution)/shard_map/ppermute | solution.py:544
  25.9 7.2 %collective-permute-start.7 = (f32[4,3,512]{2,1,0:T(4,128)S(1)}, f32[4,3,512]{2,1,0:T(4,128)S(1)}, u32[]{:S(2)}, u32[]{:S(2)}) collective-permute-start(f32[4,3,512]{2,1,0:T(4,128)S(1)} %correlate_far.1.refs_3_), channel_id=1, source_target_pairs={{0,24},{4,28},{8,16},{12,20},{16,8},{20,12},{24,0},{28,4},{1,25},{... | collective-permute-start | bytes 73736 | tf_op jit(solution)/shard_map/ppermute | solution.py:434
  29.3 5.2 %collective-permute-start.8 = (f32[4,3,512]{2,1,0:T(4,128)S(1)}, f32[4,3,512]{2,1,0:T(4,128)S(1)}, u32[]{:S(2)}, u32[]{:S(2)}) collective-permute-start(f32[4,3,512]{2,1,0:T(4,128)S(1)} %correlate_far.1.refs_3_), channel_id=1, source_target_pairs={{0,16},{4,20},{8,24},{12,28},{16,0},{20,4},{24,8},{28,12},{1,17},{... | collective-permute-start | bytes 73736 | tf_op jit(solution)/shard_map/ppermute | solution.py:434
  29.3 5.2 %collective-permute-start.9 = (f32[4,3,512]{2,1,0:T(4,128)S(1)}, f32[4,3,512]{2,1,0:T(4,128)S(1)}, u32[]{:S(2)}, u32[]{:S(2)}) collective-permute-start(f32[4,3,512]{2,1,0:T(4,128)S(1)} %correlate_far.1.refs_3_), channel_id=1, source_target_pairs={{0,8},{4,12},{8,0},{12,4},{16,24},{20,28},{24,16},{28,20},{1,9},{5... | collective-permute-start | bytes 73736 | tf_op jit(solution)/shard_map/ppermute | solution.py:434
  30.3 14.2 %collective-permute-start.13 = (bf16[2,256,1024]{2,1,0:T(8,128)(2,1)S(1)}, bf16[2,256,1024]{2,1,0:T(8,128)(2,1)S(1)}, u32[]{:S(2)}, u32[]{:S(2)}) collective-permute-start(bf16[2,256,1024]{2,1,0:T(8,128)(2,1)S(1)} %stack.1), channel_id=1, source_target_pairs={{0,8},{1,9},{2,10},{3,11},{4,0},{5,1},{6,2},{7,3},{8,16},{9,17},{1... | collective-permute-start | bytes 3145736 | tf_op jit(solution)/shard_map/ppermute | solution.py:544
  34.4 1.3 %collective-permute-start.10 = (f32[4,3,512]{2,1,0:T(4,128)S(1)}, f32[4,3,512]{2,1,0:T(4,128)S(1)}, u32[]{:S(2)}, u32[]{:S(2)}) collective-permute-start(f32[4,3,512]{2,1,0:T(4,128)S(1)} %add_rows.4.refs_0_), channel_id=1, source_target_pairs={{0,4},{4,0},{8,12},{12,8},{16,20},{20,16},{24,28},{28,24},{1,5},{5... | collective-permute-start | bytes 73736 | tf_op jit(solution)/shard_map/ppermute | solution.py:449
  34.5 3.0 %collective-permute-start.14 = (bf16[256,1024]{1,0:T(8,128)(2,1)S(1)}, bf16[256,1024]{1,0:T(8,128)(2,1)S(1)}, u32[]{:S(2)}, u32[]{:S(2)}) collective-permute-start(bf16[256,1024]{1,0:T(8,128)(2,1)S(1)} %get-tuple-element.83.p0), channel_id=1, source_target_pairs={{0,4},{1,5},{2,6},{3,7},{4,0},{5,1},{6,2},{7,3},{8,12},{9,13},{10,... | collective-permute-start | bytes 1572872 | tf_op jit(solution)/shard_map/ppermute | solution.py:544
  35.7 5.2 %collective-permute-start.11 = (bf16[256,1024]{1,0:T(8,128)(2,1)S(1)}, bf16[256,1024]{1,0:T(8,128)(2,1)S(1)}, u32[]{:S(2)}, u32[]{:S(2)}) collective-permute-start(bf16[256,1024]{1,0:T(8,128)(2,1)S(1)} %collective-permute-done.3.refs_5_), channel_id=1, source_target_pairs={{0,4},{1,5},{2,6},{3,7},{4,0},{5,1},{6,2},{7,3},{8,12},{9,13},{10,... | collective-permute-start | bytes 1572872 | tf_op jit(solution)/shard_map/ppermute | solution.py:544
  35.9 5.1 %collective-permute-start.12 = (bf16[256,1024]{1,0:T(8,128)(2,1)S(1)}, bf16[256,1024]{1,0:T(8,128)(2,1)S(1)}, u32[]{:S(2)}, u32[]{:S(2)}) collective-permute-start(bf16[256,1024]{1,0:T(8,128)(2,1)S(1)} %collective-permute-done.2.r2_ref.refs_5_), channel_id=1, source_target_pairs={{0,4},{1,5},{2,6},{3,7},{4,0},{5,1},{6,2},{7,3},{8,12},{9,13},{10,... | collective-permute-start | bytes 1572872 | tf_op jit(solution)/shard_map/ppermute | solution.py:544
  36.2 3.3 %collective-permute-start.15 = (f32[4,3,512]{2,1,0:T(4,128)S(1)}, f32[4,3,512]{2,1,0:T(4,128)S(1)}, u32[]{:S(2)}, u32[]{:S(2)}) collective-permute-start(f32[4,3,512]{2,1,0:T(4,128)S(1)} %add_rows.5.first_ref), channel_id=1, source_target_pairs={{0,5},{1,4},{2,7},{3,6},{4,1},{5,0},{6,3},{7,2},{8,13},{9,12},{10,... | collective-permute-start | bytes 73736 | tf_op jit(solution)/shard_map/ppermute | solution.py:477
  39.6 4.2 %collective-permute-start.16 = (f32[8,3,512]{2,1,0:T(4,128)S(1)}, f32[8,3,512]{2,1,0:T(4,128)S(1)}, u32[]{:S(2)}, u32[]{:S(2)}) collective-permute-start(f32[8,3,512]{2,1,0:T(4,128)S(1)} %join_rows.1.refs_0_), channel_id=1, source_target_pairs={{0,6},{1,7},{2,4},{3,5},{4,2},{5,3},{6,0},{7,1},{8,14},{9,15},{10,... | collective-permute-start | bytes 147464 | tf_op jit(solution)/shard_map/ppermute | solution.py:477

commit v4 on v3

--- a/solution.py
+++ b/solution.py
@@ -329,17 +329,22 @@
     )(lags, toeplitz, sums, *r1, *x2)
 
 
-def gated_output(role, frames, panels, total_of, gate, results):
+def gated_output(role, frames, panels, total_of, gate, results, gradients=None):
     span, width = gate.shape
     hw = width // 2
     bw = min(GSIZE, hw)
     nb = hw // bw
     role_at = 0 if role == "P" else 1
     count = len(panels)
+    lists, shapes, lay_out = gradients or ([], [], None)
+    first = count + 1 + len(lists)
 
     def body(*refs):
         lag_ref, panel_refs, gate_ref = refs[0], refs[1:count], refs[count]
-        block_ref, values_ref, held, sems = refs[-4:]
+        row_refs = refs[count + 1 : count + 1 + len(lists)]
+        outs = refs[first + len(results) :]
+        block_ref, values_ref, grad_refs = outs[0], outs[1], outs[2 : 2 + len(shapes)]
+        held, sems, grads_held = outs[2 + len(shapes)], outs[3 + len(shapes)], outs[4 + len(shapes) :]
         core = core_of()
         to_block = core == role_at
 
@@ -362,22 +367,33 @@
             def _():
                 store(at, columns, values_ref).start()
 
+        if shapes:
+            lay_out(row_refs, grads_held)
+        copies = [
+            pltpu.make_async_copy(source, target, sems.at[len(frames) * nb + i])
+            for i, (source, target) in enumerate(zip(grads_held, grad_refs))
+        ]
+        for copy in copies:
+            copy.start()
         for at in range(len(frames) * nb):
             store(at, pl.ds(0, bw), block_ref).wait()
+        for copy in copies:
+            copy.wait()
 
     shape = jax.ShapeDtypeStruct((span, width), BF16)
     return call(
         body,
         f"out_{role.lower()}" + "".join(map(str, frames)),
-        [shape, shape],
-        [SMEM] + [VMEM] * count + [HBM] * len(results),
-        [HBM, HBM],
+        [shape, shape, *shapes],
+        [SMEM] + [VMEM] * (count + len(lists)) + [HBM] * len(results),
+        [HBM] * (2 + len(shapes)),
         [
             pltpu.VMEM((len(frames) * nb, span, bw), BF16),
-            pltpu.SemaphoreType.DMA((len(frames) * nb,)),
+            pltpu.SemaphoreType.DMA((len(frames) * nb + len(shapes),)),
+            *[pltpu.VMEM(s.shape, s.dtype) for s in shapes],
         ],
-        {count + 1: 0, count + 2: 1} if results else None,
-    )(*panels, gate, *results)
+        {first: 0, first + 1: 1} if results else None,
+    )(*panels, gate, *lists, *results)
 
 
 def q_output(frame, lags, slots, toeplitz, sums, x0, x1, r2, gate, results):
@@ -392,12 +408,12 @@
     return gated_output("Q", (frame,), (lags, toeplitz, sums, x0, x1, r2), total_of, gate, results)
 
 
-def p_output(lags, toeplitz, sums, r3, gate, results):
+def p_output(lags, toeplitz, sums, r3, gate, results, gradients):
     def total_of(lag_ref, group, frame, place, at, t_ref, sums_ref, r3_ref):
         last = kept(r3_ref[frame, :, at], valid("P", 3))
         return sums_ref[frame, :, at] + jnp.dot(t_ref[0, place, 2], last, preferred_element_type=F32)
 
-    return gated_output("P", (0, 1), (lags, toeplitz, sums, r3), total_of, gate, results)
+    return gated_output("P", (0, 1), (lags, toeplitz, sums, r3), total_of, gate, results, gradients)
 
 
 def after(value, *others):
@@ -430,14 +446,11 @@
         return lax.psum(rows, "ctx")
     bit = 2
     while bit < count:
-        steps = [k * bit for k in (3, 2, 1) if k * bit < count]
+        steps = [k * bit for k in (1, 2, 3) if k * bit < count]
         others = [lax.ppermute(rows, "ctx", [(i, i ^ step) for i in range(count)]) for step in steps]
         if bit == 2:
             others = list(lax.optimization_barrier((*others, work))[:-1])
-        if len(others) == 3:
-            farthest = added(others[:1])
-            others = [farthest] + list(lax.optimization_barrier((others[1], others[2], farthest))[:2])
-        rows = added(others + [rows])
+        rows = added(others[::-1] + [rows])
         bit *= 4
     return rows
 
@@ -484,13 +497,12 @@
 
 def filter_gradients(rows, other, groups, span, scale):
     blocks, rows_per, doubled = rows.shape
-    slots = rows_per - 1
     lists = [rows] if other is None else [rows, other]
     repeat = len(lists) * blocks // groups
     count = lax.axis_size("chan")
 
-    def body(*refs):
-        far_ref, near_ref = refs[-2:]
+    def lay_out(refs, outs):
+        far_ref, near_ref = outs
         upper = lax.div(2 * lax.axis_index("chan"), count) if len(lists) == 2 else 0
         for at in range(0, len(lists) * blocks, repeat):
             source = refs[at // blocks]
@@ -503,16 +515,11 @@
             far_ref[place] = total[1:] * scale
             near_ref[pl.ds(place, 1), :] = total[:1, span:] * scale
 
-    return call(
-        body,
-        "filter_gradients",
-        [
-            jax.ShapeDtypeStruct((groups, slots, doubled), F32),
-            jax.ShapeDtypeStruct((groups, span), F32),
-        ],
-        [VMEM] * len(lists),
-        [VMEM, VMEM],
-    )(*lists)
+    shapes = [
+        jax.ShapeDtypeStruct((groups, rows_per - 1, doubled), F32),
+        jax.ShapeDtypeStruct((groups, span), F32),
+    ]
+    return lists, shapes, lay_out
 
 
 def per_device(
@@ -577,9 +584,8 @@
     sums = partial_sums(lags, slots, toeplitz, sums, r1, x2)
     rows, other = gather_over_chan(rows, [results[0], sums])
     scale = 1.0 / math.sqrt(span * count * GSIZE)
-    far, near = filter_gradients(rows, other, groups, span, scale)
-    results = p_output(lags, toeplitz, sums, r3, p_gate, results)
-    return (results[0], results[1], far, near)
+    gradients = filter_gradients(rows, other, groups, span, scale)
+    return tuple(p_output(lags, toeplitz, sums, r3, p_gate, results, gradients))
 
 
 def solution(mesh):

time: 46.5 us -> 46.2 us (level)
  Pallas kernels: 19.3 us -> 18.7 us
    pallas_call x16 -> x14, Pallas kernels: 19.3 us -> 18.7 us  [run(): pl.pallas_call(body, in_specs=in_specs, out_specs=out_specs, out_shape=ou...]
  transfers between devices with their start and end apart: 17 -> 17, of which waited for: 6 -> 6; matrix products, arithmetic and copies ran while one was open for 0% -> 0% of each run, Pallas kernels for 34% -> 33%
where the time goes in v4:
time: 46.2 us; the launch traced here: 45.6 us
  Pallas kernels  18.7 us (40%)
  starting transfers between devices  15.2 us (33%)
  waiting for transfers between devices  10.8 us (23%)
  between operations  0.79 us (2%)
    pallas_call x14, Pallas kernels, run(): pl.pallas_call(body, in_specs=in_specs, out_specs=out_specs, out_shape=ou...  18.7 us
    ppermute x11, starting transfers between devices, send(): return lax.ppermute(value, ('ctx', 'chan'), moves)  8.04 us
    ppermute x11, waiting for transfers between devices, send(): return lax.ppermute(value, ('ctx', 'chan'), moves)  6.64 us
    ppermute x3, starting transfers between devices, sum_over_chips(): lax.ppermute(rows, 'ctx', [(i, i ^ step) for i in range(count)])  4.45 us
    ppermute x2, starting transfers between devices, gather_over_chan(): other = lax.ppermute(rows, ('ctx', 'chan'), crossed(bit))  2.63 us
    ppermute x2, waiting for transfers between devices, gather_over_chan(): other = lax.ppermute(rows, ('ctx', 'chan'), crossed(bit))  2.08 us
    ppermute x3, waiting for transfers between devices, sum_over_chips(): lax.ppermute(rows, 'ctx', [(i, i ^ step) for i in range(count)])  1.37 us
  transfers between devices with their start and end apart: 17, of which 6 were waited for; matrix products, arithmetic and copies ran while one was open for 0% of the time, Pallas kernels for 33%

profile of v4, /device:TPU:0, one launch (start us, length us, event | category | flops | bytes accessed | tf_op | source)
XLA Modules:
  0.0 45.6 jit_solution(14883743594985618555)
XLA Ops:
  0.7 1.7 %q_stream.1 = (bf16[256,1024]{1,0:T(8,128)(2,1)S(1)}, bf16[256,1024]{1,0:T(8,128)(2,1)S(1)}) custom-call(bf16[256,2048]{1,0:T(8,128)(2,1)} %key_ref.1, bf16[256,2048]{1,0:T(8,128)(2,1)} %v_ref.2, bf16[256,2048]{1,0:T(8,128)(2,1)} %query_ref.1, bf16[256,2048]{1,0:T(8,128)(2,1)} %g_ref.2), custom_call_target="tpu_custom_call" | custom-call | flops 1 | bytes 5242880 | tf_op jit(solution)/shard_map/q_stream/pallas_call | solution.py:30
  2.4 3.0 %collective-permute-start = (bf16[256,1024]{1,0:T(8,128)(2,1)S(1)}, bf16[256,1024]{1,0:T(8,128)(2,1)S(1)}, u32[]{:S(2)}, u32[]{:S(2)}) collective-permute-start(bf16[256,1024]{1,0:T(8,128)(2,1)S(1)} %get-tuple-element.53.q1), channel_id=1, source_target_pairs={{0,1},{1,0},{2,3},{3,2},{4,8},{5,9},{6,10},{7,11},{8,4},{9,5},{10,... | collective-permute-start | bytes 1572872 | tf_op jit(solution)/shard_map/ppermute | solution.py:551
  5.4 0.1 collective-permute-start.1
  5.4 0.1 copy.16
  5.5 0.1 reshape.11.lag_ref.refs_0_
  5.6 3.7 %toeplitz.1.t_ref.refs_1_ = bf16[2,4,3,256,256]{4,3,2,1,0:T(8,128)(2,1)S(1)} custom-call(s32[32]{0:T(128)S(1)} %reshape.11.lag_ref.refs_0_, bf16[16,2,512]{2,1,0:T(2,128)(2,1)S(1)} %copy-done, bf16[16,256]{1,0:T(8,128)(2,1)S(1)} %copy-done.1), custom_call_target="tpu_custom_call" | custom-call | flops 1 | bytes 3186816 | tf_op jit(solution)/shard_map/toeplitz/pallas_call | solution.py:30
  9.3 1.7 %p_stream.1 = (bf16[256,1024]{1,0:T(8,128)(2,1)S(1)}, bf16[256,1024]{1,0:T(8,128)(2,1)S(1)}) custom-call(bf16[256,2048]{1,0:T(8,128)(2,1)} %key_ref.1, bf16[256,2048]{1,0:T(8,128)(2,1)} %v_ref.2, bf16[256,2048]{1,0:T(8,128)(2,1)} %query_ref.1, bf16[256,2048]{1,0:T(8,128)(2,1)} %g_ref.2), custom_call_target="tpu_custom_call" | custom-call | flops 1 | bytes 5242880 | tf_op jit(solution)/shard_map/p_stream/pallas_call | solution.py:30
  11.0 1.0 %correlate_near.1.near_ref = f32[2,2,512]{2,1,0:T(2,128)S(1)} custom-call(bf16[256,1024]{1,0:T(8,128)(2,1)S(1)} %get-tuple-element.76.p0, bf16[256,1024]{1,0:T(8,128)(2,1)S(1)} %get-tuple-element.61.p1, bf16[256,1024]{1,0:T(8,128)(2,1)S(1)} %get-tuple-element.43.q0.q_ref, bf16[256,1024]{1,0:T(8,128)(2,1)S(1)} %get-tuple-element.53.q1), custom_call_target="tpu_custom_call" | custom-call | flops 1 | bytes 2105344 | tf_op jit(solution)/shard_map/correlate_near/pallas_call | solution.py:30
  12.0 2.1 %near_sums.1 = (f32[2,2,256,1024]{3,2,1,0:T(8,128)S(1)}, bf16[256,2048]{1,0:T(8,128)(2,1)S(1)}, bf16[256,2048]{1,0:T(8,128)(2,1)S(1)}) custom-call(bf16[2,4,3,256,256]{4,3,2,1,0:T(8,128)(2,1)S(1)} %toeplitz.1.t_ref.refs_1_, bf16[256,1024]{1,0:T(8,128)(2,1)S(1)} %get-tuple-element.76.p0, bf16[256,1024]{1,0:T(8,128)(2,1)S(1)} %get-tuple-element.61.p1, ...), custom_call_target="tpu_custom_call" | custom-call | flops 1 | bytes 13631488 | tf_op jit(solution)/shard_map/near_sums/pallas_call | solution.py:30
  14.2 1.4 %collective-permute-start.2 = (bf16[256,1024]{1,0:T(8,128)(2,1)S(1)}, bf16[256,1024]{1,0:T(8,128)(2,1)S(1)}, u32[]{:S(2)}, u32[]{:S(2)}) collective-permute-start(bf16[256,1024]{1,0:T(8,128)(2,1)S(1)} %get-tuple-element.61.p1), channel_id=1, source_target_pairs={{0,12},{1,13},{2,14},{3,15},{4,5},{5,4},{6,7},{7,6},{8,20},{9,21},... | collective-permute-start | bytes 1572872 | tf_op jit(solution)/shard_map/ppermute | solution.py:551
  15.6 3.6 %collective-permute-done.1.refs_1_.r11 = bf16[256,1024]{1,0:T(8,128)(2,1)S(1)} collective-permute-done((bf16[256,1024]{1,0:T(8,128)(2,1)S(1)}, bf16[256,1024]{1,0:T(8,128)(2,1)S(1)}, u32[]{:S(2)}, u32[]{:S(2)}) %collective-permute-start.1) | collective-permute-done | bytes 524320 | tf_op jit(solution)/shard_map/ppermute | solution.py:551
  19.3 0.5 %collective-permute-start.6 = (bf16[256,1024]{1,0:T(8,128)(2,1)S(1)}, bf16[256,1024]{1,0:T(8,128)(2,1)S(1)}, u32[]{:S(2)}, u32[]{:S(2)}) collective-permute-start(bf16[256,1024]{1,0:T(8,128)(2,1)S(1)} %collective-permute-done.refs_0_.r1_ref.r10), channel_id=1, source_target_pairs={{0,4},{1,5},{2,6},{3,7},{4,0},{5,1},{6,2},{7,3},{8,12},{9,13},{10,... | collective-permute-start | bytes 1572872 | tf_op jit(solution)/shard_map/ppermute | solution.py:551
  19.8 1.0 %collective-permute-start.3 = (bf16[256,1024]{1,0:T(8,128)(2,1)S(1)}, bf16[256,1024]{1,0:T(8,128)(2,1)S(1)}, u32[]{:S(2)}, u32[]{:S(2)}) collective-permute-start(bf16[256,1024]{1,0:T(8,128)(2,1)S(1)} %get-tuple-element.76.p0), channel_id=1, source_target_pairs={{0,12},{1,13},{2,14},{3,15},{4,5},{5,4},{6,7},{7,6},{8,20},{9,21},... | collective-permute-start | bytes 1572872 | tf_op jit(solution)/shard_map/ppermute | solution.py:551
  20.9 3.0 %collective-permute-done.2.r2_ref.refs_5_ = bf16[256,1024]{1,0:T(8,128)(2,1)S(1)} collective-permute-done((bf16[256,1024]{1,0:T(8,128)(2,1)S(1)}, bf16[256,1024]{1,0:T(8,128)(2,1)S(1)}, u32[]{:S(2)}, u32[]{:S(2)}) %collective-permute-start.2) | collective-permute-done | bytes 524320 | tf_op jit(solution)/shard_map/ppermute | solution.py:551
  23.9 2.0 %correlate_far.1.refs_3_ = f32[4,3,512]{2,1,0:T(4,128)S(1)} custom-call(s32[32]{0:T(128)S(1)} %reshape.11.lag_ref.refs_0_, f32[2,2,512]{2,1,0:T(2,128)S(1)} %correlate_near.1.near_ref, bf16[256,1024]{1,0:T(8,128)(2,1)S(1)} %get-tuple-element.76.p0, bf16[256,1024]{1,0:T(8,128)(2,1)S(1)} %get-tuple-element.61.p1, ...), custom_call_target="tpu_custom_call" | custom-call | flops 1 | bytes 4227200 | tf_op jit(solution)/shard_map/correlate_far/pallas_call | solution.py:30
  25.9 3.4 %collective-permute-start.9 = (f32[4,3,512]{2,1,0:T(4,128)S(1)}, f32[4,3,512]{2,1,0:T(4,128)S(1)}, u32[]{:S(2)}, u32[]{:S(2)}) collective-permute-start(f32[4,3,512]{2,1,0:T(4,128)S(1)} %correlate_far.1.refs_3_), channel_id=1, source_target_pairs={{0,24},{4,28},{8,16},{12,20},{16,8},{20,12},{24,0},{28,4},{1,25},{... | collective-permute-start | bytes 73736 | tf_op jit(solution)/shard_map/ppermute | solution.py:450
  29.3 1.1 %collective-permute-start.7 = (f32[4,3,512]{2,1,0:T(4,128)S(1)}, f32[4,3,512]{2,1,0:T(4,128)S(1)}, u32[]{:S(2)}, u32[]{:S(2)}) collective-permute-start(f32[4,3,512]{2,1,0:T(4,128)S(1)} %correlate_far.1.refs_3_), channel_id=1, source_target_pairs={{0,8},{4,12},{8,0},{12,4},{16,24},{20,28},{24,16},{28,20},{1,9},{5... | collective-permute-start | bytes 73736 | tf_op jit(solution)/shard_map/ppermute | solution.py:450
  30.3 1.0 %collective-permute-start.13 = (bf16[2,256,1024]{2,1,0:T(8,128)(2,1)S(1)}, bf16[2,256,1024]{2,1,0:T(8,128)(2,1)S(1)}, u32[]{:S(2)}, u32[]{:S(2)}) collective-permute-start(bf16[2,256,1024]{2,1,0:T(8,128)(2,1)S(1)} %stack.1), channel_id=1, source_target_pairs={{0,8},{1,9},{2,10},{3,11},{4,0},{5,1},{6,2},{7,3},{8,16},{9,17},{1... | collective-permute-start | bytes 3145736 | tf_op jit(solution)/shard_map/ppermute | solution.py:551
  31.3 1.7 %out_q0.1 = (bf16[256,2048]{1,0:T(8,128)(2,1)}, bf16[256,2048]{1,0:T(8,128)(2,1)}) custom-call(s32[32]{0:T(128)S(1)} %reshape.11.lag_ref.refs_0_, bf16[2,4,3,256,256]{4,3,2,1,0:T(8,128)(2,1)S(1)} %toeplitz.1.t_ref.refs_1_, f32[2,2,256,1024]{3,2,1,0:T(8,128)S(1)} %get-tuple-element.63.refs_2_.sums_ref, ...), custom_call_target="tpu_custom_call" | custom-call | flops 1 | bytes 12058752 | tf_op jit(solution)/shard_map/out_q0/pallas_call | solution.py:30
  33.1 1.4 %collective-permute-done.8.refs_1_ = f32[4,3,512]{2,1,0:T(4,128)S(1)} collective-permute-done((f32[4,3,512]{2,1,0:T(4,128)S(1)}, f32[4,3,512]{2,1,0:T(4,128)S(1)}, u32[]{:S(2)}, u32[]{:S(2)}) %collective-permute-start.8) | collective-permute-done | bytes 24608 | tf_op jit(solution)/shard_map/ppermute | solution.py:450
  34.4 0.1 collective-permute-start.10
  34.5 0.5 %collective-permute-start.15 = (bf16[256,1024]{1,0:T(8,128)(2,1)S(1)}, bf16[256,1024]{1,0:T(8,128)(2,1)S(1)}, u32[]{:S(2)}, u32[]{:S(2)}) collective-permute-start(bf16[256,1024]{1,0:T(8,128)(2,1)S(1)} %get-tuple-element.76.p0), channel_id=1, source_target_pairs={{0,4},{1,5},{2,6},{3,7},{4,0},{5,1},{6,2},{7,3},{8,12},{9,13},{10,... | collective-permute-start | bytes 1572872 | tf_op jit(solution)/shard_map/ppermute | solution.py:551
  35.0 0.7 %collective-permute-done.10.refs_1_ = f32[4,3,512]{2,1,0:T(4,128)S(1)} collective-permute-done((f32[4,3,512]{2,1,0:T(4,128)S(1)}, f32[4,3,512]{2,1,0:T(4,128)S(1)}, u32[]{:S(2)}, u32[]{:S(2)}) %collective-permute-start.10) | collective-permute-done | bytes 24608 | tf_op jit(solution)/shard_map/ppermute | solution.py:462
  35.7 0.2 collective-permute-start.11
  35.9 0.3 collective-permute-start.12
  36.2 1.3 %collective-permute-start.14 = (f32[4,3,512]{2,1,0:T(4,128)S(1)}, f32[4,3,512]{2,1,0:T(4,128)S(1)}, u32[]{:S(2)}, u32[]{:S(2)}) collective-permute-start(f32[4,3,512]{2,1,0:T(4,128)S(1)} %add_rows.3.first_ref), channel_id=1, source_target_pairs={{0,5},{1,4},{2,7},{3,6},{4,1},{5,0},{6,3},{7,2},{8,13},{9,12},{10,... | collective-permute-start | bytes 73736 | tf_op jit(solution)/shard_map/ppermute | solution.py:490
  37.5 1.7 %out_q1.1 = (bf16[256,2048]{1,0:T(8,128)(2,1)}, bf16[256,2048]{1,0:T(8,128)(2,1)}) custom-call(s32[32]{0:T(128)S(1)} %reshape.11.lag_ref.refs_0_, bf16[2,4,3,256,256]{4,3,2,1,0:T(8,128)(2,1)S(1)} %toeplitz.1.t_ref.refs_1_, f32[2,2,256,1024]{3,2,1,0:T(8,128)S(1)} %get-tuple-element.63.refs_2_.sums_ref, ...), custom_call_target="tpu_custom_call", output_to_operand_aliasing={{0}: (7, {}), {1}: (8, {})} | custom-call | flops 1 | bytes 14155904 | tf_op jit(solution)/shard_map/out_q1/pallas_call | solution.py:30
  39.3 0.3 collective-permute-done.14.second_ref
  39.6 1.4 %collective-permute-start.16 = (f32[8,3,512]{2,1,0:T(4,128)S(1)}, f32[8,3,512]{2,1,0:T(4,128)S(1)}, u32[]{:S(2)}, u32[]{:S(2)}) collective-permute-start(f32[8,3,512]{2,1,0:T(4,128)S(1)} %join_rows.1.refs_5_), channel_id=1, source_target_pairs={{0,6},{1,7},{2,4},{3,5},{4,2},{5,3},{6,0},{7,1},{8,14},{9,15},{10,... | collective-permute-start | bytes 147464 | tf_op jit(solution)/shard_map/ppermute | solution.py:490
  41.0 1.1 %partial_sums.1.refs_2_ = f32[2,256,1024]{2,1,0:T(8,128)S(1)} custom-call(s32[32]{0:T(128)S(1)} %reshape.11.lag_ref.refs_0_, bf16[2,4,3,256,256]{4,3,2,1,0:T(8,128)(2,1)S(1)} %toeplitz.1.t_ref.refs_1_, f32[2,2,256,1024]{3,2,1,0:T(8,128)S(1)} %get-tuple-element.63.refs_2_.sums_ref, bf16[256,1024]{1,0:T(8,128)(2,1)S(1)} %collective-permute-done.refs_0_.r1_ref.r10, ...), custom_call_target="tpu_custom_call" | custom-call | flops 5200000000 | bytes 11534464 | tf_op jit(solution)/shard_map/partial_sums/pallas_call | solution.py:30
  42.0 1.8 %collective-permute-done.16.refs_6_ = f32[8,3,512]{2,1,0:T(4,128)S(1)} collective-permute-done((f32[8,3,512]{2,1,0:T(4,128)S(1)}, f32[8,3,512]{2,1,0:T(4,128)S(1)}, u32[]{:S(2)}, u32[]{:S(2)}) %collective-permute-start.16) | collective-permute-done | bytes 49184 | tf_op jit(solution)/shard_map/ppermute | solution.py:490
  43.8 1.8 %out_p01.1 = (bf16[256,2048]{1,0:T(8,128)(2,1)}, bf16[256,2048]{1,0:T(8,128)(2,1)}, f32[16,2,512]{2,1,0:T(2,128)}, f32[16,256]{1,0:T(8,128)}) custom-call(s32[32]{0:T(128)S(1)} %reshape.11.lag_ref.refs_0_, bf16[2,4,3,256,256]{4,3,2,1,0:T(8,128)(2,1)S(1)} %toeplitz.1.t_ref.refs_1_, ...), custom_call_target="tpu_custom_call", output_to_operand_aliasing={{0}: (7, {}), {1}: (8, {})} | custom-call | flops 1 | bytes 11714688 | tf_op jit(solution)/shard_map/out_p01/pallas_call | solution.py:30
  (24 shorter events, 0.2 us)
Async XLA Ops:
  0.6 4.8 %copy-start.2 = (s32[16,2]{0,1:T(2,128)S(1)}, s32[16,2]{0,1:T(2,128)}, u32[]{:S(2)}) copy-start(s32[16,2]{0,1:T(2,128)} %param.13) | copy-start | bytes 388
  0.6 5.0 %copy-start.1 = (bf16[16,256]{1,0:T(8,128)(2,1)S(1)}, bf16[16,256]{1,0:T(8,128)(2,1)}, u32[]{:S(2)}) copy-start(bf16[16,256]{1,0:T(8,128)(2,1)} %near_ref) | copy-start | bytes 24580
  0.7 5.0 %copy-start = (bf16[16,2,512]{2,1,0:T(2,128)(2,1)S(1)}, bf16[16,2,512]{2,1,0:T(2,128)(2,1)}, u32[]{:S(2)}) copy-start(bf16[16,2,512]{2,1,0:T(2,128)(2,1)} %far_ref) | copy-start | bytes 98308
  2.4 13.3 %collective-permute-start = (bf16[256,1024]{1,0:T(8,128)(2,1)S(1)}, bf16[256,1024]{1,0:T(8,128)(2,1)S(1)}, u32[]{:S(2)}, u32[]{:S(2)}) collective-permute-start(bf16[256,1024]{1,0:T(8,128)(2,1)S(1)} %get-tuple-element.53.q1), channel_id=1, source_target_pairs={{0,1},{1,0},{2,3},{3,2},{4,8},{5,9},{6,10},{7,11},{8,4},{9,5},{10,... | collective-permute-start | bytes 1572872 | tf_op jit(solution)/shard_map/ppermute | solution.py:551
  5.4 13.9 %collective-permute-start.1 = (bf16[256,1024]{1,0:T(8,128)(2,1)S(1)}, bf16[256,1024]{1,0:T(8,128)(2,1)S(1)}, u32[]{:S(2)}, u32[]{:S(2)}) collective-permute-start(bf16[256,1024]{1,0:T(8,128)(2,1)S(1)} %get-tuple-element.43.q0.q_ref), channel_id=1, source_target_pairs={{0,1},{1,0},{2,3},{3,2},{4,8},{5,9},{6,10},{7,11},{8,4},{9,5},{10,... | collective-permute-start | bytes 1572872 | tf_op jit(solution)/shard_map/ppermute | solution.py:551
  14.2 9.7 %collective-permute-start.2 = (bf16[256,1024]{1,0:T(8,128)(2,1)S(1)}, bf16[256,1024]{1,0:T(8,128)(2,1)S(1)}, u32[]{:S(2)}, u32[]{:S(2)}) collective-permute-start(bf16[256,1024]{1,0:T(8,128)(2,1)S(1)} %get-tuple-element.61.p1), channel_id=1, source_target_pairs={{0,12},{1,13},{2,14},{3,15},{4,5},{5,4},{6,7},{7,6},{8,20},{9,21},... | collective-permute-start | bytes 1572872 | tf_op jit(solution)/shard_map/ppermute | solution.py:551
  19.3 4.6 %collective-permute-start.4 = (bf16[256,1024]{1,0:T(8,128)(2,1)S(1)}, bf16[256,1024]{1,0:T(8,128)(2,1)S(1)}, u32[]{:S(2)}, u32[]{:S(2)}) collective-permute-start(bf16[256,1024]{1,0:T(8,128)(2,1)S(1)} %get-tuple-element.61.p1), channel_id=1, source_target_pairs={{0,4},{1,5},{2,6},{3,7},{4,0},{5,1},{6,2},{7,3},{8,12},{9,13},{10,... | collective-permute-start | bytes 1572872 | tf_op jit(solution)/shard_map/ppermute | solution.py:551
  19.3 4.6 %collective-permute-start.6 = (bf16[256,1024]{1,0:T(8,128)(2,1)S(1)}, bf16[256,1024]{1,0:T(8,128)(2,1)S(1)}, u32[]{:S(2)}, u32[]{:S(2)}) collective-permute-start(bf16[256,1024]{1,0:T(8,128)(2,1)S(1)} %collective-permute-done.refs_0_.r1_ref.r10), channel_id=1, source_target_pairs={{0,4},{1,5},{2,6},{3,7},{4,0},{5,1},{6,2},{7,3},{8,12},{9,13},{10,... | collective-permute-start | bytes 1572872 | tf_op jit(solution)/shard_map/ppermute | solution.py:551
  19.8 4.1 %collective-permute-start.5 = (bf16[256,1024]{1,0:T(8,128)(2,1)S(1)}, bf16[256,1024]{1,0:T(8,128)(2,1)S(1)}, u32[]{:S(2)}, u32[]{:S(2)}) collective-permute-start(bf16[256,1024]{1,0:T(8,128)(2,1)S(1)} %collective-permute-done.1.refs_1_.r11), channel_id=1, source_target_pairs={{0,4},{1,5},{2,6},{3,7},{4,0},{5,1},{6,2},{7,3},{8,12},{9,13},{10,... | collective-permute-start | bytes 1572872 | tf_op jit(solution)/shard_map/ppermute | solution.py:551
  19.8 11.5 %collective-permute-start.3 = (bf16[256,1024]{1,0:T(8,128)(2,1)S(1)}, bf16[256,1024]{1,0:T(8,128)(2,1)S(1)}, u32[]{:S(2)}, u32[]{:S(2)}) collective-permute-start(bf16[256,1024]{1,0:T(8,128)(2,1)S(1)} %get-tuple-element.76.p0), channel_id=1, source_target_pairs={{0,12},{1,13},{2,14},{3,15},{4,5},{5,4},{6,7},{7,6},{8,20},{9,21},... | collective-permute-start | bytes 1572872 | tf_op jit(solution)/shard_map/ppermute | solution.py:551
  25.9 7.2 %collective-permute-start.9 = (f32[4,3,512]{2,1,0:T(4,128)S(1)}, f32[4,3,512]{2,1,0:T(4,128)S(1)}, u32[]{:S(2)}, u32[]{:S(2)}) collective-permute-start(f32[4,3,512]{2,1,0:T(4,128)S(1)} %correlate_far.1.refs_3_), channel_id=1, source_target_pairs={{0,24},{4,28},{8,16},{12,20},{16,8},{20,12},{24,0},{28,4},{1,25},{... | collective-permute-start | bytes 73736 | tf_op jit(solution)/shard_map/ppermute | solution.py:450
  29.3 5.2 %collective-permute-start.8 = (f32[4,3,512]{2,1,0:T(4,128)S(1)}, f32[4,3,512]{2,1,0:T(4,128)S(1)}, u32[]{:S(2)}, u32[]{:S(2)}) collective-permute-start(f32[4,3,512]{2,1,0:T(4,128)S(1)} %correlate_far.1.refs_3_), channel_id=1, source_target_pairs={{0,16},{4,20},{8,24},{12,28},{16,0},{20,4},{24,8},{28,12},{1,17},{... | collective-permute-start | bytes 73736 | tf_op jit(solution)/shard_map/ppermute | solution.py:450
  29.3 5.2 %collective-permute-start.7 = (f32[4,3,512]{2,1,0:T(4,128)S(1)}, f32[4,3,512]{2,1,0:T(4,128)S(1)}, u32[]{:S(2)}, u32[]{:S(2)}) collective-permute-start(f32[4,3,512]{2,1,0:T(4,128)S(1)} %correlate_far.1.refs_3_), channel_id=1, source_target_pairs={{0,8},{4,12},{8,0},{12,4},{16,24},{20,28},{24,16},{28,20},{1,9},{5... | collective-permute-start | bytes 73736 | tf_op jit(solution)/shard_map/ppermute | solution.py:450
  30.3 13.5 %collective-permute-start.13 = (bf16[2,256,1024]{2,1,0:T(8,128)(2,1)S(1)}, bf16[2,256,1024]{2,1,0:T(8,128)(2,1)S(1)}, u32[]{:S(2)}, u32[]{:S(2)}) collective-permute-start(bf16[2,256,1024]{2,1,0:T(8,128)(2,1)S(1)} %stack.1), channel_id=1, source_target_pairs={{0,8},{1,9},{2,10},{3,11},{4,0},{5,1},{6,2},{7,3},{8,16},{9,17},{1... | collective-permute-start | bytes 3145736 | tf_op jit(solution)/shard_map/ppermute | solution.py:551
  34.4 1.3 %collective-permute-start.10 = (f32[4,3,512]{2,1,0:T(4,128)S(1)}, f32[4,3,512]{2,1,0:T(4,128)S(1)}, u32[]{:S(2)}, u32[]{:S(2)}) collective-permute-start(f32[4,3,512]{2,1,0:T(4,128)S(1)} %add_rows.2.refs_0_), channel_id=1, source_target_pairs={{0,4},{4,0},{8,12},{12,8},{16,20},{20,16},{24,28},{28,24},{1,5},{5... | collective-permute-start | bytes 73736 | tf_op jit(solution)/shard_map/ppermute | solution.py:462
  34.5 3.0 %collective-permute-start.15 = (bf16[256,1024]{1,0:T(8,128)(2,1)S(1)}, bf16[256,1024]{1,0:T(8,128)(2,1)S(1)}, u32[]{:S(2)}, u32[]{:S(2)}) collective-permute-start(bf16[256,1024]{1,0:T(8,128)(2,1)S(1)} %get-tuple-element.76.p0), channel_id=1, source_target_pairs={{0,4},{1,5},{2,6},{3,7},{4,0},{5,1},{6,2},{7,3},{8,12},{9,13},{10,... | collective-permute-start | bytes 1572872 | tf_op jit(solution)/shard_map/ppermute | solution.py:551
  35.7 5.2 %collective-permute-start.11 = (bf16[256,1024]{1,0:T(8,128)(2,1)S(1)}, bf16[256,1024]{1,0:T(8,128)(2,1)S(1)}, u32[]{:S(2)}, u32[]{:S(2)}) collective-permute-start(bf16[256,1024]{1,0:T(8,128)(2,1)S(1)} %collective-permute-done.3.refs_5_), channel_id=1, source_target_pairs={{0,4},{1,5},{2,6},{3,7},{4,0},{5,1},{6,2},{7,3},{8,12},{9,13},{10,... | collective-permute-start | bytes 1572872 | tf_op jit(solution)/shard_map/ppermute | solution.py:551
  35.9 5.1 %collective-permute-start.12 = (bf16[256,1024]{1,0:T(8,128)(2,1)S(1)}, bf16[256,1024]{1,0:T(8,128)(2,1)S(1)}, u32[]{:S(2)}, u32[]{:S(2)}) collective-permute-start(bf16[256,1024]{1,0:T(8,128)(2,1)S(1)} %collective-permute-done.2.r2_ref.refs_5_), channel_id=1, source_target_pairs={{0,4},{1,5},{2,6},{3,7},{4,0},{5,1},{6,2},{7,3},{8,12},{9,13},{10,... | collective-permute-start | bytes 1572872 | tf_op jit(solution)/shard_map/ppermute | solution.py:551
  36.2 3.3 %collective-permute-start.14 = (f32[4,3,512]{2,1,0:T(4,128)S(1)}, f32[4,3,512]{2,1,0:T(4,128)S(1)}, u32[]{:S(2)}, u32[]{:S(2)}) collective-permute-start(f32[4,3,512]{2,1,0:T(4,128)S(1)} %add_rows.3.first_ref), channel_id=1, source_target_pairs={{0,5},{1,4},{2,7},{3,6},{4,1},{5,0},{6,3},{7,2},{8,13},{9,12},{10,... | collective-permute-start | bytes 73736 | tf_op jit(solution)/shard_map/ppermute | solution.py:490
  39.6 4.2 %collective-permute-start.16 = (f32[8,3,512]{2,1,0:T(4,128)S(1)}, f32[8,3,512]{2,1,0:T(4,128)S(1)}, u32[]{:S(2)}, u32[]{:S(2)}) collective-permute-start(f32[8,3,512]{2,1,0:T(4,128)S(1)} %join_rows.1.refs_5_), channel_id=1, source_target_pairs={{0,6},{1,7},{2,4},{3,5},{4,2},{5,3},{6,0},{7,1},{8,14},{9,15},{10,... | collective-permute-start | bytes 147464 | tf_op jit(solution)/shard_map/ppermute | solution.py:490

commit v5 on v4

--- a/solution.py
+++ b/solution.py
@@ -214,12 +214,38 @@
     )(*p_own, *q_own)
 
 
-def correlate_far(lags, slots, near, p_own, q_own, r1, x0, x1, r2):
+def correlate_first(lags, slots, q_own, r1):
+    span, hw = r1.shape
+    bw = min(GSIZE, hw)
+    nb = hw // bw
+
+    def body(lag_ref, q_ref, r1_ref, out_ref):
+        core = core_of()
+
+        def run(pair):
+            for b in range(nb):
+                at = pl.ds(b * bw, bw)
+                is_one = short_lag(lag_ref, block_group(core, b, 2 * hw, bw), slots) == 1
+                used = jnp.logical_and(is_one, valid("P", 1))
+                out_ref[b] = pair(kept(r1_ref[:, at], used), q_ref[:, at])
+
+        by_core(run)
+
+    return call(
+        body,
+        "correlate_first",
+        jax.ShapeDtypeStruct((nb, span, span), F32),
+        [SMEM] + [VMEM] * 2,
+        VMEM,
+    )(lags, q_own, r1)
+
+
+def correlate_far(lags, slots, near, first, p_own, r1, x0, x1, r2):
     span, hw = r2.shape
     bw = min(GSIZE, hw)
     nb = hw // bw
 
-    def body(lag_ref, near_ref, p0, p1, q_ref, r1_ref, x0_ref, x10, x11, r2_ref, out_ref):
+    def body(lag_ref, near_ref, first_ref, p0, p1, r1_ref, x0_ref, x10, x11, r2_ref, out_ref):
         core = core_of()
 
         def run(pair):
@@ -227,8 +253,7 @@
                 at = pl.ds(b * bw, bw)
                 p, x, r = p0[:, at], kept(x10[:, at], valid("Q", 2)), kept(r1_ref[:, at], valid("P", 1))
                 is_one = short_lag(lag_ref, block_group(core, b, 2 * hw, bw), slots) == 1
-                short = pair(jnp.where(is_one, r, p), jnp.where(is_one, q_ref[:, at], x))
-                short += pair(p, jnp.where(is_one, x0_ref[:, at], jnp.zeros_like(p)))
+                short = first_ref[b] + pair(p, jnp.where(is_one, x0_ref[:, at], x))
                 last = pair(r, x) + pair(p, kept(r2_ref[:, at], valid("Q", 3)))
                 other = pair(p1[:, at], kept(x11[:, at], valid("Q", 2)))
                 rows = [diagonal_sums(matrix, span) for matrix in (short, last, other)]
@@ -255,7 +280,7 @@
         jax.ShapeDtypeStruct((2 * nb, slots + 1, 2 * span), F32),
         [SMEM] + [VMEM] * 9,
         VMEM,
-    )(lags, near, *p_own, q_own[0], r1, x0, *x1, r2)
+    )(lags, near, first, *p_own, r1, x0, *x1, r2)
 
 
 def near_sums(toeplitz, p_own, q_own, key, query):
@@ -571,8 +596,9 @@
     x1 = (send(r1[1], swap), send(r1[0], swap))
     x0a = send(after(pa, r1), swap)
     r2b = send(after(pb, r1), to_far)
-    both, r1 = lax.optimization_barrier((stacked(r1), r1))
-    rows = correlate_far(lags, slots, near, p_own, q_own, r1[0], x0a, x1, r2a)
+    first = correlate_first(lags, slots, q_own[0], r1[0])
+    both, first, r1 = lax.optimization_barrier((stacked(r1), first, r1))
+    rows = correlate_far(lags, slots, near, first, p_own, r1[0], x0a, x1, r2a)
     r3 = send(after(both, rows), onward)
     q_sums, pb_late, r2b, _ = lax.optimization_barrier((sums, pb, r2b, rows))
     results = q_output(0, lags, slots, toeplitz, q_sums, x0a, x1[0], r2a, q_gate, ())

time: 46.2 us -> 46.2 us (level)
  waiting for transfers between devices: 10.8 us -> 9.88 us
  Pallas kernels: 18.7 us -> 19.4 us
    ppermute x11, waiting for transfers between devices: 6.64 us -> 5.74 us  [send(): return lax.ppermute(value, ('ctx', 'chan'), moves)]
    pallas_call x14 -> x15, Pallas kernels: 18.7 us -> 19.4 us  [run(): pl.pallas_call(body, in_specs=in_specs, out_specs=out_specs, out_shape=ou...]
  transfers between devices with their start and end apart: 17 -> 17, of which waited for: 6 -> 6; matrix products, arithmetic and copies ran while one was open for 0% -> 0% of each run, Pallas kernels for 33% -> 35%
where the time goes in v5:
time: 46.2 us; the launch traced here: 45.5 us
  Pallas kernels  19.4 us (42%)
  starting transfers between devices  15.2 us (33%)
  waiting for transfers between devices  9.88 us (21%)
  between operations  0.8 us (2%)
    pallas_call x15, Pallas kernels, run(): pl.pallas_call(body, in_specs=in_specs, out_specs=out_specs, out_shape=ou...  19.4 us
    ppermute x11, starting transfers between devices, send(): return lax.ppermute(value, ('ctx', 'chan'), moves)  8.04 us
    ppermute x11, waiting for transfers between devices, send(): return lax.ppermute(value, ('ctx', 'chan'), moves)  5.74 us
    ppermute x3, starting transfers between devices, sum_over_chips(): lax.ppermute(rows, 'ctx', [(i, i ^ step) for i in range(count)])  4.45 us
    ppermute x2, starting transfers between devices, gather_over_chan(): other = lax.ppermute(rows, ('ctx', 'chan'), crossed(bit))  2.63 us
    ppermute x2, waiting for transfers between devices, gather_over_chan(): other = lax.ppermute(rows, ('ctx', 'chan'), crossed(bit))  2.07 us
    ppermute x3, waiting for transfers between devices, sum_over_chips(): lax.ppermute(rows, 'ctx', [(i, i ^ step) for i in range(count)])  1.37 us
  transfers between devices with their start and end apart: 17, of which 6 were waited for; matrix products, arithmetic and copies ran while one was open for 0% of the time, Pallas kernels for 35%

profile of v5, /device:TPU:0, one launch (start us, length us, event | category | flops | bytes accessed | tf_op | source)
XLA Modules:
  0.0 45.5 jit_solution(2706426373332534415)
XLA Ops:
  0.7 1.7 %q_stream.1 = (bf16[256,1024]{1,0:T(8,128)(2,1)S(1)}, bf16[256,1024]{1,0:T(8,128)(2,1)S(1)}) custom-call(bf16[256,2048]{1,0:T(8,128)(2,1)} %key_ref.1, bf16[256,2048]{1,0:T(8,128)(2,1)} %v_ref.2, bf16[256,2048]{1,0:T(8,128)(2,1)} %query_ref.1, bf16[256,2048]{1,0:T(8,128)(2,1)} %g_ref.2), custom_call_target="tpu_custom_call" | custom-call | flops 1 | bytes 5242880 | tf_op jit(solution)/shard_map/q_stream/pallas_call | solution.py:30
  2.4 3.0 %collective-permute-start = (bf16[256,1024]{1,0:T(8,128)(2,1)S(1)}, bf16[256,1024]{1,0:T(8,128)(2,1)S(1)}, u32[]{:S(2)}, u32[]{:S(2)}) collective-permute-start(bf16[256,1024]{1,0:T(8,128)(2,1)S(1)} %get-tuple-element.54.q1), channel_id=1, source_target_pairs={{0,1},{1,0},{2,3},{3,2},{4,8},{5,9},{6,10},{7,11},{8,4},{9,5},{10,... | collective-permute-start | bytes 1572872 | tf_op jit(solution)/shard_map/ppermute | solution.py:576
  5.4 0.1 collective-permute-start.1
  5.4 0.1 copy.16
  5.5 0.1 reshape.11.lag_ref.refs_0_
  5.6 3.7 %toeplitz.1.t_ref.refs_1_ = bf16[2,4,3,256,256]{4,3,2,1,0:T(8,128)(2,1)S(1)} custom-call(s32[32]{0:T(128)S(1)} %reshape.11.lag_ref.refs_0_, bf16[16,2,512]{2,1,0:T(2,128)(2,1)S(1)} %copy-done, bf16[16,256]{1,0:T(8,128)(2,1)S(1)} %copy-done.1), custom_call_target="tpu_custom_call" | custom-call | flops 1 | bytes 3186816 | tf_op jit(solution)/shard_map/toeplitz/pallas_call | solution.py:30
  9.3 1.7 %p_stream.1 = (bf16[256,1024]{1,0:T(8,128)(2,1)S(1)}, bf16[256,1024]{1,0:T(8,128)(2,1)S(1)}) custom-call(bf16[256,2048]{1,0:T(8,128)(2,1)} %key_ref.1, bf16[256,2048]{1,0:T(8,128)(2,1)} %v_ref.2, bf16[256,2048]{1,0:T(8,128)(2,1)} %query_ref.1, bf16[256,2048]{1,0:T(8,128)(2,1)} %g_ref.2), custom_call_target="tpu_custom_call" | custom-call | flops 1 | bytes 5242880 | tf_op jit(solution)/shard_map/p_stream/pallas_call | solution.py:30
  11.0 1.0 %correlate_near.1.near_ref = f32[2,2,512]{2,1,0:T(2,128)S(1)} custom-call(bf16[256,1024]{1,0:T(8,128)(2,1)S(1)} %get-tuple-element.78.p0, bf16[256,1024]{1,0:T(8,128)(2,1)S(1)} %get-tuple-element.63.p1, bf16[256,1024]{1,0:T(8,128)(2,1)S(1)} %get-tuple-element.44.q0.q_ref, bf16[256,1024]{1,0:T(8,128)(2,1)S(1)} %get-tuple-element.54.q1), custom_call_target="tpu_custom_call" | custom-call | flops 1 | bytes 2105344 | tf_op jit(solution)/shard_map/correlate_near/pallas_call | solution.py:30
  12.0 2.1 %near_sums.1 = (f32[2,2,256,1024]{3,2,1,0:T(8,128)S(1)}, bf16[256,2048]{1,0:T(8,128)(2,1)S(1)}, bf16[256,2048]{1,0:T(8,128)(2,1)S(1)}) custom-call(bf16[2,4,3,256,256]{4,3,2,1,0:T(8,128)(2,1)S(1)} %toeplitz.1.t_ref.refs_1_, bf16[256,1024]{1,0:T(8,128)(2,1)S(1)} %get-tuple-element.78.p0, bf16[256,1024]{1,0:T(8,128)(2,1)S(1)} %get-tuple-element.63.p1, ...), custom_call_target="tpu_custom_call" | custom-call | flops 1 | bytes 13631488 | tf_op jit(solution)/shard_map/near_sums/pallas_call | solution.py:30
  14.2 1.4 %collective-permute-start.2 = (bf16[256,1024]{1,0:T(8,128)(2,1)S(1)}, bf16[256,1024]{1,0:T(8,128)(2,1)S(1)}, u32[]{:S(2)}, u32[]{:S(2)}) collective-permute-start(bf16[256,1024]{1,0:T(8,128)(2,1)S(1)} %get-tuple-element.63.p1), channel_id=1, source_target_pairs={{0,12},{1,13},{2,14},{3,15},{4,5},{5,4},{6,7},{7,6},{8,20},{9,21},... | collective-permute-start | bytes 1572872 | tf_op jit(solution)/shard_map/ppermute | solution.py:576
  15.6 3.6 %collective-permute-done.1.refs_1_.r11 = bf16[256,1024]{1,0:T(8,128)(2,1)S(1)} collective-permute-done((bf16[256,1024]{1,0:T(8,128)(2,1)S(1)}, bf16[256,1024]{1,0:T(8,128)(2,1)S(1)}, u32[]{:S(2)}, u32[]{:S(2)}) %collective-permute-start.1) | collective-permute-done | bytes 524320 | tf_op jit(solution)/shard_map/ppermute | solution.py:576
  19.3 0.5 %collective-permute-start.5 = (bf16[256,1024]{1,0:T(8,128)(2,1)S(1)}, bf16[256,1024]{1,0:T(8,128)(2,1)S(1)}, u32[]{:S(2)}, u32[]{:S(2)}) collective-permute-start(bf16[256,1024]{1,0:T(8,128)(2,1)S(1)} %collective-permute-done.1.refs_1_.r11), channel_id=1, source_target_pairs={{0,4},{1,5},{2,6},{3,7},{4,0},{5,1},{6,2},{7,3},{8,12},{9,13},{10,... | collective-permute-start | bytes 1572872 | tf_op jit(solution)/shard_map/ppermute | solution.py:576
  19.8 1.0 %collective-permute-start.3 = (bf16[256,1024]{1,0:T(8,128)(2,1)S(1)}, bf16[256,1024]{1,0:T(8,128)(2,1)S(1)}, u32[]{:S(2)}, u32[]{:S(2)}) collective-permute-start(bf16[256,1024]{1,0:T(8,128)(2,1)S(1)} %get-tuple-element.78.p0), channel_id=1, source_target_pairs={{0,12},{1,13},{2,14},{3,15},{4,5},{5,4},{6,7},{7,6},{8,20},{9,21},... | collective-permute-start | bytes 1572872 | tf_op jit(solution)/shard_map/ppermute | solution.py:576
  20.8 0.9 %correlate_first.1.first_ref = f32[2,256,256]{2,1,0:T(8,128)S(1)} custom-call(s32[32]{0:T(128)S(1)} %reshape.11.lag_ref.refs_0_, bf16[256,1024]{1,0:T(8,128)(2,1)S(1)} %get-tuple-element.44.q0.q_ref, bf16[256,1024]{1,0:T(8,128)(2,1)S(1)} %collective-permute-done.refs_0_.r1_ref.r10), custom_call_target="tpu_custom_call" | custom-call | flops 1 | bytes 1572992 | tf_op jit(solution)/shard_map/correlate_first/pallas_call | solution.py:30
  21.8 2.1 %collective-permute-done.2.r2_ref.refs_5_ = bf16[256,1024]{1,0:T(8,128)(2,1)S(1)} collective-permute-done((bf16[256,1024]{1,0:T(8,128)(2,1)S(1)}, bf16[256,1024]{1,0:T(8,128)(2,1)S(1)}, u32[]{:S(2)}, u32[]{:S(2)}) %collective-permute-start.2) | collective-permute-done | bytes 524320 | tf_op jit(solution)/shard_map/ppermute | solution.py:576
  23.9 1.9 %correlate_far.1.refs_3_ = f32[4,3,512]{2,1,0:T(4,128)S(1)} custom-call(s32[32]{0:T(128)S(1)} %reshape.11.lag_ref.refs_0_, f32[2,2,512]{2,1,0:T(2,128)S(1)} %correlate_near.1.near_ref, f32[2,256,256]{2,1,0:T(8,128)S(1)} %correlate_first.1.first_ref, bf16[256,1024]{1,0:T(8,128)(2,1)S(1)} %get-tuple-element.78.p0, bf16[256,1024]{1,0:T(8,128)(2,1)S(1)} %get-tuple-element.63.p1, ...), custom_call_target="tpu_custom_call" | custom-call | flops 1 | bytes 4227200 | tf_op jit(solution)/shard_map/correlate_far/pallas_call | solution.py:30
  25.7 3.4 %collective-permute-start.9 = (f32[4,3,512]{2,1,0:T(4,128)S(1)}, f32[4,3,512]{2,1,0:T(4,128)S(1)}, u32[]{:S(2)}, u32[]{:S(2)}) collective-permute-start(f32[4,3,512]{2,1,0:T(4,128)S(1)} %correlate_far.1.refs_3_), channel_id=1, source_target_pairs={{0,24},{4,28},{8,16},{12,20},{16,8},{20,12},{24,0},{28,4},{1,25},{... | collective-permute-start | bytes 73736 | tf_op jit(solution)/shard_map/ppermute | solution.py:475
  29.1 1.1 %collective-permute-start.7 = (f32[4,3,512]{2,1,0:T(4,128)S(1)}, f32[4,3,512]{2,1,0:T(4,128)S(1)}, u32[]{:S(2)}, u32[]{:S(2)}) collective-permute-start(f32[4,3,512]{2,1,0:T(4,128)S(1)} %correlate_far.1.refs_3_), channel_id=1, source_target_pairs={{0,8},{4,12},{8,0},{12,4},{16,24},{20,28},{24,16},{28,20},{1,9},{5... | collective-permute-start | bytes 73736 | tf_op jit(solution)/shard_map/ppermute | solution.py:475
  30.2 1.0 %collective-permute-start.13 = (bf16[2,256,1024]{2,1,0:T(8,128)(2,1)S(1)}, bf16[2,256,1024]{2,1,0:T(8,128)(2,1)S(1)}, u32[]{:S(2)}, u32[]{:S(2)}) collective-permute-start(bf16[2,256,1024]{2,1,0:T(8,128)(2,1)S(1)} %stack.1), channel_id=1, source_target_pairs={{0,8},{1,9},{2,10},{3,11},{4,0},{5,1},{6,2},{7,3},{8,16},{9,17},{1... | collective-permute-start | bytes 3145736 | tf_op jit(solution)/shard_map/ppermute | solution.py:576
  31.2 1.7 %out_q0.1 = (bf16[256,2048]{1,0:T(8,128)(2,1)}, bf16[256,2048]{1,0:T(8,128)(2,1)}) custom-call(s32[32]{0:T(128)S(1)} %reshape.11.lag_ref.refs_0_, bf16[2,4,3,256,256]{4,3,2,1,0:T(8,128)(2,1)S(1)} %toeplitz.1.t_ref.refs_1_, f32[2,2,256,1024]{3,2,1,0:T(8,128)S(1)} %get-tuple-element.65.refs_2_.sums_ref, ...), custom_call_target="tpu_custom_call" | custom-call | flops 1 | bytes 12058752 | tf_op jit(solution)/shard_map/out_q0/pallas_call | solution.py:30
  32.9 1.4 %collective-permute-done.8.refs_1_ = f32[4,3,512]{2,1,0:T(4,128)S(1)} collective-permute-done((f32[4,3,512]{2,1,0:T(4,128)S(1)}, f32[4,3,512]{2,1,0:T(4,128)S(1)}, u32[]{:S(2)}, u32[]{:S(2)}) %collective-permute-start.8) | collective-permute-done | bytes 24608 | tf_op jit(solution)/shard_map/ppermute | solution.py:475
  34.4 0.5 %collective-permute-start.15 = (bf16[256,1024]{1,0:T(8,128)(2,1)S(1)}, bf16[256,1024]{1,0:T(8,128)(2,1)S(1)}, u32[]{:S(2)}, u32[]{:S(2)}) collective-permute-start(bf16[256,1024]{1,0:T(8,128)(2,1)S(1)} %get-tuple-element.78.p0), channel_id=1, source_target_pairs={{0,4},{1,5},{2,6},{3,7},{4,0},{5,1},{6,2},{7,3},{8,12},{9,13},{10,... | collective-permute-start | bytes 1572872 | tf_op jit(solution)/shard_map/ppermute | solution.py:576
  34.9 0.7 %collective-permute-done.10.refs_1_ = f32[4,3,512]{2,1,0:T(4,128)S(1)} collective-permute-done((f32[4,3,512]{2,1,0:T(4,128)S(1)}, f32[4,3,512]{2,1,0:T(4,128)S(1)}, u32[]{:S(2)}, u32[]{:S(2)}) %collective-permute-start.10) | collective-permute-done | bytes 24608 | tf_op jit(solution)/shard_map/ppermute | solution.py:487
  35.6 0.2 collective-permute-start.11
  35.8 0.3 collective-permute-start.12
  36.1 1.3 %collective-permute-start.14 = (f32[4,3,512]{2,1,0:T(4,128)S(1)}, f32[4,3,512]{2,1,0:T(4,128)S(1)}, u32[]{:S(2)}, u32[]{:S(2)}) collective-permute-start(f32[4,3,512]{2,1,0:T(4,128)S(1)} %add_rows.3.first_ref), channel_id=1, source_target_pairs={{0,5},{1,4},{2,7},{3,6},{4,1},{5,0},{6,3},{7,2},{8,13},{9,12},{10,... | collective-permute-start | bytes 73736 | tf_op jit(solution)/shard_map/ppermute | solution.py:515
  37.4 1.8 %out_q1.1 = (bf16[256,2048]{1,0:T(8,128)(2,1)}, bf16[256,2048]{1,0:T(8,128)(2,1)}) custom-call(s32[32]{0:T(128)S(1)} %reshape.11.lag_ref.refs_0_, bf16[2,4,3,256,256]{4,3,2,1,0:T(8,128)(2,1)S(1)} %toeplitz.1.t_ref.refs_1_, f32[2,2,256,1024]{3,2,1,0:T(8,128)S(1)} %get-tuple-element.65.refs_2_.sums_ref, ...), custom_call_target="tpu_custom_call", output_to_operand_aliasing={{0}: (7, {}), {1}: (8, {})} | custom-call | flops 1 | bytes 14155904 | tf_op jit(solution)/shard_map/out_q1/pallas_call | solution.py:30
  39.1 0.3 collective-permute-done.14.second_ref
  39.5 1.4 %collective-permute-start.16 = (f32[8,3,512]{2,1,0:T(4,128)S(1)}, f32[8,3,512]{2,1,0:T(4,128)S(1)}, u32[]{:S(2)}, u32[]{:S(2)}) collective-permute-start(f32[8,3,512]{2,1,0:T(4,128)S(1)} %join_rows.1.refs_5_), channel_id=1, source_target_pairs={{0,6},{1,7},{2,4},{3,5},{4,2},{5,3},{6,0},{7,1},{8,14},{9,15},{10,... | collective-permute-start | bytes 147464 | tf_op jit(solution)/shard_map/ppermute | solution.py:515
  40.8 1.1 %partial_sums.1.refs_2_ = f32[2,256,1024]{2,1,0:T(8,128)S(1)} custom-call(s32[32]{0:T(128)S(1)} %reshape.11.lag_ref.refs_0_, bf16[2,4,3,256,256]{4,3,2,1,0:T(8,128)(2,1)S(1)} %toeplitz.1.t_ref.refs_1_, f32[2,2,256,1024]{3,2,1,0:T(8,128)S(1)} %get-tuple-element.65.refs_2_.sums_ref, bf16[256,1024]{1,0:T(8,128)(2,1)S(1)} %collective-permute-done.refs_0_.r1_ref.r10, ...), custom_call_target="tpu_custom_call" | custom-call | flops 5200000000 | bytes 11534464 | tf_op jit(solution)/shard_map/partial_sums/pallas_call | solution.py:30
  41.9 1.8 %collective-permute-done.16.refs_6_ = f32[8,3,512]{2,1,0:T(4,128)S(1)} collective-permute-done((f32[8,3,512]{2,1,0:T(4,128)S(1)}, f32[8,3,512]{2,1,0:T(4,128)S(1)}, u32[]{:S(2)}, u32[]{:S(2)}) %collective-permute-start.16) | collective-permute-done | bytes 49184 | tf_op jit(solution)/shard_map/ppermute | solution.py:515
  43.7 1.8 %out_p01.1 = (bf16[256,2048]{1,0:T(8,128)(2,1)}, bf16[256,2048]{1,0:T(8,128)(2,1)}, f32[16,2,512]{2,1,0:T(2,128)}, f32[16,256]{1,0:T(8,128)}) custom-call(s32[32]{0:T(128)S(1)} %reshape.11.lag_ref.refs_0_, bf16[2,4,3,256,256]{4,3,2,1,0:T(8,128)(2,1)S(1)} %toeplitz.1.t_ref.refs_1_, ...), custom_call_target="tpu_custom_call", output_to_operand_aliasing={{0}: (7, {}), {1}: (8, {})} | custom-call | flops 1 | bytes 11714688 | tf_op jit(solution)/shard_map/out_p01/pallas_call | solution.py:30
  (25 shorter events, 0.3 us)
Async XLA Ops:
  0.6 4.8 %copy-start.2 = (s32[16,2]{0,1:T(2,128)S(1)}, s32[16,2]{0,1:T(2,128)}, u32[]{:S(2)}) copy-start(s32[16,2]{0,1:T(2,128)} %param.13) | copy-start | bytes 388
  0.6 5.0 %copy-start.1 = (bf16[16,256]{1,0:T(8,128)(2,1)S(1)}, bf16[16,256]{1,0:T(8,128)(2,1)}, u32[]{:S(2)}) copy-start(bf16[16,256]{1,0:T(8,128)(2,1)} %near_ref) | copy-start | bytes 24580
  0.7 5.0 %copy-start = (bf16[16,2,512]{2,1,0:T(2,128)(2,1)S(1)}, bf16[16,2,512]{2,1,0:T(2,128)(2,1)}, u32[]{:S(2)}) copy-start(bf16[16,2,512]{2,1,0:T(2,128)(2,1)} %far_ref) | copy-start | bytes 98308
  2.4 13.3 %collective-permute-start = (bf16[256,1024]{1,0:T(8,128)(2,1)S(1)}, bf16[256,1024]{1,0:T(8,128)(2,1)S(1)}, u32[]{:S(2)}, u32[]{:S(2)}) collective-permute-start(bf16[256,1024]{1,0:T(8,128)(2,1)S(1)} %get-tuple-element.54.q1), channel_id=1, source_target_pairs={{0,1},{1,0},{2,3},{3,2},{4,8},{5,9},{6,10},{7,11},{8,4},{9,5},{10,... | collective-permute-start | bytes 1572872 | tf_op jit(solution)/shard_map/ppermute | solution.py:576
  5.4 13.9 %collective-permute-start.1 = (bf16[256,1024]{1,0:T(8,128)(2,1)S(1)}, bf16[256,1024]{1,0:T(8,128)(2,1)S(1)}, u32[]{:S(2)}, u32[]{:S(2)}) collective-permute-start(bf16[256,1024]{1,0:T(8,128)(2,1)S(1)} %get-tuple-element.44.q0.q_ref), channel_id=1, source_target_pairs={{0,1},{1,0},{2,3},{3,2},{4,8},{5,9},{6,10},{7,11},{8,4},{9,5},{10,... | collective-permute-start | bytes 1572872 | tf_op jit(solution)/shard_map/ppermute | solution.py:576
  14.2 9.7 %collective-permute-start.2 = (bf16[256,1024]{1,0:T(8,128)(2,1)S(1)}, bf16[256,1024]{1,0:T(8,128)(2,1)S(1)}, u32[]{:S(2)}, u32[]{:S(2)}) collective-permute-start(bf16[256,1024]{1,0:T(8,128)(2,1)S(1)} %get-tuple-element.63.p1), channel_id=1, source_target_pairs={{0,12},{1,13},{2,14},{3,15},{4,5},{5,4},{6,7},{7,6},{8,20},{9,21},... | collective-permute-start | bytes 1572872 | tf_op jit(solution)/shard_map/ppermute | solution.py:576
  19.3 4.6 %collective-permute-start.4 = (bf16[256,1024]{1,0:T(8,128)(2,1)S(1)}, bf16[256,1024]{1,0:T(8,128)(2,1)S(1)}, u32[]{:S(2)}, u32[]{:S(2)}) collective-permute-start(bf16[256,1024]{1,0:T(8,128)(2,1)S(1)} %get-tuple-element.63.p1), channel_id=1, source_target_pairs={{0,4},{1,5},{2,6},{3,7},{4,0},{5,1},{6,2},{7,3},{8,12},{9,13},{10,... | collective-permute-start | bytes 1572872 | tf_op jit(solution)/shard_map/ppermute | solution.py:576
  19.3 4.6 %collective-permute-start.5 = (bf16[256,1024]{1,0:T(8,128)(2,1)S(1)}, bf16[256,1024]{1,0:T(8,128)(2,1)S(1)}, u32[]{:S(2)}, u32[]{:S(2)}) collective-permute-start(bf16[256,1024]{1,0:T(8,128)(2,1)S(1)} %collective-permute-done.1.refs_1_.r11), channel_id=1, source_target_pairs={{0,4},{1,5},{2,6},{3,7},{4,0},{5,1},{6,2},{7,3},{8,12},{9,13},{10,... | collective-permute-start | bytes 1572872 | tf_op jit(solution)/shard_map/ppermute | solution.py:576
  19.8 4.1 %collective-permute-start.6 = (bf16[256,1024]{1,0:T(8,128)(2,1)S(1)}, bf16[256,1024]{1,0:T(8,128)(2,1)S(1)}, u32[]{:S(2)}, u32[]{:S(2)}) collective-permute-start(bf16[256,1024]{1,0:T(8,128)(2,1)S(1)} %collective-permute-done.refs_0_.r1_ref.r10), channel_id=1, source_target_pairs={{0,4},{1,5},{2,6},{3,7},{4,0},{5,1},{6,2},{7,3},{8,12},{9,13},{10,... | collective-permute-start | bytes 1572872 | tf_op jit(solution)/shard_map/ppermute | solution.py:576
  19.8 11.4 %collective-permute-start.3 = (bf16[256,1024]{1,0:T(8,128)(2,1)S(1)}, bf16[256,1024]{1,0:T(8,128)(2,1)S(1)}, u32[]{:S(2)}, u32[]{:S(2)}) collective-permute-start(bf16[256,1024]{1,0:T(8,128)(2,1)S(1)} %get-tuple-element.78.p0), channel_id=1, source_target_pairs={{0,12},{1,13},{2,14},{3,15},{4,5},{5,4},{6,7},{7,6},{8,20},{9,21},... | collective-permute-start | bytes 1572872 | tf_op jit(solution)/shard_map/ppermute | solution.py:576
  25.7 7.2 %collective-permute-start.9 = (f32[4,3,512]{2,1,0:T(4,128)S(1)}, f32[4,3,512]{2,1,0:T(4,128)S(1)}, u32[]{:S(2)}, u32[]{:S(2)}) collective-permute-start(f32[4,3,512]{2,1,0:T(4,128)S(1)} %correlate_far.1.refs_3_), channel_id=1, source_target_pairs={{0,24},{4,28},{8,16},{12,20},{16,8},{20,12},{24,0},{28,4},{1,25},{... | collective-permute-start | bytes 73736 | tf_op jit(solution)/shard_map/ppermute | solution.py:475
  29.1 5.2 %collective-permute-start.8 = (f32[4,3,512]{2,1,0:T(4,128)S(1)}, f32[4,3,512]{2,1,0:T(4,128)S(1)}, u32[]{:S(2)}, u32[]{:S(2)}) collective-permute-start(f32[4,3,512]{2,1,0:T(4,128)S(1)} %correlate_far.1.refs_3_), channel_id=1, source_target_pairs={{0,16},{4,20},{8,24},{12,28},{16,0},{20,4},{24,8},{28,12},{1,17},{... | collective-permute-start | bytes 73736 | tf_op jit(solution)/shard_map/ppermute | solution.py:475
  29.1 5.2 %collective-permute-start.7 = (f32[4,3,512]{2,1,0:T(4,128)S(1)}, f32[4,3,512]{2,1,0:T(4,128)S(1)}, u32[]{:S(2)}, u32[]{:S(2)}) collective-permute-start(f32[4,3,512]{2,1,0:T(4,128)S(1)} %correlate_far.1.refs_3_), channel_id=1, source_target_pairs={{0,8},{4,12},{8,0},{12,4},{16,24},{20,28},{24,16},{28,20},{1,9},{5... | collective-permute-start | bytes 73736 | tf_op jit(solution)/shard_map/ppermute | solution.py:475
  30.2 13.5 %collective-permute-start.13 = (bf16[2,256,1024]{2,1,0:T(8,128)(2,1)S(1)}, bf16[2,256,1024]{2,1,0:T(8,128)(2,1)S(1)}, u32[]{:S(2)}, u32[]{:S(2)}) collective-permute-start(bf16[2,256,1024]{2,1,0:T(8,128)(2,1)S(1)} %stack.1), channel_id=1, source_target_pairs={{0,8},{1,9},{2,10},{3,11},{4,0},{5,1},{6,2},{7,3},{8,16},{9,17},{1... | collective-permute-start | bytes 3145736 | tf_op jit(solution)/shard_map/ppermute | solution.py:576
  34.3 1.3 %collective-permute-start.10 = (f32[4,3,512]{2,1,0:T(4,128)S(1)}, f32[4,3,512]{2,1,0:T(4,128)S(1)}, u32[]{:S(2)}, u32[]{:S(2)}) collective-permute-start(f32[4,3,512]{2,1,0:T(4,128)S(1)} %add_rows.2.refs_0_), channel_id=1, source_target_pairs={{0,4},{4,0},{8,12},{12,8},{16,20},{20,16},{24,28},{28,24},{1,5},{5... | collective-permute-start | bytes 73736 | tf_op jit(solution)/shard_map/ppermute | solution.py:487
  34.4 3.0 %collective-permute-start.15 = (bf16[256,1024]{1,0:T(8,128)(2,1)S(1)}, bf16[256,1024]{1,0:T(8,128)(2,1)S(1)}, u32[]{:S(2)}, u32[]{:S(2)}) collective-permute-start(bf16[256,1024]{1,0:T(8,128)(2,1)S(1)} %get-tuple-element.78.p0), channel_id=1, source_target_pairs={{0,4},{1,5},{2,6},{3,7},{4,0},{5,1},{6,2},{7,3},{8,12},{9,13},{10,... | collective-permute-start | bytes 1572872 | tf_op jit(solution)/shard_map/ppermute | solution.py:576
  35.6 5.2 %collective-permute-start.11 = (bf16[256,1024]{1,0:T(8,128)(2,1)S(1)}, bf16[256,1024]{1,0:T(8,128)(2,1)S(1)}, u32[]{:S(2)}, u32[]{:S(2)}) collective-permute-start(bf16[256,1024]{1,0:T(8,128)(2,1)S(1)} %collective-permute-done.3.refs_5_), channel_id=1, source_target_pairs={{0,4},{1,5},{2,6},{3,7},{4,0},{5,1},{6,2},{7,3},{8,12},{9,13},{10,... | collective-permute-start | bytes 1572872 | tf_op jit(solution)/shard_map/ppermute | solution.py:576
  35.8 5.1 %collective-permute-start.12 = (bf16[256,1024]{1,0:T(8,128)(2,1)S(1)}, bf16[256,1024]{1,0:T(8,128)(2,1)S(1)}, u32[]{:S(2)}, u32[]{:S(2)}) collective-permute-start(bf16[256,1024]{1,0:T(8,128)(2,1)S(1)} %collective-permute-done.2.r2_ref.refs_5_), channel_id=1, source_target_pairs={{0,4},{1,5},{2,6},{3,7},{4,0},{5,1},{6,2},{7,3},{8,12},{9,13},{10,... | collective-permute-start | bytes 1572872 | tf_op jit(solution)/shard_map/ppermute | solution.py:576
  36.1 3.3 %collective-permute-start.14 = (f32[4,3,512]{2,1,0:T(4,128)S(1)}, f32[4,3,512]{2,1,0:T(4,128)S(1)}, u32[]{:S(2)}, u32[]{:S(2)}) collective-permute-start(f32[4,3,512]{2,1,0:T(4,128)S(1)} %add_rows.3.first_ref), channel_id=1, source_target_pairs={{0,5},{1,4},{2,7},{3,6},{4,1},{5,0},{6,3},{7,2},{8,13},{9,12},{10,... | collective-permute-start | bytes 73736 | tf_op jit(solution)/shard_map/ppermute | solution.py:515
  39.5 4.2 %collective-permute-start.16 = (f32[8,3,512]{2,1,0:T(4,128)S(1)}, f32[8,3,512]{2,1,0:T(4,128)S(1)}, u32[]{:S(2)}, u32[]{:S(2)}) collective-permute-start(f32[8,3,512]{2,1,0:T(4,128)S(1)} %join_rows.1.refs_5_), channel_id=1, source_target_pairs={{0,6},{1,7},{2,4},{3,5},{4,2},{5,3},{6,0},{7,1},{8,14},{9,15},{10,... | collective-permute-start | bytes 147464 | tf_op jit(solution)/shard_map/ppermute | solution.py:515
